TPU v7x, 128 devices: a whole 4x4x4 slice. The times are simulated.
128 devices in a mesh: seq: 64 (over z, y, x_hi, core), head: 2 (over x_lo).
Axes of the slice: x: 4 (x_hi: 2, x_lo: 2; x = x_hi * 2 + x_lo), y: 4, z: 4, core: 2. Of those that a mesh axis runs over, the one named last changes fastest.
Arguments:
- queries: bfloat16 [6144, 2560], P('seq', 'head'), may hold values from -20 to 20
- keys: bfloat16 [6144, 2560], P('seq', 'head'), may hold values from -5 to 5
- values: bfloat16 [6144, 2560], P('seq', 'head'), may hold values from -6 to 6
- queries_tan: bfloat16 [6144, 2560], P('seq', 'head'), may hold values from -6 to 6
- keys_tan: bfloat16 [6144, 2560], P('seq', 'head'), may hold values from -6 to 6
- values_tan: bfloat16 [6144, 2560], P('seq', 'head'), may hold values from -6 to 6
- segments: int32 [6144], P('seq'), may hold values from 0 to 1, as said below
- positions: int32 [6144], P('seq'), may hold values from 0 to 3839, as said below
- out_weight: bfloat16 [2560, 5120], P('head'), may hold values from -0.125 to 0.125
- residual: float32 [6144, 5120], P('seq', 'head'), may hold values from -30 to 30
- residual_tan: float32 [6144, 5120], P('seq', 'head'), may hold values from -6 to 6
- gate: float32 [2, 5120], replicated, may hold values from -3 to 3
- gate_tan: float32 [2, 5120], replicated, may hold values from -3 to 3
- mod_scale: float32 [2, 5120], replicated, may hold values from -2 to 2
- mod_scale_tan: float32 [2, 5120], replicated, may hold values from -2 to 2
- mod_shift: float32 [2, 5120], replicated, may hold values from -2 to 2
- mod_shift_tan: float32 [2, 5120], replicated, may hold values from -2 to 2
Outputs:
- resid_out: float32 [6144, 5120], P('seq', 'head')
- resid_tan_out: float32 [6144, 5120], P('seq', 'head')
- ffn_in: bfloat16 [6144, 5120], P('seq')
- ffn_in_tan: bfloat16 [6144, 5120], P('seq')
Inputs may be any that keep to these rules, and one draw needn't show every extreme that they name: `segments`: 0 and 1 name the two clips; each clip is one run of consecutive tokens when the last token is taken as followed by the first; one of the two clips holds exactly 3840 tokens and the other the rest. Within each clip the positions of its tokens are a permutation of 0 to the clip's length minus 1.
All inputs are finite; a program needn't handle non-finite values.
Results may differ from a plain program's by a relative error of at most 0.029.
Values may be sent and summed in bfloat16 or wider, within the bound.
No kernel may reach another device: no remote copies, remote signals or barrier semaphores. Data moves between devices by JAX's collectives and lax.ppermute only.
A program may use at most 320 MiB of HBM per device.

v0:
```python
import math

import jax
import jax.numpy as jnp
from jax import lax
from jax.sharding import PartitionSpec as P

D = 5120
HEAD_DIM = 128


neg_fill = -1e30
norm_eps = 1e-06
rope_base = 10000.0


def rotary(flat_rows, position, head_width):
    token_count = flat_rows.shape[0]
    head_count = flat_rows.shape[1] // head_width
    half_width = head_width // 2
    per_head = flat_rows.astype(jnp.float32).reshape(token_count, head_count, head_width)
    frequency = rope_base ** (-jnp.arange(half_width, dtype=jnp.float32) / half_width)
    angles = position.astype(jnp.float32)[:, None] * frequency[None, :]
    cosine = jnp.cos(angles)[:, None, :]
    sine_part = jnp.sin(angles)[:, None, :]
    first_half = per_head[..., :half_width]
    second_half = per_head[..., half_width:]
    turned = jnp.concatenate(
        [
            first_half * cosine - second_half * sine_part,
            first_half * sine_part + second_half * cosine,
        ],
        axis=-1,
    )
    return turned.reshape(token_count, head_count * head_width).astype(jnp.bfloat16)


def pick_clip(clip_table, segments):
    return jnp.where(segments[:, None] == 1, clip_table[1][None, :], clip_table[0][None, :])


def moments(resid_rows, resid_tan_rows):
    return (
        jnp.sum(resid_rows, axis=1),
        jnp.sum(resid_rows * resid_rows, axis=1),
        jnp.sum(resid_tan_rows, axis=1),
        jnp.sum(resid_rows * resid_tan_rows, axis=1),
    )


def finish_norm(
    resid_rows,
    resid_tan_rows,
    moment_sums,
    width,
    scale_rows,
    scale_tan_rows,
    shift_rows,
    shift_tan_rows,
):
    first_sum, square_sum, tan_sum, cross_sum = moment_sums
    mean_rows = first_sum / width
    rstd = lax.rsqrt(square_sum / width - mean_rows * mean_rows + norm_eps)
    mean_tan = tan_sum / width
    cov_rows = cross_sum / width - mean_rows * mean_tan
    centered = resid_rows - mean_rows[:, None]
    normed = centered * rstd[:, None]
    normed_tan = (resid_tan_rows - mean_tan[:, None]) * rstd[:, None] - centered * (
        rstd * rstd * rstd * cov_rows
    )[:, None]
    ffn_rows = (normed * (1.0 + scale_rows) + shift_rows).astype(jnp.bfloat16)
    ffn_tan_rows = (
        normed_tan * (1.0 + scale_rows) + normed * scale_tan_rows + shift_tan_rows
    ).astype(jnp.bfloat16)
    return (ffn_rows, ffn_tan_rows)


def body(
    queries,
    keys,
    values,
    queries_tan,
    keys_tan,
    values_tan,
    segments,
    positions,
    out_weight,
    residual,
    residual_tan,
    gate,
    gate_tan,
    mod_scale,
    mod_scale_tan,
    mod_shift,
    mod_shift_tan,
):
    row_count = queries.shape[0]
    local_width = queries.shape[1]
    head_count = local_width // HEAD_DIM
    score_scale = 1.0 / math.sqrt(HEAD_DIM)
    rotated_queries = rotary(queries, positions, HEAD_DIM)
    rotated_keys = rotary(keys, positions, HEAD_DIM)
    rotated_queries_tan = rotary(queries_tan, positions, HEAD_DIM)
    rotated_keys_tan = rotary(keys_tan, positions, HEAD_DIM)
    query_heads = rotated_queries.reshape(row_count, head_count, HEAD_DIM)
    query_tan_heads = rotated_queries_tan.reshape(row_count, head_count, HEAD_DIM)
    query_segments = segments.astype(jnp.float32)
    head_rows = (head_count, row_count)
    key_piece = lax.all_gather(rotated_keys, "seq", axis=0, tiled=True)
    value_piece = lax.all_gather(values, "seq", axis=0, tiled=True)
    key_tan_piece = lax.all_gather(rotated_keys_tan, "seq", axis=0, tiled=True)
    value_tan_piece = lax.all_gather(values_tan, "seq", axis=0, tiled=True)
    segment_piece = lax.all_gather(segments.astype(jnp.bfloat16), "seq", axis=0, tiled=True)
    key_count = key_piece.shape[0]
    key_heads = key_piece.reshape(key_count, head_count, HEAD_DIM)
    key_tan_heads = key_tan_piece.reshape(key_count, head_count, HEAD_DIM)
    value_heads = value_piece.reshape(key_count, head_count, HEAD_DIM)
    value_tan_heads = value_tan_piece.reshape(key_count, head_count, HEAD_DIM)
    allowed = query_segments[:, None] == segment_piece.astype(jnp.float32)[None, :]
    best = jnp.full(head_rows, neg_fill, jnp.float32)
    scores = (
        jnp.einsum("qhd,khd->hqk", query_heads, key_heads, preferred_element_type=jnp.float32)
        * score_scale
    )
    score_tan = (
        jnp.einsum("qhd,khd->hqk", query_tan_heads, key_heads, preferred_element_type=jnp.float32)
        + jnp.einsum("qhd,khd->hqk", query_heads, key_tan_heads, preferred_element_type=jnp.float32)
    ) * score_scale
    block_best = jnp.max(jnp.where(allowed[None], scores, neg_fill), axis=2)
    new_best = jnp.maximum(best, block_best)
    raised = jnp.where(allowed[None], jnp.exp(scores - new_best[:, :, None]), 0.0)
    raised_tan = raised * score_tan
    raised_low = raised.astype(jnp.bfloat16)
    raised_tan_low = raised_tan.astype(jnp.bfloat16)
    value_sum = jnp.einsum(
        "hqk,khd->hqd", raised_low, value_heads, preferred_element_type=jnp.float32
    )
    tangent_sum = jnp.einsum(
        "hqk,khd->hqd", raised_tan_low, value_heads, preferred_element_type=jnp.float32
    ) + jnp.einsum("hqk,khd->hqd", raised_low, value_tan_heads, preferred_element_type=jnp.float32)
    best, total, drift_sum, value_sum, tangent_sum = (
        new_best,
        jnp.sum(raised, axis=2),
        jnp.sum(raised_tan, axis=2),
        value_sum,
        tangent_sum,
    )
    attended_heads = value_sum / total[:, :, None]
    drift = drift_sum / total
    attended_tan_heads = tangent_sum / total[:, :, None] - drift[:, :, None] * attended_heads
    attended = (
        attended_heads.transpose(1, 0, 2).reshape(row_count, local_width).astype(jnp.bfloat16)
    )
    attended_tan = (
        attended_tan_heads.transpose(1, 0, 2).reshape(row_count, local_width).astype(jnp.bfloat16)
    )
    projected_both = jnp.dot(
        jnp.concatenate([attended, attended_tan], axis=0),
        out_weight,
        preferred_element_type=jnp.float32,
    )
    projected = projected_both[:row_count]
    projected_tan = projected_both[row_count:]
    gate_rows = pick_clip(gate, segments)
    branch_term = gate_rows * projected
    branch_tan = pick_clip(gate_tan, segments) * projected + gate_rows * projected_tan
    head_index = lax.axis_index("head")
    half_width = residual.shape[1]
    offset = head_index * half_width
    blank = jnp.zeros((row_count, D), jnp.float32)
    lifted = lax.dynamic_update_slice_in_dim(blank, residual, offset, 1)
    lifted_tan = lax.dynamic_update_slice_in_dim(blank, residual_tan, offset, 1)
    full_rows, full_tan = (
        lax.psum((branch_term + lifted).astype(jnp.bfloat16), "head").astype(jnp.float32),
        lax.psum((branch_tan + lifted_tan).astype(jnp.bfloat16), "head").astype(jnp.float32),
    )
    ffn_in, ffn_in_tan = finish_norm(
        full_rows,
        full_tan,
        moments(full_rows, full_tan),
        D,
        pick_clip(mod_scale, segments),
        pick_clip(mod_scale_tan, segments),
        pick_clip(mod_shift, segments),
        pick_clip(mod_shift_tan, segments),
    )
    resid_out = lax.dynamic_slice_in_dim(full_rows, offset, half_width, 1)
    resid_tan_out = lax.dynamic_slice_in_dim(full_tan, offset, half_width, 1)
    return (resid_out, resid_tan_out, ffn_in, ffn_in_tan)


def solution(mesh):
    in_specs = (
        P("seq", "head"),
        P("seq", "head"),
        P("seq", "head"),
        P("seq", "head"),
        P("seq", "head"),
        P("seq", "head"),
        P("seq"),
        P("seq"),
        P("head", None),
        P("seq", "head"),
        P("seq", "head"),
        P(),
        P(),
        P(),
        P(),
        P(),
        P(),
    )
    out_specs = (P("seq", "head"), P("seq", "head"), P("seq", None), P("seq", None))
    return jax.shard_map(body, mesh=mesh, in_specs=in_specs, out_specs=out_specs, check_vma=False)
```

profile of v0, /device:TPU:0, one launch (start us, length us, event | category | flops | bytes accessed | tf_op | source)
XLA Modules:
  0.0 652.9 jit_solution(10711924716304512374)
XLA Ops:
  7.2 1.1 copy.45
  8.8 1.1 copy.48
  10.4 1.1 copy.58
  11.6 0.8 fusion.44
  12.3 1.2 copy.83
  13.5 1.0 copy.84
  14.5 1.1 copy.62
  15.6 0.8 fusion.43
  16.4 1.2 copy.85
  17.6 1.0 copy.86
  18.5 0.2 multiply_cosine_fusion
  18.8 2.5 subtract_convert_fusion
  21.3 0.3 pad_maximum_fusion.1
  21.8 0.9 copy.52
  23.0 0.9 copy.66
  23.9 0.7 all-gather.11.cloned.1.call-update
  24.7 0.5 all-gather.7.cloned.1.call-update
  25.3 0.6 dynamic-slice.2
  26.6 0.2 dynamic-update-slice.2
  26.8 334.8 %all-reduce = bf16[6144]{0:T(1024)(128)(2,1)S(1)} all-reduce(bf16[6144]{0:T(1024)(128)(2,1)S(1)} %dynamic-update-slice.2), channel_id=1, replica_groups=mesh['seq'=64,'head'=2] {'seq'}, use_global_device_ids=true, to_apply=%add | all-reduce | flops 6144 | bytes 24576
  361.6 0.9 fusion.52
  362.5 0.9 fusion.51
  363.4 0.9 fusion.49
  364.3 0.9 fusion.50
  365.2 0.4 broadcast_compare_fusion
  365.7 19.1 %copy.53 = bf16[6144,1280]{0,1:T(8,128)(2,1)} copy(bf16[6144,1280]{1,0:T(8,128)(2,1)} %all-gather.5.cloned.1.call-done) | data formatting | bytes 31457280 | tf_op jit(solution)/shard_map/all_gather | solution.py:109
  384.7 20.8 %copy.67 = bf16[6144,1280]{0,1:T(8,128)(2,1)} copy(bf16[6144,1280]{1,0:T(8,128)(2,1)} %all-gather.9.cloned.1.call-done) | data formatting | bytes 31457280 | tf_op jit(solution)/shard_map/all_gather | solution.py:111
  405.5 20.7 %copy.70 = bf16[6144,1280]{0,1:T(8,128)(2,1)} copy(bf16[6144,1280]{1,0:T(8,128)(2,1)} %all-gather.11.cloned.1.call-done) | data formatting | bytes 31457280 | tf_op jit(solution)/shard_map/all_gather | solution.py:112
  426.2 14.7 %select_reduce_fusion = (f32[10,96]{1,0:T(8,128)S(1)}, f32[10,96,6144]{2,1,0:T(8,128)}) fusion(pred[96,6144]{1,0:T(8,128)(4,1)S(1)} %broadcast_compare_fusion, bf16[6144,10,128]{0,2,1:T(8,128)(2,1)} %bitcast.49, bf16[96,10,64]{2,0,1:T(8,128)(2,1)S(1)} %get-tuple-element.34, bf16[96,10,64]{2,0,1:T(8,128)(2,1)S(1)} %get-tuple-element.35), kind=kOutput, calls=%fused_computation.2 | convolution fusion | flops 1528134656 | bytes 40161024 | tf_op jit(solution)/shard_map/qhd,khd->hqk/dot_general | solution.py:122
  441.0 11.3 %fusion = f32[10,96]{1,0:T(8,128)S(1)} fusion(f32[10,96,6144]{2,1,0:T(8,128)} %get-tuple-element.57, f32[10,96]{1,0:T(8,128)S(1)} %broadcast_maximum_fusion, pred[96,6144]{1,0:T(8,128)(4,1)S(1)} %broadcast_compare_fusion), kind=kLoop, calls=%fused_computation.3 | loop fusion | flops 23592000 | bytes 24190464 | tf_op jit(solution)/shard_map/reduce_sum | solution.py:143
  452.3 16.6 %fusion.26 = f32[10,96,6144]{2,1,0:T(8,128)} fusion(bf16[6144,10,128]{0,2,1:T(8,128)(2,1)} %bitcast.50, bf16[96,10,64]{2,0,1:T(8,128)(2,1)S(1)} %copy-done.2, bf16[96,10,64]{2,0,1:T(8,128)(2,1)S(1)} %copy-done.3), kind=kOutput, calls=%fused_computation.43 | convolution fusion | flops 1510440960 | bytes 39567360 | tf_op jit(solution)/shard_map/qhd,khd->hqk/dot_general | solution.py:126
  469.0 27.5 %fusion.54 = (f32[10,96]{1,0:T(8,128)S(1)}, bf16[10,96,6144]{2,1,0:T(8,128)(2,1)}) fusion(f32[10,96,6144]{2,1,0:T(8,128)} %fusion.26, bf16[6144,10,128]{0,2,1:T(8,128)(2,1)} %bitcast.53, bf16[96,10,64]{2,0,1:T(8,128)(2,1)S(1)} %get-tuple-element.34, bf16[96,10,64]{2,0,1:T(8,128)(2,1)S(1)} %get-tuple-element.35, f32[10,96]{1,0:T(8,128)S(1)} %broadcast_maximum_fusion, ...), kind=kOutput, calls=%fused_computation.82 | convolution fusion | flops 1557625856 | bytes 75554304 | tf_op jit(solution)/shard_map/qhd,khd->hqk/dot_general | solution.py:127
  496.4 18.7 %fusion.31 = f32[10,96,128]{2,1,0:T(8,128)S(1)} fusion(bf16[6144,10,128]{0,2,1:T(8,128)(2,1)} %bitcast.54, f32[10,96,6144]{2,1,0:T(8,128)} %get-tuple-element.57, f32[10,96]{1,0:T(8,128)S(1)} %broadcast_maximum_fusion, pred[96,6144]{1,0:T(8,128)(4,1)S(1)} %broadcast_compare_fusion), kind=kOutput, calls=%fused_computation.51 | convolution fusion | flops 1533542400 | bytes 40406784 | tf_op jit(solution)/shard_map/hqk,khd->hqd/dot_general | solution.py:140
  515.1 19.2 %copy.55 = bf16[6144,1280]{0,1:T(8,128)(2,1)} copy(bf16[6144,1280]{1,0:T(8,128)(2,1)} %all-gather.7.cloned.1.call-done) | data formatting | bytes 31457280 | tf_op jit(solution)/shard_map/all_gather | solution.py:110
  534.4 18.8 %fusion.55 = (bf16[96,10,128]{2,0,1:T(8,128)(2,1)S(1)}, f32[96,10,128]{2,0,1:T(8,128)S(1)}) fusion(f32[96,10]{0,1:T(8,128)S(1)} %bitcast.63, bf16[6144,10,128]{0,2,1:T(8,128)(2,1)} %bitcast.51, f32[10,96,6144]{2,1,0:T(8,128)} %get-tuple-element.57, f32[10,96]{1,0:T(8,128)S(1)} %broadcast_maximum_fusion, pred[96,6144]{1,0:T(8,128)(4,1)S(1)} %broadcast_compare_fusion), kind=kOutput, calls=%fused_computation.83 | convolution fusion | flops 1533788160 | bytes 40656384 | tf_op jit(solution)/shard_map/hqk,khd->hqd/dot_general | solution.py:135
  553.2 11.5 %fusion.18 = bf16[96,10,128]{2,0,1:T(8,128)(2,1)S(1)} fusion(f32[10,96,128]{2,1,0:T(8,128)S(1)} %fusion.31, bf16[6144,10,128]{0,2,1:T(8,128)(2,1)} %bitcast.52, bf16[10,96,6144]{2,1,0:T(8,128)(2,1)} %get-tuple-element.59, f32[96,10,128]{2,0,1:T(8,128)S(1)} %get-tuple-element.61, f32[96,10]{0,1:T(8,128)S(1)} %bitcast_divide_fusion, f32[96,10]{0,1:T(8,128)S(1)} %bitcast.64), kind=kOutput, calls=%fused_computation.25 | convolution fusion | flops 1510563840 | bytes 28761600 | tf_op jit(solution)/shard_map/hqk,khd->hqd/dot_general | solution.py:138
  564.7 0.2 copy.72
  565.2 6.7 %fusion.22 = f32[192,5120]{1,0:T(8,128)S(1)} fusion(bf16[1280,5120]{1,0:T(8,128)(2,1)} %param.25, bf16[96,1280]{0,1:T(8,128)(2,1)S(1)} %bitcast.61, bf16[96,1280]{0,1:T(8,128)(2,1)S(1)} %bitcast.62), kind=kOutput, calls=%fused_computation.29 | convolution fusion | flops 2517565440 | bytes 17530880 | tf_op jit(solution)/shard_map/dot_general | solution.py:157
  571.9 0.6 fusion.4
  572.7 1.1 convert_element_type.81
  573.9 1.1 convert_element_type.79
  575.1 61.4 %all-reduce.4.cloned.1.call-done = (bf16[96,5120]{1,0:T(8,128)(2,1)}, bf16[96,5120]{1,0:T(8,128)(2,1)}) async-done(((bf16[96,5120]{1,0:T(8,128)(2,1)}, bf16[96,5120]{1,0:T(8,128)(2,1)}), (bf16[96,5120]{1,0:T(8,128)(2,1)}, bf16[96,5120]{1,0:T(8,128)(2,1)})) %all-reduce.4.cloned.1.call-update) | async-done | bytes 1966096 | tf_op jit(solution)/shard_map/psum | solution.py:174
  636.6 1.5 convert_element_type.82
  638.1 2.1 convert_reduce_fusion.1
  640.2 1.4 convert_element_type.80
  641.6 1.0 constant_dynamic-slice_fusion
  642.6 1.0 constant_dynamic-slice_fusion.1
  643.6 2.8 add_convert_fusion
  (56 shorter events, 2.4 us)
Async XLA Ops:
  7.2 11.4 %copy-start.8 = (s32[96]{0:T(128)S(1)}, s32[96]{0:T(128)}, u32[]{:S(2)}) copy-start(s32[96]{0:T(128)} %param.24) | copy-start | bytes 1156
  7.2 358.5 %all-gather.5.cloned.1.call-start = ((), (), s32[]{:S(2)}) async-start(), calls=%async_computation | async-start | bytes 15974400 | tf_op jit(solution)/shard_map/all_gather | solution.py:109
  8.6 16.6 %copy-start.10 = (u32[128]{0:T(128)S(1)}, u32[128]{0:T(128)}, u32[]{:S(2)}) copy-start(u32[128]{0:T(128)} %constant.49) | copy-start | bytes 1540
  8.6 17.9 %copy-start.9 = (s32[96]{0:T(128)S(1)}, s32[96]{0:T(128)}, u32[]{:S(2)}) copy-start(s32[96]{0:T(128)} %param.23) | copy-start | bytes 1156
  22.7 362.0 %all-gather.9.cloned.1.call-start = ((), (), s32[]{:S(2)}) async-start(), calls=%async_computation.2 | async-start | bytes 15974400 | tf_op jit(solution)/shard_map/all_gather | solution.py:111
  23.9 381.6 %all-gather.11.cloned.1.call-start = ((), (), s32[]{:S(2)}) async-start(), calls=%async_computation.3 | async-start | bytes 15974400 | tf_op jit(solution)/shard_map/all_gather | solution.py:112
  24.6 490.5 %all-gather.7.cloned.1.call-start = ((), (), s32[]{:S(2)}) async-start(), calls=%async_computation.1 | async-start | bytes 15974400 | tf_op jit(solution)/shard_map/all_gather | solution.py:110
  25.2 611.3 %all-reduce.4.cloned.1.call-start = ((), (), s32[]{:S(2)}) async-start(), calls=%async_computation.4 | async-start | bytes 3932160 | tf_op jit(solution)/shard_map/psum | solution.py:174
  441.0 11.3 %copy-start.2 = (bf16[96,10,64]{2,0,1:T(8,128)(2,1)S(1)}, bf16[96,10,64]{2,0,1:T(8,128)(2,1)}, u32[]{:S(2)}) copy-start(bf16[96,10,64]{2,0,1:T(8,128)(2,1)} %get-tuple-element.32) | copy-start | bytes 368644
  441.0 11.3 %copy-start.3 = (bf16[96,10,64]{2,0,1:T(8,128)(2,1)S(1)}, bf16[96,10,64]{2,0,1:T(8,128)(2,1)}, u32[]{:S(2)}) copy-start(bf16[96,10,64]{2,0,1:T(8,128)(2,1)} %get-tuple-element.33) | copy-start | bytes 368644
  565.2 7.3 %copy-start.4 = (f32[96,2560]{1,0:T(8,128)S(1)}, f32[96,2560]{1,0:T(8,128)}, u32[]{:S(2)}) copy-start(f32[96,2560]{1,0:T(8,128)} %param.27) | copy-start | bytes 2949124
  571.8 1.9 copy-start.5
  571.8 3.2 copy-start.6
  571.9 3.2 copy-start.7
  636.5 7.1 %copy-start = (bf16[96,5120]{1,0:T(8,128)(2,1)S(1)}, bf16[96,5120]{1,0:T(8,128)(2,1)}, u32[]{:S(2)}) copy-start(bf16[96,5120]{1,0:T(8,128)(2,1)} %get-tuple-element.8) | copy-start | bytes 2949124
  636.6 7.1 %copy-start.1 = (bf16[96,5120]{1,0:T(8,128)(2,1)S(1)}, bf16[96,5120]{1,0:T(8,128)(2,1)}, u32[]{:S(2)}) copy-start(bf16[96,5120]{1,0:T(8,128)(2,1)} %get-tuple-element.9) | copy-start | bytes 2949124
Sparse Core Ops, SparseCore 0:
  22.8 105.2 all-gather.4
  131.8 100.7 all-gather.8
  235.7 100.5 all-gather.10
  339.2 99.9 all-gather.6
  575.1 61.3 all-reduce.3
where the time goes:
time: 656 us; the launch traced here: 653 us
  blocking collectives  335 us (51%)
  matrix products  114 us (17%)
  local copies, waits for them, and re-layouts  100 us (15%)
  waiting for transfers between devices  62.7 us (10%)
  other arithmetic  25.7 us (4%)
  between operations  14.8 us (2%)
    unnamed x1, blocking collectives  335 us
    psum x1, waiting for transfers between devices, body(): lax.psum((branch_term + lifted).astype(jnp.bfloat16), 'head')  61.4 us
    dot_general x1, matrix products, body(): jnp.einsum('qhd,khd->hqk', query_heads, key_tan_heads, preferred_element_...  27.5 us
    all_gather x1, local copies, waits for them, and re-layouts, body(): key_tan_piece = lax.all_gather(rotated_keys_tan, 'seq', axis=0, tiled=True)  20.8 us
    all_gather x1, local copies, waits for them, and re-layouts, body(): value_tan_piece = lax.all_gather(values_tan, 'seq', axis=0, tiled=True)  20.7 us
    all_gather x1, local copies, waits for them, and re-layouts, body(): value_piece = lax.all_gather(values, 'seq', axis=0, tiled=True)  19.2 us
    all_gather x1, local copies, waits for them, and re-layouts, body(): key_piece = lax.all_gather(rotated_keys, 'seq', axis=0, tiled=True)  19.1 us
    dot_general x1, matrix products, body(): jnp.einsum('hqk,khd->hqd', raised_low, value_heads, preferred_element_typ...  18.8 us
  transfers between devices with their start and end apart: 5, of which 1 were waited for; matrix products, arithmetic and copies ran while one was open for 24% of the time, Pallas kernels for 0%

commit v1 on v0

v1 whole, which is shorter than its diff:
```python
import math

import jax
import jax.numpy as jnp
from jax import lax
from jax.experimental import pallas as pl
from jax.experimental.pallas import tpu as pltpu
from jax.sharding import Mesh, PartitionSpec as P

D = 5120
HD = 128
NH = 10
ROWS = 96
THIRD = 32
CHIPS = 32
PARTS = 3
MSG = 240
KEYS = CHIPS * ROWS
QUERIES = CHIPS * THIRD
HALF = D // 2

QB = 8
KB = 4
QR = QB * THIRD
KR = KB * ROWS
NQ = CHIPS // QB
NK = CHIPS // KB

neg_fill = -1e30
norm_eps = 1e-06
rope_base = 10000.0
score_scale = 1.0 / math.sqrt(HD)
exp_scale = score_scale * math.log2(math.e)

f32 = jnp.float32
bf16 = jnp.bfloat16
VMEM = pl.BlockSpec(memory_space=pltpu.VMEM)


def params(**kw):
    return pltpu.CompilerParams(vmem_limit_bytes=56 * 2**20, **kw)


def pack_kernel(q_ref, k_ref, v_ref, qt_ref, kt_ref, vt_ref, cos_ref, sin_ref, seg_ref, out_ref):
    cos = cos_ref[...]
    sin = sin_ref[...]

    def rot(ref, cols):
        x = ref[:, cols].astype(f32)
        return (x * cos + jnp.roll(x, HD // 2, axis=1) * sin).astype(bf16)

    for h in range(NH):
        cols = slice(h * HD, (h + 1) * HD)
        k, kt = rot(k_ref, cols), rot(kt_ref, cols)
        q, qt = rot(q_ref, cols), rot(qt_ref, cols)
        v, vt = v_ref[:, cols], vt_ref[:, cols]
        for t in range(PARTS):
            s = h * PARTS + t
            mine = slice(t * THIRD, (t + 1) * THIRD)
            out_ref[s, 0:96, 0:128] = k
            out_ref[s, 0:96, 128:256] = kt
            out_ref[s, 96:192, 0:128] = v
            out_ref[s, 96:192, 128:256] = vt
            out_ref[s, 192:224, 0:128] = qt[mine]
            out_ref[s, 192:224, 128:256] = q[mine]
            out_ref[s, 224:240, :] = seg_ref[t]
    for s in range(NH * PARTS, CHIPS):
        out_ref[s] = jnp.zeros((MSG, 256), bf16)


def attn_kernel(q_ref, kv_ref, kseg_ref, out_ref, stat_ref, s_ref, acc_ref, acct_ref, m_ref, l_ref, d_ref, flag_ref):
    for kb in range(NK):
        row = kseg_ref[kb]
        flag_ref[0, kb] = jnp.min(row)
        flag_ref[1, kb] = jnp.max(row)

    eye = lax.broadcasted_iota(jnp.int32, (THIRD, HD), 0) == lax.broadcasted_iota(jnp.int32, (THIRD, HD), 1)
    lane = lax.broadcasted_iota(jnp.int32, (QR, HD), 1)
    nt = (((1,), (1,)), ((), ()))

    @pl.loop(0, NQ)
    def _(g):
        qq = q_ref[pl.ds(g * QB, QB), 0:THIRD, :].reshape(QR, 256)
        q = qq[:, 128:256]
        cols = []
        for i in range(QB):
            tile = q_ref[g * QB + i, 32:48, 0:128].astype(f32)
            cols.append(jnp.sum(jnp.where(eye, tile[1:2, :], 0.0), axis=1, keepdims=True))
        qseg = jnp.concatenate(cols, axis=0)
        qmin, qmax = jnp.min(qseg), jnp.max(qseg)
        m_ref[...] = jnp.full((QR, HD), neg_fill, f32)
        l_ref[...] = jnp.zeros((QR, HD), f32)
        d_ref[...] = jnp.zeros((QR, HD), f32)
        acc_ref[...] = jnp.zeros((QR, 256), f32)
        acct_ref[...] = jnp.zeros((QR, HD), f32)

        @pl.loop(0, NK)
        def _(kb):
            @pl.when((flag_ref[0, kb] <= qmax) & (flag_ref[1, kb] >= qmin))
            def _():
                k = kv_ref[pl.ds(kb * KB, KB), 0:96, 0:128].reshape(KR, HD)
                s = lax.dot_general(q, k, nt, preferred_element_type=f32)
                s = jnp.where(qseg == kseg_ref[kb], s, neg_fill)
                s_ref[kb] = s
                m = m_ref[...]
                for j in range(KR // HD):
                    m = jnp.maximum(m, s[:, j * HD : (j + 1) * HD])
                m_ref[...] = m

        top = jnp.max(m_ref[...], axis=1, keepdims=True)

        @pl.loop(0, NK)
        def _(kb):
            @pl.when((flag_ref[0, kb] <= qmax) & (flag_ref[1, kb] >= qmin))
            def _():
                kk = kv_ref[pl.ds(kb * KB, KB), 0:96, :].reshape(KR, 256)
                vv = kv_ref[pl.ds(kb * KB, KB), 96:192, :].reshape(KR, 256)
                st = lax.dot_general(qq, kk, nt, preferred_element_type=f32)
                p = jnp.exp2((s_ref[kb] - top) * exp_scale)
                pt = p * st
                l, d = l_ref[...], d_ref[...]
                for j in range(KR // HD):
                    l = l + p[:, j * HD : (j + 1) * HD]
                    d = d + pt[:, j * HD : (j + 1) * HD]
                l_ref[...] = l
                d_ref[...] = d
                acc_ref[...] += jnp.dot(p.astype(bf16), vv, preferred_element_type=f32)
                acct_ref[...] += jnp.dot(pt.astype(bf16), vv[:, 0:128], preferred_element_type=f32)

        total = jnp.sum(l_ref[...], axis=1, keepdims=True)
        inv = 1.0 / total
        drift = jnp.sum(d_ref[...], axis=1, keepdims=True) * inv * score_scale
        o = acc_ref[:, 0:128] * inv
        t = (acct_ref[...] * score_scale + acc_ref[:, 128:256]) * inv - drift * o
        out_ref[pl.ds(g * QB, QB), 0:32, :] = o.astype(bf16).reshape(QB, THIRD, HD)
        out_ref[pl.ds(g * QB, QB), 32:64, :] = t.astype(bf16).reshape(QB, THIRD, HD)
        lse = top * exp_scale + jnp.log2(total)
        stats = jnp.where(lane == 0, lse, jnp.where(lane == 1, drift, 0.0))
        stat_ref[g] = jnp.transpose(stats)[0:8, :]


def combine_kernel(a_ref, sa_ref, b_ref, sb_ref, out_ref):
    def cols(ref, g):
        tile = jnp.concatenate([ref[g], jnp.zeros((HD - 8, QR), f32)], axis=0)
        tile = jnp.transpose(tile)
        return tile[:, 0:1], tile[:, 1:2]

    for g in range(NQ):
        rows = slice(g * QB, (g + 1) * QB)
        (la, da), (lb, db) = cols(sa_ref, g), cols(sb_ref, g)
        top = jnp.maximum(la, lb)
        wa, wb = jnp.exp2(la - top), jnp.exp2(lb - top)
        inv = 1.0 / (wa + wb)
        wa, wb = wa * inv, wb * inv
        drift = wa * da + wb * db
        oa = a_ref[rows, 0:32, :].astype(f32).reshape(QR, HD)
        ta = a_ref[rows, 32:64, :].astype(f32).reshape(QR, HD)
        ob = b_ref[rows, 0:32, :].astype(f32).reshape(QR, HD)
        tb = b_ref[rows, 32:64, :].astype(f32).reshape(QR, HD)
        o = wa * oa + wb * ob
        t = wa * (ta + (da - drift) * oa) + wb * (tb + (db - drift) * ob)
        out_ref[rows, 0:32, :] = o.astype(bf16).reshape(QB, THIRD, HD)
        out_ref[rows, 32:64, :] = t.astype(bf16).reshape(QB, THIRD, HD)


CT = 512


def project_kernel(side_ref, x_ref, w_ref, seg_ref, gate_ref, gate_tan_ref, *refs, own):
    if own:
        resid_ref, resid_tan_ref, keep_ref, send_ref, lhs_ref = refs
    else:
        keep_ref, send_ref, lhs_ref = refs

    @pl.when(pl.program_id(0) == 0)
    def _():
        for h in range(NH):
            for t in range(PARTS):
                s = h * PARTS + t
                lhs_ref[t * 32 : t * 32 + 32, h * HD : (h + 1) * HD] = x_ref[s, 0:32, :]
                lhs_ref[96 + t * 32 : 128 + t * 32, h * HD : (h + 1) * HD] = x_ref[s, 32:64, :]

    out = jnp.dot(lhs_ref[...], w_ref[...], preferred_element_type=f32)
    one = seg_ref[...] == 1.0
    gate = jnp.where(one, gate_ref[1:2, :], gate_ref[0:1, :])
    gate_tan = jnp.where(one, gate_tan_ref[1:2, :], gate_tan_ref[0:1, :])
    a = gate * out[0:96]
    b = gate_tan * out[0:96] + gate * out[96:192]
    if own:
        a = a + resid_ref[...]
        b = b + resid_tan_ref[...]
    keep_ref[0] = a
    keep_ref[1] = b
    send_ref[0] = a.astype(bf16)
    send_ref[1] = b.astype(bf16)


def project(side, x, w, seg, gate, gate_tan, resid, resid_tan, own):
    steps = HALF // CT
    table = pl.BlockSpec((2, CT), lambda j, s: (0, s[0] * steps + j))
    here = pl.BlockSpec((2, ROWS, CT), lambda j, s: (0, 0, j))
    rows = pl.BlockSpec((ROWS, CT), lambda j, s: (0, j))
    return pl.pallas_call(
        lambda *refs: project_kernel(*refs, own=own),
        grid_spec=pltpu.PrefetchScalarGridSpec(
            num_scalar_prefetch=1,
            grid=(steps,),
            in_specs=[
                pl.BlockSpec((CHIPS, 64, HD), lambda j, s: (0, 0, 0)),
                pl.BlockSpec((NH * HD, CT), lambda j, s: (0, s[0] * steps + j)),
                pl.BlockSpec((ROWS, 1), lambda j, s: (0, 0)),
                table,
                table,
            ]
            + [rows, rows] * own,
            out_specs=[here, here],
            scratch_shapes=[pltpu.VMEM((2 * ROWS, NH * HD), bf16)],
        ),
        out_shape=[
            jax.ShapeDtypeStruct((2, ROWS, HALF), f32),
            jax.ShapeDtypeStruct((2, ROWS, HALF), bf16),
        ],
        compiler_params=params(),
        cost_estimate=pl.CostEstimate(flops=2 * 192 * 1280 * HALF, bytes_accessed=12 * 2**20, transcendentals=0),
    )(side, x, w, seg, gate, gate_tan, *([resid, resid_tan] if own else []))


FT = 32


def final_kernel(
    side_ref, mine_ref, other_ref, got_mine_ref, got_other_ref, seg_ref, scale_ref, scale_tan_ref, shift_ref, shift_tan_ref,
    resid_ref, resid_tan_ref, ffn_ref, ffn_tan_ref,
):
    a = (mine_ref[0] + got_mine_ref[0].astype(f32), other_ref[0] + got_other_ref[0].astype(f32))
    b = (mine_ref[1] + got_mine_ref[1].astype(f32), other_ref[1] + got_other_ref[1].astype(f32))
    resid_ref[...] = a[0]
    resid_tan_ref[...] = b[0]

    def total(x, y):
        return (jnp.sum(x, axis=1, keepdims=True) + jnp.sum(y, axis=1, keepdims=True)) / D

    mean = total(a[0], a[1])
    rstd = lax.rsqrt(total(a[0] * a[0], a[1] * a[1]) - mean * mean + norm_eps)
    mean_tan = total(b[0], b[1])
    cov = total(a[0] * b[0], a[1] * b[1]) - mean * mean_tan
    slope = rstd * rstd * rstd * cov
    one = seg_ref[...] == 1.0
    side = side_ref[0]
    for i in range(2):
        at = pl.multiple_of((side if i == 0 else 1 - side) * HALF, HALF)
        cols = pl.ds(at, HALF)

        def pick(ref):
            return jnp.where(one, ref[1:2, cols], ref[0:1, cols])

        centered = a[i] - mean
        normed = centered * rstd
        normed_tan = (b[i] - mean_tan) * rstd - centered * slope
        scale = 1.0 + pick(scale_ref)
        ffn_ref[:, cols] = (normed * scale + pick(shift_ref)).astype(bf16)
        ffn_tan_ref[:, cols] = (normed_tan * scale + normed * pick(scale_tan_ref) + pick(shift_tan_ref)).astype(bf16)


def finish(side, mine, other, got_mine, got_other, seg, scale, scale_tan, shift, shift_tan):
    pair = pl.BlockSpec((2, FT, HALF), lambda j, s: (0, j, 0))
    table = pl.BlockSpec((2, D), lambda j, s: (0, 0))
    half = pl.BlockSpec((FT, HALF), lambda j, s: (j, 0))
    full = pl.BlockSpec((FT, D), lambda j, s: (j, 0))
    return pl.pallas_call(
        final_kernel,
        grid_spec=pltpu.PrefetchScalarGridSpec(
            num_scalar_prefetch=1,
            grid=(ROWS // FT,),
            in_specs=[pair] * 4 + [pl.BlockSpec((FT, 1), lambda j, s: (j, 0))] + [table] * 4,
            out_specs=[half, half, full, full],
        ),
        out_shape=[
            jax.ShapeDtypeStruct((ROWS, HALF), f32),
            jax.ShapeDtypeStruct((ROWS, HALF), f32),
            jax.ShapeDtypeStruct((ROWS, D), bf16),
            jax.ShapeDtypeStruct((ROWS, D), bf16),
        ],
        compiler_params=params(),
    )(side, mine, other, got_mine, got_other, seg, scale, scale_tan, shift, shift_tan)


def attend(q, kv, kseg):
    return pl.pallas_call(
        attn_kernel,
        in_specs=[VMEM] * 3,
        out_specs=[VMEM] * 2,
        out_shape=[
            jax.ShapeDtypeStruct((CHIPS, 64, HD), bf16),
            jax.ShapeDtypeStruct((NQ, 8, QR), f32),
        ],
        scratch_shapes=[
            pltpu.VMEM((NK, QR, KR), f32),
            pltpu.VMEM((QR, 256), f32),
            pltpu.VMEM((QR, HD), f32),
            pltpu.VMEM((QR, HD), f32),
            pltpu.VMEM((QR, HD), f32),
            pltpu.VMEM((QR, HD), f32),
            pltpu.SMEM((2, NK), f32),
        ],
        compiler_params=params(),
        cost_estimate=pl.CostEstimate(
            flops=12 * QUERIES * KEYS * HD, bytes_accessed=6 * 2**20, transcendentals=QUERIES * KEYS
        ),
    )(q, kv, kseg)


def body(
    queries, keys, values, queries_tan, keys_tan, values_tan, segments, positions, out_weight,
    residual, residual_tan, gate, gate_tan, mod_scale, mod_scale_tan, mod_shift, mod_shift_tan,
):
    frequency = rope_base ** (-jnp.arange(HD // 2, dtype=f32) / (HD // 2))
    angles = positions.astype(f32)[:, None] * jnp.concatenate([frequency, frequency])[None, :]
    sign = jnp.where(jnp.arange(HD) < HD // 2, -1.0, 1.0).astype(f32)
    cosine, sine = jnp.cos(angles), jnp.sin(angles) * sign[None, :]
    clips = segments.astype(bf16)
    rows = jnp.stack([jnp.zeros((PARTS, 256), bf16).at[:, :ROWS].set(clips[None, :]),
                      jnp.zeros((PARTS, 256), bf16).at[:, :THIRD].set(clips.reshape(PARTS, THIRD))], axis=1)
    tiles = jnp.zeros((PARTS, 16, 256), bf16).at[:, 0:2].set(rows)

    with jax.named_scope("pack"):
        message = pl.pallas_call(
            pack_kernel,
            in_specs=[VMEM] * 9,
            out_specs=VMEM,
            out_shape=jax.ShapeDtypeStruct((CHIPS, MSG, 256), bf16),
            compiler_params=params(),
        )(queries, keys, values, queries_tan, keys_tan, values_tan, cosine, sine, tiles)
    with jax.named_scope("spread"):
        arrived = lax.all_to_all(message, ("z", "y", "x"), 0, 0, tiled=True)
    with jax.named_scope("attend"):
        swap = [(0, 1), (1, 0)]
        asked = lax.slice_in_dim(arrived, 192, MSG, axis=1)
        asked_there = lax.ppermute(asked, "c", swap)
        kseg = arrived[:, 224, :ROWS].astype(f32).reshape(NK, 1, KR)
        part, stats = attend(asked, arrived, kseg)
        part_there, stats_there = attend(asked_there, arrived, kseg)
        part_back = lax.ppermute(part_there, "c", swap)
        stats_back = lax.ppermute(stats_there, "c", swap)
        answer = pl.pallas_call(
            combine_kernel,
            in_specs=[VMEM] * 4,
            out_specs=VMEM,
            out_shape=jax.ShapeDtypeStruct((CHIPS, 64, HD), bf16),
            compiler_params=params(),
        )(part, stats, part_back, stats_back)
    with jax.named_scope("collect"):
        attended = lax.all_to_all(answer, ("z", "y", "x"), 0, 0, tiled=True)
    with jax.named_scope("project"):
        side = lax.axis_index("head").astype(jnp.int32).reshape(1)
        seg = segments.astype(f32)[:, None]
        swap = [(0, 1), (1, 0)]
        other, other_low = project(1 - side, attended, out_weight, seg, gate, gate_tan, None, None, False)
        got_mine = lax.ppermute(other_low, "head", swap)
        mine, mine_low = project(side, attended, out_weight, seg, gate, gate_tan, residual, residual_tan, True)
        got_other = lax.ppermute(mine_low, "head", swap)
    with jax.named_scope("norm"):
        return tuple(
            finish(side, mine, other, got_mine, got_other, seg, mod_scale, mod_scale_tan, mod_shift, mod_shift_tan)
        )


def solution(mesh):
    fine = Mesh(mesh.devices.reshape(4, 4, 2, 2, 2), ("z", "y", "x", "c", "head"))
    seq = ("z", "y", "x", "c")
    split = P(seq, "head")
    in_specs = (split,) * 6 + (P(seq), P(seq), P("head", None), split, split) + (P(),) * 6
    out_specs = (split, split, P(seq, None), P(seq, None))
    return jax.shard_map(body, mesh=fine, in_specs=in_specs, out_specs=out_specs, check_vma=False)
```

time: 656 us -> 210 us (0.32)
  blocking collectives: 335 us -> 61.1 us
  matrix products: 114 us -> 0 us
  local copies, waits for them, and re-layouts: 100 us -> 7.3 us
  Pallas kernels: 0 us -> 77 us
  other arithmetic: 25.7 us -> 4.93 us
  waiting for transfers between devices: 62.7 us -> 47 us
  between operations: 14.8 us -> 0.73 us
  starting transfers between devices: 0.2 us -> 11.2 us
    unnamed x1 -> x0, blocking collectives: 335 us -> none
    dot_general x7 -> x0, matrix products: 114 us -> none  [the longest x1 27.5 us: body(): jnp.einsum('qhd,khd->hqk', query_heads, key_tan_heads, preferred_element_...]
    all_gather x4 -> x0, local copies, waits for them, and re-layouts: 79.8 us -> none  [the longest x1 20.8 us: body(): key_tan_piece = lax.all_gather(rotated_keys_tan, 'seq', axis=0, tiled=True)]
    pallas_call x0 -> x7, Pallas kernels: none -> 77 us  [the longest x2 48.1 us: attend(): pl.pallas_call(attn_kernel, in_specs=[VMEM] * 3, out_specs=[VMEM] * 2, ou...]
    psum x1 -> x0, waiting for transfers between devices: 61.4 us -> none  [body(): lax.psum((branch_term + lifted).astype(jnp.bfloat16), 'head')]
    all_to_all x0 -> x1, blocking collectives: none -> 61.1 us  [body(): arrived = lax.all_to_all(message, ('z', 'y', 'x'), 0, 0, tiled=True)]
    ppermute x0 -> x5, waiting for transfers between devices: none -> 33.8 us  [the longest x1 18.7 us: body(): got_other = lax.ppermute(mine_low, 'head', swap)]
    reduce_sum x2 -> x0, other arithmetic: 13.5 us -> none  [the longest x1 11.3 us: body(): jnp.sum(raised, axis=2)]
  transfers between devices with their start and end apart: 5 -> 6, of which waited for: 1 -> 3; matrix products, arithmetic and copies ran while one was open for 24% -> 1% of each run, Pallas kernels for 0% -> 15%
where the time goes in v1:
time: 210 us; the launch traced here: 209 us
  Pallas kernels  77 us (37%)
  blocking collectives  61.1 us (29%)
  waiting for transfers between devices  47 us (22%)
  starting transfers between devices  11.2 us (5%)
  local copies, waits for them, and re-layouts  7.3 us (3%)
  other arithmetic  4.93 us (2%)
    all_to_all x1, blocking collectives, body(): arrived = lax.all_to_all(message, ('z', 'y', 'x'), 0, 0, tiled=True)  61.1 us
    pallas_call x2, Pallas kernels, attend(): pl.pallas_call(attn_kernel, in_specs=[VMEM] * 3, out_specs=[VMEM] * 2, ou...  48.1 us
    ppermute x1, waiting for transfers between devices, body(): got_other = lax.ppermute(mine_low, 'head', swap)  18.7 us
    ppermute x1, waiting for transfers between devices, body(): got_mine = lax.ppermute(other_low, 'head', swap)  15.1 us
    pallas_call x2, Pallas kernels, project(): pl.pallas_call(lambda *refs: project_kernel(*refs, own=own), grid_spec=pl...  15.1 us
    all_to_all x1, waiting for transfers between devices, body(): attended = lax.all_to_all(answer, ('z', 'y', 'x'), 0, 0, tiled=True)  13.2 us
    all_to_all x1, starting transfers between devices, body(): attended = lax.all_to_all(answer, ('z', 'y', 'x'), 0, 0, tiled=True)  8.61 us
    pallas_call x1, Pallas kernels, finish(): pl.pallas_call(final_kernel, grid_spec=pltpu.PrefetchScalarGridSpec(num_s...  6.14 us
  transfers between devices with their start and end apart: 6, of which 3 were waited for; matrix products, arithmetic and copies ran while one was open for 1% of the time, Pallas kernels for 15%

profile of v1, /device:TPU:0, one launch (start us, length us, event | category | flops | bytes accessed | tf_op | source)
XLA Modules:
  0.0 209.3 jit_solution(14109311199161127728)
XLA Ops:
  0.6 0.6 compare_reduce_fusion.1
  1.3 0.6 compare_reduce_fusion
  1.9 0.7 convert_element_type.22
  2.6 0.1 compare_select_fusion.1
  2.7 2.0 broadcast_select_fusion.1
  4.6 0.1 stack.15
  4.7 0.6 scatter.20.seg_ref
  5.3 0.9 fusion
  6.2 4.0 %pack.1 = bf16[32,240,256]{2,1,0:T(8,128)(2,1)} custom-call(bf16[96,1280]{1,0:T(8,128)(2,1)} %q_ref.1, bf16[96,1280]{1,0:T(8,128)(2,1)} %k_ref.1, bf16[96,1280]{1,0:T(8,128)(2,1)} %v_ref.1, bf16[96,1280]{1,0:T(8,128)(2,1)} %qt_ref.1, bf16[96,1280]{1,0:T(8,128)(2,1)} %kt_ref.1, bf16[96,1280]{1,0:T(8,128)(2,1)} %vt_ref.1, ...), custom_call_target="tpu_custom_call" | custom-call | tf_op jit(solution)/shard_map/pack/pallas_call | solution.py:327
  10.2 61.1 %all_to_all.10.kv_ref = bf16[32,240,256]{2,1,0:T(8,128)(2,1)S(1)} all-to-all(bf16[32,240,256]{2,1,0:T(8,128)(2,1)} %pack.1), channel_id=1, replica_groups=mesh['z'=4,'y'=4,'x'=2,'c'=2,'head'=2] {'z','y','x'}, dimensions={0} | all-to-all | bytes 7864320 | tf_op jit(solution)/shard_map/spread/all_to_all | solution.py:335
  71.4 0.0 copy-start
  71.4 0.1 slice.61.q_ref
  71.4 0.0 copy-start.4
  71.4 0.1 collective-permute-start
  71.5 1.7 copy-done
  73.3 0.7 reshape.130.kseg_ref
  73.9 0.0 collective-permute-done.q_ref
  73.9 0.0 copy-start.8
  73.9 0.9 copy-done.8
  74.8 24.1 %attend.4 = (bf16[32,64,128]{2,1,0:T(8,128)(2,1)}, f32[4,8,256]{2,1,0:T(8,128)}) custom-call(bf16[32,48,256]{2,1,0:T(8,128)(2,1)} %copy-done.8, bf16[32,240,256]{2,1,0:T(8,128)(2,1)} %copy-done, f32[8,1,384]{2,1,0:T(1,128)} %reshape.130.kseg_ref), custom_call_target="tpu_custom_call" | custom-call | flops 4831838208 | bytes 6291456 | tf_op jit(solution)/shard_map/attend/pallas_call | solution.py:289
  98.9 0.0 copy-done.4
  98.9 0.0 collective-permute-start.1
  98.9 0.0 copy-start.7
  98.9 0.5 collective-permute-start.2
  99.4 24.0 %attend.3 = (bf16[32,64,128]{2,1,0:T(8,128)(2,1)}, f32[4,8,256]{2,1,0:T(8,128)}) custom-call(bf16[32,48,256]{2,1,0:T(8,128)(2,1)} %copy-done.4, bf16[32,240,256]{2,1,0:T(8,128)(2,1)} %copy-done, f32[8,1,384]{2,1,0:T(1,128)} %reshape.130.kseg_ref), custom_call_target="tpu_custom_call" | custom-call | flops 4831838208 | bytes 6291456 | tf_op jit(solution)/shard_map/attend/pallas_call | solution.py:289
  123.4 0.0 collective-permute-done.2.sb_ref
  123.4 0.0 copy-start.6
  123.4 0.0 collective-permute-done.1.b_ref
  123.4 0.0 copy-start.5
  123.5 0.6 copy-done.6
  124.1 0.2 copy-done.5
  124.2 3.7 %attend.5 = bf16[32,64,128]{2,1,0:T(8,128)(2,1)} custom-call(bf16[32,64,128]{2,1,0:T(8,128)(2,1)} %get-tuple-element.48.a_ref, f32[4,8,256]{2,1,0:T(8,128)} %get-tuple-element.49.sa_ref, bf16[32,64,128]{2,1,0:T(8,128)(2,1)} %copy-done.5, f32[4,8,256]{2,1,0:T(8,128)} %copy-done.6), custom_call_target="tpu_custom_call" | custom-call | tf_op jit(solution)/shard_map/attend/pallas_call | solution.py:345
  127.9 8.6 %all-to-all-start.1 = ((bf16[32,64,128]{2,1,0:T(8,128)(2,1)}), bf16[32,64,128]{2,1,0:T(8,128)(2,1)S(1)}, u32[]{:S(2)}, u32[]{:S(2)}) async-start(bf16[32,64,128]{2,1,0:T(8,128)(2,1)} %attend.5), calls=%async_computation.1 | async-start | bytes 1048576 | tf_op jit(solution)/shard_map/collect/all_to_all | solution.py:353
  136.6 0.0 copy-done.7
  136.6 0.7 copy.22.refs_3_.seg_ref
  137.3 13.2 %all-to-all-done.1.refs_1_ = bf16[32,64,128]{2,1,0:T(8,128)(2,1)S(1)} async-done(((bf16[32,64,128]{2,1,0:T(8,128)(2,1)}), bf16[32,64,128]{2,1,0:T(8,128)(2,1)S(1)}, u32[]{:S(2)}, u32[]{:S(2)}) %all-to-all-start.1) | async-done | bytes 524320 | tf_op jit(solution)/shard_map/collect/all_to_all | solution.py:353
  150.5 0.0 copy-start.1
  150.5 0.8 copy-done.1
  151.3 7.3 %project.3 = (f32[2,96,2560]{2,1,0:T(8,128)}, bf16[2,96,2560]{2,1,0:T(8,128)(2,1)}) custom-call(s32[1]{0:T(128)S(6)} %sub.3.refs_0_, bf16[32,64,128]{2,1,0:T(8,128)(2,1)} %copy-done.1, bf16[1280,5120]{1,0:T(8,128)(2,1)} %refs_2_.3, f32[96,1]{1,0:T(8,128)} %copy.22.refs_3_.seg_ref, f32[2,5120]{1,0:T(2,128)} %refs_4_.3, f32[2,5120]{1,0:T(2,128)} %refs_5_.3), custom_call_target="tpu_custom_call" | custom-call | flops 1258291200 | bytes 12582912 | tf_op jit(solution)/shard_map/project/pallas_call | solution.py:203
  158.6 0.5 collective-permute-start.3
  159.2 7.8 %project.2 = (f32[2,96,2560]{2,1,0:T(8,128)}, bf16[2,96,2560]{2,1,0:T(8,128)(2,1)}) custom-call(s32[1]{0:T(128)} %bitcast.refs_0_.side_ref, bf16[32,64,128]{2,1,0:T(8,128)(2,1)} %copy-done.1, bf16[1280,5120]{1,0:T(8,128)(2,1)} %refs_2_.3, f32[96,1]{1,0:T(8,128)} %copy.22.refs_3_.seg_ref, f32[2,5120]{1,0:T(2,128)} %refs_4_.3, f32[2,5120]{1,0:T(2,128)} %refs_5_.3, ...), custom_call_target="tpu_custom_call" | custom-call | flops 1258291200 | bytes 12582912 | tf_op jit(solution)/shard_map/project/pallas_call | solution.py:203
  166.9 1.5 collective-permute-start.4
  168.5 15.1 %collective-permute-done.3.got_mine_ref = bf16[2,96,2560]{2,1,0:T(8,128)(2,1)S(1)} collective-permute-done((bf16[2,96,2560]{2,1,0:T(8,128)(2,1)}, bf16[2,96,2560]{2,1,0:T(8,128)(2,1)S(1)}, u32[]{:S(2)}, u32[]{:S(2)}) %collective-permute-start.3) | collective-permute-done | bytes 983072 | tf_op jit(solution)/shard_map/project/ppermute | solution.py:359
  183.6 0.0 copy-start.2
  183.6 18.7 %collective-permute-done.4.got_other_ref = bf16[2,96,2560]{2,1,0:T(8,128)(2,1)S(1)} collective-permute-done((bf16[2,96,2560]{2,1,0:T(8,128)(2,1)}, bf16[2,96,2560]{2,1,0:T(8,128)(2,1)S(1)}, u32[]{:S(2)}, u32[]{:S(2)}) %collective-permute-start.4) | collective-permute-done | bytes 983072 | tf_op jit(solution)/shard_map/project/ppermute | solution.py:361
  202.2 0.0 copy-done.2
  202.2 1.0 copy-done.3
  203.2 6.1 %norm.1 = (f32[96,2560]{1,0:T(8,128)}, f32[96,2560]{1,0:T(8,128)}, bf16[96,5120]{1,0:T(8,128)(2,1)}, bf16[96,5120]{1,0:T(8,128)(2,1)}) custom-call(s32[1]{0:T(128)} %bitcast.refs_0_.side_ref, f32[2,96,2560]{2,1,0:T(8,128)} %get-tuple-element.52.mine_ref, f32[2,96,2560]{2,1,0:T(8,128)} %get-tuple-element.53.other_ref, bf16[2,96,2560]{2,1,0:T(8,128)(2,1)} %copy-done.2, ...), custom_call_target="tpu_custom_call" | custom-call | tf_op jit(solution)/shard_map/norm/pallas_call | solution.py:270
  (7 shorter events, 0.1 us)
Async XLA Ops:
  71.4 1.9 copy-start
  71.4 27.5 %copy-start.4 = (bf16[32,48,256]{2,1,0:T(8,128)(2,1)}, bf16[32,48,256]{2,1,0:T(8,128)(2,1)S(1)}, u32[]{:S(2)}) copy-start(bf16[32,48,256]{2,1,0:T(8,128)(2,1)S(1)} %slice.61.q_ref) | copy-start | bytes 2359300
  71.4 2.5 %collective-permute-start = (bf16[32,48,256]{2,1,0:T(8,128)(2,1)S(1)}, bf16[32,48,256]{2,1,0:T(8,128)(2,1)S(1)}, u32[]{:S(2)}, u32[]{:S(2)}) collective-permute-start(bf16[32,48,256]{2,1,0:T(8,128)(2,1)S(1)} %slice.61.q_ref), channel_id=1, source_target_pairs={{0,2},{2,0},{1,3},{3,1},{4,6},{6,4},{5,7},{7,5},{8,10},{10,8},{9,1... | collective-permute-start | bytes 2359304 | tf_op jit(solution)/shard_map/attend/ppermute | solution.py:339
  73.9 0.9 copy-start.8
  98.9 24.6 %collective-permute-start.1 = (bf16[32,64,128]{2,1,0:T(8,128)(2,1)}, bf16[32,64,128]{2,1,0:T(8,128)(2,1)S(1)}, u32[]{:S(2)}, u32[]{:S(2)}) collective-permute-start(bf16[32,64,128]{2,1,0:T(8,128)(2,1)} %get-tuple-element.50), channel_id=1, source_target_pairs={{0,2},{2,0},{1,3},{3,1},{4,6},{6,4},{5,7},{7,5},{8,10},{10,8},{9,1... | collective-permute-start | bytes 1572872 | tf_op jit(solution)/shard_map/attend/ppermute | solution.py:343
  98.9 37.7 %copy-start.7 = (s32[96]{0:T(128)S(1)}, s32[96]{0:T(128)}, u32[]{:S(2)}) copy-start(s32[96]{0:T(128)} %param.29) | copy-start | bytes 1156
  98.9 24.5 %collective-permute-start.2 = (f32[4,8,256]{2,1,0:T(8,128)}, f32[4,8,256]{2,1,0:T(8,128)S(1)}, u32[]{:S(2)}, u32[]{:S(2)}) collective-permute-start(f32[4,8,256]{2,1,0:T(8,128)} %get-tuple-element.51), channel_id=1, source_target_pairs={{0,2},{2,0},{1,3},{3,1},{4,6},{6,4},{5,7},{7,5},{8,10},{10,8},{9,1... | collective-permute-start | bytes 98312 | tf_op jit(solution)/shard_map/attend/ppermute | solution.py:344
  123.4 0.6 copy-start.6
  123.4 0.8 copy-start.5
  127.9 22.6 %all-to-all-start.1 = ((bf16[32,64,128]{2,1,0:T(8,128)(2,1)}), bf16[32,64,128]{2,1,0:T(8,128)(2,1)S(1)}, u32[]{:S(2)}, u32[]{:S(2)}) async-start(bf16[32,64,128]{2,1,0:T(8,128)(2,1)} %attend.5), calls=%async_computation.1 | async-start | bytes 1048576 | tf_op jit(solution)/shard_map/collect/all_to_all | solution.py:353
  150.5 0.8 copy-start.1
  158.6 24.9 %collective-permute-start.3 = (bf16[2,96,2560]{2,1,0:T(8,128)(2,1)}, bf16[2,96,2560]{2,1,0:T(8,128)(2,1)S(1)}, u32[]{:S(2)}, u32[]{:S(2)}) collective-permute-start(bf16[2,96,2560]{2,1,0:T(8,128)(2,1)} %get-tuple-element.54), channel_id=1, source_target_pairs={{0,1},{1,0},{2,3},{3,2},{4,5},{5,4},{6,7},{7,6},{8,9},{9,8},{10,11... | collective-permute-start | bytes 2949128 | tf_op jit(solution)/shard_map/project/ppermute | solution.py:359
  166.9 35.3 %collective-permute-start.4 = (bf16[2,96,2560]{2,1,0:T(8,128)(2,1)}, bf16[2,96,2560]{2,1,0:T(8,128)(2,1)S(1)}, u32[]{:S(2)}, u32[]{:S(2)}) collective-permute-start(bf16[2,96,2560]{2,1,0:T(8,128)(2,1)} %get-tuple-element.55), channel_id=1, source_target_pairs={{0,1},{1,0},{2,3},{3,2},{4,5},{5,4},{6,7},{7,6},{8,9},{9,8},{10,11... | collective-permute-start | bytes 2949128 | tf_op jit(solution)/shard_map/project/ppermute | solution.py:361
  183.6 18.7 %copy-start.2 = (bf16[2,96,2560]{2,1,0:T(8,128)(2,1)}, bf16[2,96,2560]{2,1,0:T(8,128)(2,1)S(1)}, u32[]{:S(2)}) copy-start(bf16[2,96,2560]{2,1,0:T(8,128)(2,1)S(1)} %collective-permute-done.3.got_mine_ref) | copy-start | bytes 2949124
  202.2 1.0 copy-start.3

commit v2 on v1

v2 whole, which is shorter than its diff:
```python
import math

import jax
import jax.numpy as jnp
from jax import lax
from jax.experimental import pallas as pl
from jax.experimental.pallas import tpu as pltpu
from jax.sharding import Mesh, PartitionSpec as P

D = 5120
HD = 128
NH = 10
ROWS = 96
THIRD = 32
CHIPS = 32
PARTS = 3
MSG = 240
HALF = D // 2

ROUNDS = 2
W = THIRD // ROUNDS
SB = 8
KR = SB * ROWS
LONG, SHORT = (21, 3), (13, 2)
RMAX = LONG[0] * 2 * W

neg_fill = -1e30
norm_eps = 1e-06
rope_base = 10000.0
ln2 = math.log(2.0)
exp_scale = math.log2(math.e) / math.sqrt(HD)

f32 = jnp.float32
bf16 = jnp.bfloat16
i32 = jnp.int32
VMEM = pl.BlockSpec(memory_space=pltpu.VMEM)
ANY = pl.BlockSpec(memory_space=pl.ANY)
NT = (((1,), (1,)), ((), ()))


def params(mib):
    return pltpu.CompilerParams(vmem_limit_bytes=mib * 2**20)


def pack_kernel(q_ref, k_ref, v_ref, qt_ref, kt_ref, vt_ref, cos_ref, sin_ref, seg_ref, row_ref, out_ref):
    cos = cos_ref[...]
    sin = sin_ref[...]
    lane = lax.broadcasted_iota(i32, (ROWS, HD), 1)
    clips = jnp.where(lane == 0, seg_ref[...], row_ref[...]).astype(bf16)

    def rot(ref, cols, factor):
        x = ref[:, cols].astype(f32)
        y = x * cos + jnp.roll(x, HD // 2, axis=1) * sin
        return (y if factor is None else y * factor).astype(bf16)

    for h in range(NH):
        cols = slice(h * HD, (h + 1) * HD)
        k, kt = rot(k_ref, cols, None), rot(kt_ref, cols, None)
        q, qt = rot(q_ref, cols, exp_scale), rot(qt_ref, cols, exp_scale)
        v, vt = v_ref[:, cols], vt_ref[:, cols]
        for t in range(PARTS):
            s = h * PARTS + t
            at = t * THIRD
            out_ref[s, 0:96, 0:128] = k
            out_ref[s, 0:96, 128:256] = kt
            out_ref[s, 96:192, 0:128] = v
            out_ref[s, 96:192, 128:256] = vt
            out_ref[s, 192:224, 0:128] = qt[at : at + 32]
            out_ref[s, 192:224, 128:256] = q[at : at + 32]
            out_ref[s, 224:240, 0:128] = clips[at : at + 16]
            out_ref[s, 224:240, 128:256] = clips[at + 16 : at + 32]
    for s in range(NH * PARTS, CHIPS):
        out_ref[s] = jnp.zeros((MSG, 256), bf16)


def bits(tiles):
    rows = jnp.concatenate([t.astype(f32)[0:1, :] for t in tiles], axis=0)
    lane = lax.broadcasted_iota(i32, (CHIPS, HD), 1)
    at = lax.broadcasted_iota(i32, (CHIPS, 1), 0)
    power = jnp.left_shift(jnp.ones((CHIPS, 1), i32), at & 15).astype(f32)
    has0 = 1.0 - jnp.min(jnp.where(lane < 32, 1.0, rows), axis=1, keepdims=True)
    has1 = jnp.max(jnp.where(lane < 32, 0.0, rows), axis=1, keepdims=True)

    def scalar(has):
        low = jnp.sum(jnp.where(at < 16, has * power, 0.0)).astype(i32)
        high = jnp.sum(jnp.where(at < 16, 0.0, has * power)).astype(i32)
        return low | (high << 16)

    return scalar(has0), scalar(has1)


def attn_kernel(qa_ref, qb_ref, kv_ref, tie_ref, oa_ref, ob_ref, s_ref, acc_ref, acct_ref, l_ref, pen_ref, keys_ref, kind_ref, chips_ref, cut_ref, *, turn):
    del tie_ref
    own = bits([kv_ref[j, 224:240, 0:128] for j in range(CHIPS)])
    sib = bits([qb_ref[j, 32:48, 0:128] for j in range(CHIPS)])
    cut_ref[0] = i32(0)
    cut_ref[1] = i32(0)

    def sort(j, carry):
        cuts, counts = carry[0], list(carry[1:])
        has = [(own[c] >> j) & 1 for c in range(2)]
        both = has[0] & has[1]
        cut_ref[jnp.where(both == 1, jnp.minimum(cuts, 1), 2)] = j
        for c in range(2):
            at = jnp.where(has[c] == 1, counts[c], 31 - (j - counts[c]))
            keys_ref[c, at] = j
            kind_ref[c, at] = jnp.where(both == 1, 2 + 2 * c + jnp.minimum(cuts, 1), 1 - has[c])
            counts[c] = counts[c] + has[c]
            any_has = ((own[c] | sib[c]) >> j) & 1
            n = counts[2 + c]
            chips_ref[c, jnp.where(any_has == 1, n, 31 - (j - n))] = j
            counts[2 + c] = n + any_has
        return (cuts + both, *counts)

    zero = i32(0)
    counted = lax.fori_loop(0, CHIPS, sort, (zero,) * 5)
    long_clip = jnp.where(counted[4] > 16, 1, 0)

    lane = lax.broadcasted_iota(i32, (ROWS, HD), 1)
    eye = lane == lax.broadcasted_iota(i32, (ROWS, HD), 0) + 32
    pen_ref[0] = jnp.zeros((ROWS, HD), bf16)
    pen_ref[1] = jnp.where(lane == 0, neg_fill, 0.0).astype(bf16)
    for p in range(2):
        row = kv_ref[cut_ref[p], 224:240, 0:128].astype(f32)[0:1, :]
        col = jnp.sum(jnp.where(eye, row, 0.0), axis=1, keepdims=True)
        pen_ref[2 + p] = jnp.where(lane == 0, col * neg_fill, 0.0).astype(bf16)
        pen_ref[4 + p] = jnp.where(lane == 0, (1.0 - col) * neg_fill, 0.0).astype(bf16)

    rows = slice(turn * W, (turn + 1) * W)
    tag = slice(turn * HD, turn * HD + HD)
    for (chips, blocks), clip in ((LONG, long_clip), (SHORT, 1 - long_clip)):
        R = chips * 2 * W
        listed = [chips_ref[clip, i] for i in range(chips)]
        qq = jnp.concatenate([ref[j, rows, :] for j in listed for ref in (qa_ref, qb_ref)], axis=0)
        one = jnp.where(lax.broadcasted_iota(i32, (R, HD), 1) == 0, 1.0, 0.0).astype(bf16)
        q = jnp.concatenate([qq[:, 128:256], one], axis=1)
        m = jnp.full((R, HD), neg_fill, f32)
        for b in range(blocks):
            pairs = [(keys_ref[clip, b * SB + u], kind_ref[clip, b * SB + u]) for u in range(SB)]
            k = jnp.concatenate([jnp.concatenate([kv_ref[j, 0:96, 0:128], pen_ref[n]], axis=1) for j, n in pairs], axis=0)
            s = lax.dot_general(q, k, NT, preferred_element_type=f32)
            s_ref[b, 0:R] = s
            for j in range(KR // HD):
                m = jnp.maximum(m, s[:, j * HD : (j + 1) * HD])
        top = jnp.max(m, axis=1, keepdims=True)
        for b in range(blocks):
            js = [keys_ref[clip, b * SB + u] for u in range(SB)]
            k = jnp.concatenate([kv_ref[j, 0:96, :] for j in js], axis=0)
            v = jnp.concatenate([kv_ref[j, 96:192, :] for j in js], axis=0)
            v1 = jnp.concatenate([v[:, 0:128], jnp.ones((KR, HD), bf16)], axis=1)
            st = lax.dot_general(qq, k, NT, preferred_element_type=f32)
            p = jnp.exp2(s_ref[b, 0:R] - top)
            pt = (p * st).astype(bf16)
            l = p[:, 0:HD]
            for j in range(1, KR // HD):
                l = l + p[:, j * HD : (j + 1) * HD]
            acc = jnp.dot(p.astype(bf16), v, preferred_element_type=f32)
            acct = jnp.dot(pt, v1, preferred_element_type=f32)
            if b == 0:
                l_ref[0:R], acc_ref[0:R], acct_ref[0:R] = l, acc, acct
            else:
                l_ref[0:R] += l
                acc_ref[0:R] += acc
                acct_ref[0:R] += acct
        total = jnp.sum(l_ref[0:R], axis=1, keepdims=True)
        inv = 1.0 / total
        inv_tan = inv * ln2
        drift = acct_ref[0:R, 128:256] * inv_tan
        o = acc_ref[0:R, 0:128] * inv
        t = acct_ref[0:R, 0:128] * inv_tan + acc_ref[0:R, 128:256] * inv - drift * o
        lse = jnp.broadcast_to(top + jnp.log2(total), (R, HD))
        where = lax.broadcasted_iota(i32, (R, HD), 1)
        pieces = jnp.zeros((R, HD), f32)
        for first, x in ((0, lse), (3, drift)):
            for i in range(3):
                piece = x.astype(bf16).astype(f32)
                pieces = jnp.where(where == first + i, piece, pieces)
                x = x - piece
        whole = [x.astype(bf16) for x in (o, t, pieces)]
        wanted = clip.astype(f32)
        for i, j in enumerate(listed):
            for core, (q_ref, out_ref) in enumerate(((qa_ref, oa_ref), (qb_ref, ob_ref))):
                at = (2 * i + core) * W
                hit = jnp.broadcast_to(q_ref[j, 32:48, tag].astype(f32)[:, 0:1], (W, HD)) == wanted
                for n, x in enumerate(whole):
                    old = out_ref[j, n * W : (n + 1) * W, :].astype(f32)
                    out_ref[j, n * W : (n + 1) * W, :] = jnp.where(hit, x[at : at + W].astype(f32), old).astype(bf16)


def attend(asked, asked_there, arrived, tie, turn):
    out = jax.ShapeDtypeStruct((CHIPS, 3 * W, HD), bf16)
    return pl.pallas_call(
        lambda *refs: attn_kernel(*refs, turn=turn),
        in_specs=[VMEM, VMEM, VMEM, ANY],
        out_specs=[VMEM] * 2,
        out_shape=[out, out],
        scratch_shapes=[
            pltpu.VMEM((LONG[1], RMAX, KR), f32),
            pltpu.VMEM((RMAX, 256), f32),
            pltpu.VMEM((RMAX, 256), f32),
            pltpu.VMEM((RMAX, HD), f32),
            pltpu.VMEM((6, ROWS, HD), bf16),
            pltpu.SMEM((2, CHIPS), i32),
            pltpu.SMEM((2, CHIPS), i32),
            pltpu.SMEM((2, CHIPS), i32),
            pltpu.SMEM((3,), i32),
        ],
        compiler_params=params(32),
        cost_estimate=pl.CostEstimate(flops=5 * 10**9, bytes_accessed=6 * 2**20, transcendentals=2 * 10**6),
    )(asked, asked_there, arrived, tie)


def combine_kernel(a_ref, b_ref, tie_ref, out_ref):
    del tie_ref
    R = CHIPS * W

    def read(ref):
        o, t, s = [ref[:, n * W : (n + 1) * W, :].astype(f32).reshape(R, HD) for n in range(3)]
        lse = s[:, 0:1] + s[:, 1:2] + s[:, 2:3]
        drift = s[:, 3:4] + s[:, 4:5] + s[:, 5:6]
        return o, t, lse, drift

    oa, ta, la, da = read(a_ref)
    ob, tb, lb, db = read(b_ref)
    top = jnp.maximum(la, lb)
    wa, wb = jnp.exp2(la - top), jnp.exp2(lb - top)
    inv = 1.0 / (wa + wb)
    wa, wb = wa * inv, wb * inv
    gap = wa * wb * (da - db)
    out_ref[:, 0:W, :] = (wa * oa + wb * ob).astype(bf16).reshape(CHIPS, W, HD)
    out_ref[:, W : 2 * W, :] = (wa * ta + wb * tb + gap * (oa - ob)).astype(bf16).reshape(CHIPS, W, HD)


def combine(a, b, tie):
    return pl.pallas_call(
        combine_kernel,
        in_specs=[VMEM, VMEM, ANY],
        out_specs=VMEM,
        out_shape=jax.ShapeDtypeStruct((CHIPS, 2 * W, HD), bf16),
        compiler_params=params(24),
    )(a, b, tie)


CT = 512
RT = PARTS * W


def project_kernel(side_ref, x_ref, w_ref, seg_ref, gate_ref, gate_tan_ref, resid_ref, resid_tan_ref, keep_ref, send_ref, lhs_ref):
    step = pl.program_id(0)

    @pl.when(step == 0)
    def _():
        for h in range(NH):
            for t in range(PARTS):
                s = h * PARTS + t
                lhs_ref[t * W : (t + 1) * W, h * HD : (h + 1) * HD] = x_ref[s, 0:W, :]
                lhs_ref[RT + t * W : RT + (t + 1) * W, h * HD : (h + 1) * HD] = x_ref[s, W : 2 * W, :]

    out = jnp.dot(lhs_ref[...], w_ref[...], preferred_element_type=f32)
    one = seg_ref[...].reshape(RT, 1) == 1.0
    gate = jnp.where(one, gate_ref[1:2, :], gate_ref[0:1, :])
    gate_tan = jnp.where(one, gate_tan_ref[1:2, :], gate_tan_ref[0:1, :])
    mine = jnp.where(step // (HALF // CT) == side_ref[0], 1.0, 0.0).astype(f32)
    a = gate * out[0:RT] + mine * resid_ref[...].reshape(RT, CT)
    b = gate_tan * out[0:RT] + gate * out[RT : 2 * RT] + mine * resid_tan_ref[...].reshape(RT, CT)
    keep_ref[0] = a
    keep_ref[1] = b
    send_ref[0] = a.astype(bf16)
    send_ref[1] = b.astype(bf16)


def project(side, x, w, seg, gate, gate_tan, resid, resid_tan, turn):
    half_steps = HALF // CT
    table = pl.BlockSpec((2, CT), lambda j, s: (0, j))
    here = pl.BlockSpec((2, RT, CT), lambda j, s: (0, 0, j))
    rows = pl.BlockSpec((PARTS, None, W, CT), lambda j, s: (0, turn, 0, jnp.clip(j - s[0] * half_steps, 0, half_steps - 1)))
    return pl.pallas_call(
        project_kernel,
        grid_spec=pltpu.PrefetchScalarGridSpec(
            num_scalar_prefetch=1,
            grid=(D // CT,),
            in_specs=[
                pl.BlockSpec((CHIPS, 2 * W, HD), lambda j, s: (0, 0, 0)),
                pl.BlockSpec((NH * HD, CT), lambda j, s: (0, j)),
                pl.BlockSpec((PARTS, None, W, 1), lambda j, s: (0, turn, 0, 0)),
                table,
                table,
                rows,
                rows,
            ],
            out_specs=[here, here],
            scratch_shapes=[pltpu.VMEM((2 * RT, NH * HD), bf16)],
        ),
        out_shape=[
            jax.ShapeDtypeStruct((2, RT, D), f32),
            jax.ShapeDtypeStruct((2, RT, D), bf16),
        ],
        compiler_params=params(24),
        cost_estimate=pl.CostEstimate(flops=2 * 2 * RT * NH * HD * D, bytes_accessed=16 * 2**20, transcendentals=0),
    )(side, x, w, seg, gate, gate_tan, resid, resid_tan)


def norm_kernel(side_ref, keep_ref, got_ref, seg_ref, scale_ref, scale_tan_ref, shift_ref, shift_tan_ref, *refs):
    resid_ref, resid_tan_ref, ffn_ref, ffn_tan_ref = refs[-4:]
    a = keep_ref[0] + got_ref[0].astype(f32)
    b = keep_ref[1] + got_ref[1].astype(f32)
    mine = pl.ds(pl.multiple_of(side_ref[0] * HALF, HALF), HALF)
    resid_ref[...] = keep_ref[0, :, mine] + got_ref[0, :, mine].astype(f32)
    resid_tan_ref[...] = keep_ref[1, :, mine] + got_ref[1, :, mine].astype(f32)

    def average(x):
        return jnp.sum(x, axis=1, keepdims=True) / D

    mean = average(a)
    rstd = lax.rsqrt(average(a * a) - mean * mean + norm_eps)
    mean_tan = average(b)
    cov = average(a * b) - mean * mean_tan
    slope = rstd * rstd * rstd * cov
    one = seg_ref[...] == 1.0

    def pick(ref):
        return jnp.where(one, ref[1:2, :], ref[0:1, :])

    centered = a - mean
    normed = centered * rstd
    normed_tan = (b - mean_tan) * rstd - centered * slope
    scale = 1.0 + pick(scale_ref)
    ffn_ref[...] = (normed * scale + pick(shift_ref)).astype(bf16)
    ffn_tan_ref[...] = (normed_tan * scale + normed * pick(scale_tan_ref) + pick(shift_tan_ref)).astype(bf16)


def norm(side, keep, got, seg, tables, before, turn):
    pair = pl.BlockSpec((2, W, D), lambda j, s: (0, j, 0))
    table = pl.BlockSpec((2, D), lambda j, s: (0, 0))
    half = pl.BlockSpec((None, None, W, HALF), lambda j, s: (j, turn, 0, 0))
    full = pl.BlockSpec((None, None, W, D), lambda j, s: (j, turn, 0, 0))
    return pl.pallas_call(
        norm_kernel,
        grid_spec=pltpu.PrefetchScalarGridSpec(
            num_scalar_prefetch=1,
            grid=(PARTS,),
            in_specs=[pair, pair, pl.BlockSpec((None, None, W, 1), lambda j, s: (j, turn, 0, 0))] + [table] * 4 + [ANY] * len(before),
            out_specs=[half, half, full, full],
        ),
        out_shape=[
            jax.ShapeDtypeStruct((PARTS, ROUNDS, W, HALF), f32),
            jax.ShapeDtypeStruct((PARTS, ROUNDS, W, HALF), f32),
            jax.ShapeDtypeStruct((PARTS, ROUNDS, W, D), bf16),
            jax.ShapeDtypeStruct((PARTS, ROUNDS, W, D), bf16),
        ],
        input_output_aliases={8 + i: i for i in range(len(before))},
        compiler_params=params(24),
    )(side, keep, got, seg, *tables, *before)


def body(
    queries, keys, values, queries_tan, keys_tan, values_tan, segments, positions, out_weight,
    residual, residual_tan, gate, gate_tan, mod_scale, mod_scale_tan, mod_shift, mod_shift_tan,
):
    frequency = rope_base ** (-jnp.arange(HD // 2, dtype=f32) / (HD // 2))
    angles = positions.astype(f32)[:, None] * jnp.concatenate([frequency, frequency])[None, :]
    sign = jnp.where(jnp.arange(HD) < HD // 2, -1.0, 1.0).astype(f32)
    cosine, sine = jnp.cos(angles), jnp.sin(angles) * sign[None, :]
    clips = segments.astype(f32)
    seg = clips[:, None]
    row = jnp.pad(clips, (HD - ROWS, 0))[None, :]
    swap = [(0, 1), (1, 0)]

    with jax.named_scope("pack"):
        message = pl.pallas_call(
            pack_kernel,
            in_specs=[VMEM] * 10,
            out_specs=VMEM,
            out_shape=jax.ShapeDtypeStruct((CHIPS, MSG, 256), bf16),
            compiler_params=params(24),
        )(queries, keys, values, queries_tan, keys_tan, values_tan, cosine, sine, seg, row)
    with jax.named_scope("spread"):
        arrived = lax.all_to_all(message, ("z", "y", "x"), 0, 0, tiled=True)
        asked = lax.slice_in_dim(arrived, 192, MSG, axis=1)
        asked_there = lax.ppermute(asked, "c", swap)

    side = lax.axis_index("head").astype(i32).reshape(1)
    seg = seg.reshape(PARTS, ROUNDS, W, 1)
    resid = residual.reshape(PARTS, ROUNDS, W, HALF)
    resid_tan = residual_tan.reshape(PARTS, ROUNDS, W, HALF)
    tables = (mod_scale, mod_scale_tan, mod_shift, mod_shift_tan)

    def answer_of(turn, tie_attend, tie_combine):
        with jax.named_scope("attend"):
            part, part_there = attend(asked, asked_there, arrived, tie_attend, turn)
            part_back = lax.ppermute(part_there, "c", swap)
            return combine(part, part_back, side if tie_combine is None else tie_combine)

    def project_of(turn, answer):
        with jax.named_scope("collect"):
            attended = lax.all_to_all(answer, ("z", "y", "x"), 0, 0, tiled=True)
        with jax.named_scope("project"):
            return project(side, attended, out_weight, seg, gate, gate_tan, resid, resid_tan, turn)

    first = answer_of(0, side, None)
    keep0, send0 = project_of(0, first)
    second = answer_of(1, first, send0)
    got0 = lax.ppermute(send0, "head", swap)
    keep1, send1 = project_of(1, second)
    got1 = lax.ppermute(send1, "head", swap)
    with jax.named_scope("norm"):
        outs = norm(side, keep0, got0, seg, tables, (), 0)
        outs = norm(side, keep1, got1, seg, tables, outs, 1)
    return tuple(x.reshape(ROWS, -1) for x in outs)


def solution(mesh):
    fine = Mesh(mesh.devices.reshape(4, 4, 2, 2, 2), ("z", "y", "x", "c", "head"))
    seq = ("z", "y", "x", "c")
    split = P(seq, "head")
    in_specs = (split,) * 6 + (P(seq), P(seq), P("head", None), split, split) + (P(),) * 6
    out_specs = (split, split, P(seq, None), P(seq, None))
    return jax.shard_map(body, mesh=fine, in_specs=in_specs, out_specs=out_specs, check_vma=False)
```

time: 210 us -> 179 us (0.85)
  Pallas kernels: 77 us -> 36.1 us
  local copies, waits for them, and re-layouts: 7.3 us -> 23 us
  other arithmetic: 4.93 us -> 1.65 us
    pallas_call x7 -> x9, Pallas kernels: 77 us -> 36.1 us  [the longest x2 14.7 us: attend(): pl.pallas_call(lambda *refs: attn_kernel(*refs, turn=turn), in_specs=[VME...]
    unnamed x18 -> x48, local copies, waits for them, and re-layouts: 5.14 us -> 22.6 us
    ppermute x4, waiting for transfers between devices: 33.8 us -> 20.2 us  [the longest x1 15.5 us: body(): got1 = lax.ppermute(send1, 'head', swap)]
    all_to_all x1 -> x2, waiting for transfers between devices: 13.2 us -> 23.2 us  [project_of(): attended = lax.all_to_all(answer, ('z', 'y', 'x'), 0, 0, tiled=True)]
    another operation x4 -> x0, other arithmetic: 3.24 us -> none  [the longest x2 1.96 us: body(): jnp.stack([jnp.zeros((PARTS, 256), bf16).at[:, :ROWS].set(clips[None, :])...]
    ppermute x1, waiting for transfers between devices: 0.01 us -> 2.28 us  [body(): asked_there = lax.ppermute(asked, 'c', swap)]
    all_to_all x1 -> x2, starting transfers between devices: 8.61 us -> 7.89 us  [project_of(): attended = lax.all_to_all(answer, ('z', 'y', 'x'), 0, 0, tiled=True)]
  transfers between devices with their start and end apart: 6 -> 7, of which waited for: 3 -> 6; matrix products, arithmetic and copies ran while one was open for 1% -> 0% of each run, Pallas kernels for 15% -> 8%
where the time goes in v2:
time: 179 us; the launch traced here: 178 us
  blocking collectives  60.9 us (34%)
  waiting for transfers between devices  45.7 us (26%)
  Pallas kernels  36.1 us (20%)
  local copies, waits for them, and re-layouts  23 us (13%)
  starting transfers between devices  9.84 us (5%)
    all_to_all x1, blocking collectives, body(): arrived = lax.all_to_all(message, ('z', 'y', 'x'), 0, 0, tiled=True)  60.9 us
    all_to_all x2, waiting for transfers between devices, project_of(): attended = lax.all_to_all(answer, ('z', 'y', 'x'), 0, 0, tiled=True)  23.2 us
    unnamed x48, local copies, waits for them, and re-layouts  22.6 us
    ppermute x1, waiting for transfers between devices, body(): got1 = lax.ppermute(send1, 'head', swap)  15.5 us
    pallas_call x2, Pallas kernels, attend(): pl.pallas_call(lambda *refs: attn_kernel(*refs, turn=turn), in_specs=[VME...  14.7 us
    pallas_call x2, Pallas kernels, project(): pl.pallas_call(project_kernel, grid_spec=pltpu.PrefetchScalarGridSpec(num...  10.5 us
    all_to_all x2, starting transfers between devices, project_of(): attended = lax.all_to_all(answer, ('z', 'y', 'x'), 0, 0, tiled=True)  7.89 us
    pallas_call x2, Pallas kernels, norm(): pl.pallas_call(norm_kernel, grid_spec=pltpu.PrefetchScalarGridSpec(num_sc...  6.62 us
  transfers between devices with their start and end apart: 7, of which 6 were waited for; matrix products, arithmetic and copies ran while one was open for 0% of the time, Pallas kernels for 8%

profile of v2, /device:TPU:0, one launch (start us, length us, event | category | flops | bytes accessed | tf_op | source)
XLA Modules:
  0.0 178.0 jit_solution(8181688589223764424)
XLA Ops:
  0.6 0.7 convert_element_type.8
  1.3 0.1 compare_select_fusion
  1.4 0.7 fusion.1
  2.0 0.1 pad_bitcast_fusion.row_ref
  2.1 0.1 copy.25.seg_ref
  2.2 0.2 fusion
  2.5 0.0 copy-start.10
  2.5 0.9 copy-done.10
  3.4 0.9 copy-done.11
  4.4 0.9 copy-done.12
  5.3 0.9 copy-done.13
  6.3 0.9 copy-done.14
  7.2 0.9 copy-done.15
  8.1 0.7 pack.1
  8.8 60.9 %all_to_all.15.refs_2_ = bf16[32,240,256]{2,1,0:T(8,128)(2,1)S(1)} all-to-all(bf16[32,240,256]{2,1,0:T(8,128)(2,1)S(1)} %pack.1), channel_id=1, replica_groups=mesh['z'=4,'y'=4,'x'=2,'c'=2,'head'=2] {'z','y','x'}, dimensions={0} | all-to-all | bytes 7864320 | tf_op jit(solution)/shard_map/spread/all_to_all | solution.py:378
  69.8 0.1 slice.4.refs_0_
  69.8 0.0 copy-start.2
  69.8 1.9 %copy-done.2 = bf16[32,240,256]{2,1,0:T(8,128)(2,1)} copy-done((bf16[32,240,256]{2,1,0:T(8,128)(2,1)}, bf16[32,240,256]{2,1,0:T(8,128)(2,1)S(1)}, u32[]{:S(2)}) %copy-start.2) | copy-done | bytes 3932184
  71.7 0.0 collective-permute-start
  71.7 2.3 %collective-permute-done.refs_1_ = bf16[32,48,256]{2,1,0:T(8,128)(2,1)S(1)} collective-permute-done((bf16[32,48,256]{2,1,0:T(8,128)(2,1)S(1)}, bf16[32,48,256]{2,1,0:T(8,128)(2,1)S(1)}, u32[]{:S(2)}, u32[]{:S(2)}) %collective-permute-start) | collective-permute-done | bytes 786464 | tf_op jit(solution)/shard_map/spread/ppermute | solution.py:380
  74.0 2.4 %copy-done.3 = bf16[32,240,256]{2,1,0:T(8,128)(2,1)S(1)} copy-done((bf16[32,240,256]{2,1,0:T(8,128)(2,1)S(1)}, bf16[32,240,256]{2,1,0:T(8,128)(2,1)}, u32[]{:S(2)}) %copy-start.3) | copy-done | bytes 3932184
  76.4 7.0 %attend.4 = (bf16[32,48,128]{2,1,0:T(8,128)(2,1)S(1)}, bf16[32,48,128]{2,1,0:T(8,128)(2,1)S(1)}) custom-call(bf16[32,48,256]{2,1,0:T(8,128)(2,1)S(1)} %slice.4.refs_0_, bf16[32,48,256]{2,1,0:T(8,128)(2,1)S(1)} %collective-permute-done.refs_1_, bf16[32,240,256]{2,1,0:T(8,128)(2,1)S(1)} %copy-done.3, s32[1]{0:T(128)} %bitcast.refs_3_.tie_ref.side_ref), custom_call_target="tpu_custom_call" | custom-call | flops 5000000000 | bytes 6291456 | tf_op jit(solution)/shard_map/attend/pallas_call | solution.py:192
  83.4 0.4 collective-permute-start.1
  83.8 1.6 collective-permute-done.1.b_ref
  85.3 1.3 attend.5.refs_3_
  86.7 1.1 copy-done.23
  87.8 7.7 %attend.6 = (bf16[32,48,128]{2,1,0:T(8,128)(2,1)S(1)}, bf16[32,48,128]{2,1,0:T(8,128)(2,1)}) custom-call(bf16[32,48,256]{2,1,0:T(8,128)(2,1)S(1)} %slice.4.refs_0_, bf16[32,48,256]{2,1,0:T(8,128)(2,1)S(1)} %copy-done.23, bf16[32,240,256]{2,1,0:T(8,128)(2,1)S(1)} %copy-done.3, bf16[32,32,128]{2,1,0:T(8,128)(2,1)} %attend.5.refs_3_), custom_call_target="tpu_custom_call" | custom-call | flops 5000000000 | bytes 6291456 | tf_op jit(solution)/shard_map/attend/pallas_call | solution.py:192
  95.5 0.7 copy-done.8
  96.3 0.1 collective-permute-start.2
  96.4 3.9 %all-to-all-start.1 = ((bf16[32,32,128]{2,1,0:T(8,128)(2,1)}), bf16[32,32,128]{2,1,0:T(8,128)(2,1)S(1)}, u32[]{:S(2)}, u32[]{:S(2)}) async-start(bf16[32,32,128]{2,1,0:T(8,128)(2,1)} %attend.5.refs_3_), calls=%async_computation.1 | async-start | bytes 524288 | tf_op jit(solution)/shard_map/collect/all_to_all | solution.py:396
  100.3 0.2 reshape_broadcast_in_dim.4.seg_ref
  100.4 11.6 %all-to-all-done.1.x_ref = bf16[32,32,128]{2,1,0:T(8,128)(2,1)S(1)} async-done(((bf16[32,32,128]{2,1,0:T(8,128)(2,1)}), bf16[32,32,128]{2,1,0:T(8,128)(2,1)S(1)}, u32[]{:S(2)}, u32[]{:S(2)}) %all-to-all-start.1) | async-done | bytes 262176 | tf_op jit(solution)/shard_map/collect/all_to_all | solution.py:396
  112.0 0.0 copy-start
  112.0 4.7 %copy-done = bf16[1280,5120]{1,0:T(8,128)(2,1)S(1)} copy-done((bf16[1280,5120]{1,0:T(8,128)(2,1)S(1)}, bf16[1280,5120]{1,0:T(8,128)(2,1)}, u32[]{:S(2)}) %copy-start) | copy-done | bytes 13107224
  116.8 5.3 %project.2 = (f32[2,48,5120]{2,1,0:T(8,128)S(1)}, bf16[2,48,5120]{2,1,0:T(8,128)(2,1)S(1)}) custom-call(s32[1]{0:T(128)} %bitcast.refs_3_.tie_ref.side_ref, bf16[32,32,128]{2,1,0:T(8,128)(2,1)S(1)} %all-to-all-done.1.x_ref, bf16[1280,5120]{1,0:T(8,128)(2,1)S(1)} %copy-done, f32[3,2,16,1]{3,2,1,0:T(8,128)S(1)} %reshape_broadcast_in_dim.4.seg_ref, ...), custom_call_target="tpu_custom_call" | custom-call | flops 1258291200 | bytes 16777216 | tf_op jit(solution)/shard_map/project/pallas_call | solution.py:277
  122.0 1.3 copy-done.6
  123.4 0.0 collective-permute-done.2.b_ref
  123.4 2.3 %attend.7 = bf16[32,32,128]{2,1,0:T(8,128)(2,1)} custom-call(bf16[32,48,128]{2,1,0:T(8,128)(2,1)S(1)} %copy-done.9, bf16[32,48,128]{2,1,0:T(8,128)(2,1)} %collective-permute-done.2.b_ref, bf16[2,48,5120]{2,1,0:T(8,128)(2,1)S(1)} %get-tuple-element.24.tie_ref), custom_call_target="tpu_custom_call" | custom-call | tf_op jit(solution)/shard_map/attend/pallas_call | solution.py:235
  125.7 4.0 %all-to-all-start.2 = ((bf16[32,32,128]{2,1,0:T(8,128)(2,1)}), bf16[32,32,128]{2,1,0:T(8,128)(2,1)S(1)}, u32[]{:S(2)}, u32[]{:S(2)}) async-start(bf16[32,32,128]{2,1,0:T(8,128)(2,1)} %attend.7), calls=%async_computation.2 | async-start | bytes 524288 | tf_op jit(solution)/shard_map/collect/all_to_all | solution.py:396
  129.7 0.7 collective-permute-start.4
  130.4 11.7 %all-to-all-done.2.x_ref = bf16[32,32,128]{2,1,0:T(8,128)(2,1)S(1)} async-done(((bf16[32,32,128]{2,1,0:T(8,128)(2,1)}), bf16[32,32,128]{2,1,0:T(8,128)(2,1)S(1)}, u32[]{:S(2)}, u32[]{:S(2)}) %all-to-all-start.2) | async-done | bytes 262176 | tf_op jit(solution)/shard_map/collect/all_to_all | solution.py:396
  142.1 4.7 %copy-done.1 = bf16[1280,5120]{1,0:T(8,128)(2,1)S(1)} copy-done((bf16[1280,5120]{1,0:T(8,128)(2,1)S(1)}, bf16[1280,5120]{1,0:T(8,128)(2,1)}, u32[]{:S(2)}) %copy-start.1) | copy-done | bytes 13107224
  146.8 5.3 %project.3 = (f32[2,48,5120]{2,1,0:T(8,128)S(1)}, bf16[2,48,5120]{2,1,0:T(8,128)(2,1)S(1)}) custom-call(s32[1]{0:T(128)} %bitcast.refs_3_.tie_ref.side_ref, bf16[32,32,128]{2,1,0:T(8,128)(2,1)S(1)} %all-to-all-done.2.x_ref, bf16[1280,5120]{1,0:T(8,128)(2,1)S(1)} %copy-done.1, f32[3,2,16,1]{3,2,1,0:T(8,128)S(1)} %reshape_broadcast_in_dim.4.seg_ref, ...), custom_call_target="tpu_custom_call" | custom-call | flops 1258291200 | bytes 16777216 | tf_op jit(solution)/shard_map/project/pallas_call | solution.py:277
  152.1 0.7 collective-permute-start.3
  152.8 3.1 %collective-permute-done.4.got_ref = bf16[2,48,5120]{2,1,0:T(8,128)(2,1)} collective-permute-done((bf16[2,48,5120]{2,1,0:T(8,128)(2,1)S(1)}, bf16[2,48,5120]{2,1,0:T(8,128)(2,1)}, u32[]{:S(2)}, u32[]{:S(2)}) %collective-permute-start.4) | collective-permute-done | bytes 983072 | tf_op jit(solution)/shard_map/ppermute | solution.py:403
  155.9 3.9 %norm.2 = (f32[3,2,16,2560]{3,2,1,0:T(8,128)}, f32[3,2,16,2560]{3,2,1,0:T(8,128)}, bf16[3,2,16,5120]{3,2,1,0:T(8,128)(2,1)}, bf16[3,2,16,5120]{3,2,1,0:T(8,128)(2,1)}) custom-call(s32[1]{0:T(128)} %bitcast.refs_3_.tie_ref.side_ref, f32[2,48,5120]{2,1,0:T(8,128)S(1)} %copy-done.7, bf16[2,48,5120]{2,1,0:T(8,128)(2,1)} %collective-permute-done.4.got_ref, ...), custom_call_target="tpu_custom_call" | custom-call | tf_op jit(solution)/shard_map/norm/pallas_call | solution.py:337
  159.8 15.5 %collective-permute-done.3.got_ref = bf16[2,48,5120]{2,1,0:T(8,128)(2,1)S(1)} collective-permute-done((bf16[2,48,5120]{2,1,0:T(8,128)(2,1)S(1)}, bf16[2,48,5120]{2,1,0:T(8,128)(2,1)S(1)}, u32[]{:S(2)}, u32[]{:S(2)}) %collective-permute-start.3) | collective-permute-done | bytes 983072 | tf_op jit(solution)/shard_map/ppermute | solution.py:405
  175.3 2.7 %norm.3 = (f32[3,2,16,2560]{3,2,1,0:T(8,128)}, f32[3,2,16,2560]{3,2,1,0:T(8,128)}, bf16[3,2,16,5120]{3,2,1,0:T(8,128)(2,1)}, bf16[3,2,16,5120]{3,2,1,0:T(8,128)(2,1)}) custom-call(s32[1]{0:T(128)} %bitcast.refs_3_.tie_ref.side_ref, ...), custom_call_target="tpu_custom_call", output_to_operand_aliasing={{0}: (8, {}), {1}: (9, {}), {2}: (10, {}), {3}: (11, {})} | custom-call | tf_op jit(solution)/shard_map/norm/pallas_call | solution.py:337
  (33 shorter events, 0.1 us)
Async XLA Ops:
  2.5 0.9 copy-start.10
  3.4 0.9 copy-start.11
  4.4 0.9 copy-start.12
  5.3 0.9 copy-start.13
  6.3 0.9 copy-start.14
  7.2 0.9 copy-start.15
  69.8 1.9 %copy-start.2 = (bf16[32,240,256]{2,1,0:T(8,128)(2,1)}, bf16[32,240,256]{2,1,0:T(8,128)(2,1)S(1)}, u32[]{:S(2)}) copy-start(bf16[32,240,256]{2,1,0:T(8,128)(2,1)S(1)} %all_to_all.15.refs_2_) | copy-start | bytes 11796484
  71.7 2.3 %collective-permute-start = (bf16[32,48,256]{2,1,0:T(8,128)(2,1)S(1)}, bf16[32,48,256]{2,1,0:T(8,128)(2,1)S(1)}, u32[]{:S(2)}, u32[]{:S(2)}) collective-permute-start(bf16[32,48,256]{2,1,0:T(8,128)(2,1)S(1)} %slice.4.refs_0_), channel_id=1, source_target_pairs={{0,2},{2,0},{1,3},{3,1},{4,6},{6,4},{5,7},{7,5},{8,10},{10,8},{9,1... | collective-permute-start | bytes 2359304 | tf_op jit(solution)/shard_map/spread/ppermute | solution.py:380
  74.0 9.4 %copy-start.22 = (bf16[32,48,256]{2,1,0:T(8,128)(2,1)}, bf16[32,48,256]{2,1,0:T(8,128)(2,1)S(1)}, u32[]{:S(2)}) copy-start(bf16[32,48,256]{2,1,0:T(8,128)(2,1)S(1)} %collective-permute-done.refs_1_) | copy-start | bytes 2359300
  74.0 2.4 %copy-start.3 = (bf16[32,240,256]{2,1,0:T(8,128)(2,1)S(1)}, bf16[32,240,256]{2,1,0:T(8,128)(2,1)}, u32[]{:S(2)}) copy-start(bf16[32,240,256]{2,1,0:T(8,128)(2,1)} %copy-done.2) | copy-start | bytes 11796484
  83.4 2.0 %collective-permute-start.1 = (bf16[32,48,128]{2,1,0:T(8,128)(2,1)S(1)}, bf16[32,48,128]{2,1,0:T(8,128)(2,1)S(1)}, u32[]{:S(2)}, u32[]{:S(2)}) collective-permute-start(bf16[32,48,128]{2,1,0:T(8,128)(2,1)S(1)} %get-tuple-element.21), channel_id=1, source_target_pairs={{0,2},{2,0},{1,3},{3,1},{4,6},{6,4},{5,7},{7,5},{8,10},{10,8},{9,1... | collective-permute-start | bytes 1179656 | tf_op jit(solution)/shard_map/attend/ppermute | solution.py:391
  86.7 1.1 copy-start.23
  87.8 24.2 %copy-start.4 = (f32[96,2560]{1,0:T(8,128)S(1)}, f32[96,2560]{1,0:T(8,128)}, u32[]{:S(2)}) copy-start(f32[96,2560]{1,0:T(8,128)} %param.26) | copy-start | bytes 2949124
  87.8 24.2 %copy-start.5 = (f32[96,2560]{1,0:T(8,128)S(1)}, f32[96,2560]{1,0:T(8,128)}, u32[]{:S(2)}) copy-start(f32[96,2560]{1,0:T(8,128)} %param.27) | copy-start | bytes 2949124
  87.8 24.2 %copy-start.16 = (f32[2,5120]{1,0:T(2,128)S(1)}, f32[2,5120]{1,0:T(2,128)}, u32[]{:S(2)}) copy-start(f32[2,5120]{1,0:T(2,128)} %gate_ref.3) | copy-start | bytes 122884
  87.8 24.2 %copy-start.17 = (f32[2,5120]{1,0:T(2,128)S(1)}, f32[2,5120]{1,0:T(2,128)}, u32[]{:S(2)}) copy-start(f32[2,5120]{1,0:T(2,128)} %gate_tan_ref.3) | copy-start | bytes 122884
  95.5 0.7 copy-start.8
  96.3 27.1 %collective-permute-start.2 = (bf16[32,48,128]{2,1,0:T(8,128)(2,1)}, bf16[32,48,128]{2,1,0:T(8,128)(2,1)}, u32[]{:S(2)}, u32[]{:S(2)}) collective-permute-start(bf16[32,48,128]{2,1,0:T(8,128)(2,1)} %get-tuple-element.23), channel_id=1, source_target_pairs={{0,2},{2,0},{1,3},{3,1},{4,6},{6,4},{5,7},{7,5},{8,10},{10,8},{9,1... | collective-permute-start | bytes 1179656 | tf_op jit(solution)/shard_map/attend/ppermute | solution.py:391
  96.4 15.6 %all-to-all-start.1 = ((bf16[32,32,128]{2,1,0:T(8,128)(2,1)}), bf16[32,32,128]{2,1,0:T(8,128)(2,1)S(1)}, u32[]{:S(2)}, u32[]{:S(2)}) async-start(bf16[32,32,128]{2,1,0:T(8,128)(2,1)} %attend.5.refs_3_), calls=%async_computation.1 | async-start | bytes 524288 | tf_op jit(solution)/shard_map/collect/all_to_all | solution.py:396
  112.0 4.7 %copy-start = (bf16[1280,5120]{1,0:T(8,128)(2,1)S(1)}, bf16[1280,5120]{1,0:T(8,128)(2,1)}, u32[]{:S(2)}) copy-start(bf16[1280,5120]{1,0:T(8,128)(2,1)} %w_ref.3) | copy-start | bytes 39321604
  116.8 6.6 %copy-start.9 = (bf16[32,48,128]{2,1,0:T(8,128)(2,1)S(1)}, bf16[32,48,128]{2,1,0:T(8,128)(2,1)}, u32[]{:S(2)}) copy-start(bf16[32,48,128]{2,1,0:T(8,128)(2,1)} %copy-done.8) | copy-start | bytes 1179652
  122.0 1.3 copy-start.6
  125.7 30.2 %copy-start.18 = (f32[2,5120]{1,0:T(2,128)S(1)}, f32[2,5120]{1,0:T(2,128)}, u32[]{:S(2)}) copy-start(f32[2,5120]{1,0:T(2,128)} %scale_ref.3) | copy-start | bytes 122884
  125.7 30.2 %copy-start.19 = (f32[2,5120]{1,0:T(2,128)S(1)}, f32[2,5120]{1,0:T(2,128)}, u32[]{:S(2)}) copy-start(f32[2,5120]{1,0:T(2,128)} %scale_tan_ref.3) | copy-start | bytes 122884
  125.7 30.2 %copy-start.20 = (f32[2,5120]{1,0:T(2,128)S(1)}, f32[2,5120]{1,0:T(2,128)}, u32[]{:S(2)}) copy-start(f32[2,5120]{1,0:T(2,128)} %shift_ref.3) | copy-start | bytes 122884
  125.7 30.2 %copy-start.21 = (f32[2,5120]{1,0:T(2,128)S(1)}, f32[2,5120]{1,0:T(2,128)}, u32[]{:S(2)}) copy-start(f32[2,5120]{1,0:T(2,128)} %shift_tan_ref.3) | copy-start | bytes 122884
  125.7 16.4 %all-to-all-start.2 = ((bf16[32,32,128]{2,1,0:T(8,128)(2,1)}), bf16[32,32,128]{2,1,0:T(8,128)(2,1)S(1)}, u32[]{:S(2)}, u32[]{:S(2)}) async-start(bf16[32,32,128]{2,1,0:T(8,128)(2,1)} %attend.7), calls=%async_computation.2 | async-start | bytes 524288 | tf_op jit(solution)/shard_map/collect/all_to_all | solution.py:396
  129.7 26.2 %collective-permute-start.4 = (bf16[2,48,5120]{2,1,0:T(8,128)(2,1)S(1)}, bf16[2,48,5120]{2,1,0:T(8,128)(2,1)}, u32[]{:S(2)}, u32[]{:S(2)}) collective-permute-start(bf16[2,48,5120]{2,1,0:T(8,128)(2,1)S(1)} %get-tuple-element.24.tie_ref), channel_id=1, source_target_pairs={{0,1},{1,0},{2,3},{3,2},{4,5},{5,4},{6,7},{7,6},{8,9},{9,8},{10,11... | collective-permute-start | bytes 2949128 | tf_op jit(solution)/shard_map/ppermute | solution.py:403
  142.1 4.7 %copy-start.1 = (bf16[1280,5120]{1,0:T(8,128)(2,1)S(1)}, bf16[1280,5120]{1,0:T(8,128)(2,1)}, u32[]{:S(2)}) copy-start(bf16[1280,5120]{1,0:T(8,128)(2,1)} %w_ref.3) | copy-start | bytes 39321604
  146.8 9.1 %copy-start.7 = (f32[2,48,5120]{2,1,0:T(8,128)S(1)}, f32[2,48,5120]{2,1,0:T(8,128)}, u32[]{:S(2)}) copy-start(f32[2,48,5120]{2,1,0:T(8,128)} %copy-done.6) | copy-start | bytes 5898244
  152.1 23.2 %collective-permute-start.3 = (bf16[2,48,5120]{2,1,0:T(8,128)(2,1)S(1)}, bf16[2,48,5120]{2,1,0:T(8,128)(2,1)S(1)}, u32[]{:S(2)}, u32[]{:S(2)}) collective-permute-start(bf16[2,48,5120]{2,1,0:T(8,128)(2,1)S(1)} %get-tuple-element.26), channel_id=1, source_target_pairs={{0,1},{1,0},{2,3},{3,2},{4,5},{5,4},{6,7},{7,6},{8,9},{9,8},{10,11... | collective-permute-start | bytes 2949128 | tf_op jit(solution)/shard_map/ppermute | solution.py:405

commit v3 on v2

v3 whole, which is shorter than its diff:
```python
import math

import jax
import jax.numpy as jnp
from jax import lax
from jax.experimental import pallas as pl
from jax.experimental.pallas import tpu as pltpu
from jax.sharding import Mesh, PartitionSpec as P

D = 5120
HD = 128
NH = 10
ROWS = 96
THIRD = 32
CHIPS = 32
PARTS = 3
SPAN = 5
MSG = 240
HALF = D // 2

W = THIRD
SB = 8
KR = SB * ROWS
LONG, SHORT = (21, 3), (13, 2)
RMAX = LONG[0] * 2 * THIRD

neg_fill = -1e30
norm_eps = 1e-06
rope_base = 10000.0
ln2 = math.log(2.0)
exp_scale = math.log2(math.e) / math.sqrt(HD)

f32 = jnp.float32
bf16 = jnp.bfloat16
i32 = jnp.int32
VMEM = pl.BlockSpec(memory_space=pltpu.VMEM)
ANY = pl.BlockSpec(memory_space=pl.ANY)
NT = (((1,), (1,)), ((), ()))


def worker(h, t):
    return h // SPAN * (CHIPS // 2) + h % SPAN * PARTS + t


def params(mib=56):
    return pltpu.CompilerParams(vmem_limit_bytes=mib * 2**20)


def pack_kernel(q_ref, k_ref, v_ref, qt_ref, kt_ref, vt_ref, cos_ref, sin_ref, seg_ref, row_ref, out_ref):
    cos = cos_ref[...]
    sin = sin_ref[...]
    lane = lax.broadcasted_iota(i32, (ROWS, HD), 1)
    clips = jnp.where(lane == 0, seg_ref[...], row_ref[...]).astype(bf16)

    def rot(ref, cols, factor):
        x = ref[:, cols].astype(f32)
        y = x * cos + jnp.roll(x, HD // 2, axis=1) * sin
        return (y if factor is None else y * factor).astype(bf16)

    for h in range(SPAN):
        cols = slice(h * HD, (h + 1) * HD)
        k, kt = rot(k_ref, cols, None), rot(kt_ref, cols, None)
        q, qt = rot(q_ref, cols, exp_scale), rot(qt_ref, cols, exp_scale)
        v, vt = v_ref[:, cols], vt_ref[:, cols]
        for t in range(PARTS):
            s = worker(h, t)
            at = t * THIRD
            out_ref[s, 0:96, 0:128] = k
            out_ref[s, 0:96, 128:256] = kt
            out_ref[s, 96:192, 0:128] = v
            out_ref[s, 96:192, 128:256] = vt
            out_ref[s, 192:224, 0:128] = qt[at : at + 32]
            out_ref[s, 192:224, 128:256] = q[at : at + 32]
            out_ref[s, 224:240, 0:128] = clips[at : at + 16]
            out_ref[s, 224:240, 128:256] = clips[at + 16 : at + 32]
    out_ref[SPAN * PARTS] = jnp.zeros((MSG, 256), bf16)


def bits(tiles):
    rows = jnp.concatenate([t.astype(f32)[0:1, :] for t in tiles], axis=0)
    lane = lax.broadcasted_iota(i32, (CHIPS, HD), 1)
    at = lax.broadcasted_iota(i32, (CHIPS, 1), 0)
    power = jnp.left_shift(jnp.ones((CHIPS, 1), i32), at & 15).astype(f32)
    has0 = 1.0 - jnp.min(jnp.where(lane < 32, 1.0, rows), axis=1, keepdims=True)
    has1 = jnp.max(jnp.where(lane < 32, 0.0, rows), axis=1, keepdims=True)

    def scalar(has):
        low = jnp.sum(jnp.where(at < 16, has * power, 0.0)).astype(i32)
        high = jnp.sum(jnp.where(at < 16, 0.0, has * power)).astype(i32)
        return low | (high << 16)

    return scalar(has0), scalar(has1)


def attn_kernel(qa_ref, qb_ref, kv_ref, oa_ref, ob_ref, s_ref, acc_ref, acct_ref, l_ref, pen_ref, keys_ref, kind_ref, chips_ref, cut_ref):
    own = bits([kv_ref[j, 224:240, 0:128] for j in range(CHIPS)])
    sib = bits([qb_ref[j, 32:48, 0:128] for j in range(CHIPS)])
    cut_ref[0] = i32(0)
    cut_ref[1] = i32(0)

    def sort(j, carry):
        cuts, counts = carry[0], list(carry[1:])
        has = [(own[c] >> j) & 1 for c in range(2)]
        both = has[0] & has[1]
        cut_ref[jnp.where(both == 1, jnp.minimum(cuts, 1), 2)] = j
        for c in range(2):
            at = jnp.where(has[c] == 1, counts[c], 31 - (j - counts[c]))
            keys_ref[c, at] = j
            kind_ref[c, at] = jnp.where(both == 1, 2 + 2 * c + jnp.minimum(cuts, 1), 1 - has[c])
            counts[c] = counts[c] + has[c]
            any_has = ((own[c] | sib[c]) >> j) & 1
            n = counts[2 + c]
            chips_ref[c, jnp.where(any_has == 1, n, 31 - (j - n))] = j
            counts[2 + c] = n + any_has
        return (cuts + both, *counts)

    zero = i32(0)
    counted = lax.fori_loop(0, CHIPS, sort, (zero,) * 5)
    long_clip = jnp.where(counted[4] > 16, 1, 0)

    lane = lax.broadcasted_iota(i32, (ROWS, HD), 1)
    eye = lane == lax.broadcasted_iota(i32, (ROWS, HD), 0) + 32
    pen_ref[0] = jnp.zeros((ROWS, HD), bf16)
    pen_ref[1] = jnp.where(lane == 0, neg_fill, 0.0).astype(bf16)
    for p in range(2):
        row = kv_ref[cut_ref[p], 224:240, 0:128].astype(f32)[0:1, :]
        col = jnp.sum(jnp.where(eye, row, 0.0), axis=1, keepdims=True)
        pen_ref[2 + p] = jnp.where(lane == 0, col * neg_fill, 0.0).astype(bf16)
        pen_ref[4 + p] = jnp.where(lane == 0, (1.0 - col) * neg_fill, 0.0).astype(bf16)

    for (chips, blocks), clip in ((LONG, long_clip), (SHORT, 1 - long_clip)):
        R = chips * 2 * THIRD
        listed = [chips_ref[clip, i] for i in range(chips)]
        qq = jnp.concatenate([ref[j, 0:THIRD, :] for j in listed for ref in (qa_ref, qb_ref)], axis=0)
        one = jnp.where(lax.broadcasted_iota(i32, (R, HD), 1) == 0, 1.0, 0.0).astype(bf16)
        q = jnp.concatenate([qq[:, 128:256], one], axis=1)
        m = jnp.full((R, HD), neg_fill, f32)
        for b in range(blocks):
            pairs = [(keys_ref[clip, b * SB + u], kind_ref[clip, b * SB + u]) for u in range(SB)]
            k = jnp.concatenate([jnp.concatenate([kv_ref[j, 0:96, 0:128], pen_ref[n]], axis=1) for j, n in pairs], axis=0)
            s = lax.dot_general(q, k, NT, preferred_element_type=f32)
            s_ref[b, 0:R] = s
            for j in range(KR // HD):
                m = jnp.maximum(m, s[:, j * HD : (j + 1) * HD])
        top = jnp.max(m, axis=1, keepdims=True)
        for b in range(blocks):
            js = [keys_ref[clip, b * SB + u] for u in range(SB)]
            k = jnp.concatenate([kv_ref[j, 0:96, :] for j in js], axis=0)
            v = jnp.concatenate([kv_ref[j, 96:192, :] for j in js], axis=0)
            v1 = jnp.concatenate([v[:, 0:128], jnp.ones((KR, HD), bf16)], axis=1)
            st = lax.dot_general(qq, k, NT, preferred_element_type=f32)
            p = jnp.exp2(s_ref[b, 0:R] - top)
            pt = (p * st).astype(bf16)
            l = p[:, 0:HD]
            for j in range(1, KR // HD):
                l = l + p[:, j * HD : (j + 1) * HD]
            acc = jnp.dot(p.astype(bf16), v, preferred_element_type=f32)
            acct = jnp.dot(pt, v1, preferred_element_type=f32)
            if b == 0:
                l_ref[0:R], acc_ref[0:R], acct_ref[0:R] = l, acc, acct
            else:
                l_ref[0:R] += l
                acc_ref[0:R] += acc
                acct_ref[0:R] += acct
        total = jnp.sum(l_ref[0:R], axis=1, keepdims=True)
        inv = 1.0 / total
        inv_tan = inv * ln2
        drift = acct_ref[0:R, 128:256] * inv_tan
        o = acc_ref[0:R, 0:128] * inv
        t = acct_ref[0:R, 0:128] * inv_tan + acc_ref[0:R, 128:256] * inv - drift * o
        lse = jnp.broadcast_to(top + jnp.log2(total), (R, HD))
        where = lax.broadcasted_iota(i32, (R, HD), 1)
        pieces = jnp.zeros((R, HD), f32)
        for first, x in ((0, lse), (3, drift)):
            for i in range(3):
                piece = x.astype(bf16).astype(f32)
                pieces = jnp.where(where == first + i, piece, pieces)
                x = x - piece
        whole = [x.astype(bf16) for x in (o, t, pieces)]
        wanted = clip.astype(f32)
        for i, j in enumerate(listed):
            for core, (q_ref, out_ref) in enumerate(((qa_ref, oa_ref), (qb_ref, ob_ref))):
                at = (2 * i + core) * W
                tags = q_ref[j, 32:48, :].astype(f32)
                tag = jnp.concatenate([tags[:, 0:1], tags[:, HD : HD + 1]], axis=0)
                hit = jnp.broadcast_to(tag, (W, HD)) == wanted
                for n, x in enumerate(whole):
                    old = out_ref[j, n * W : (n + 1) * W, :].astype(f32)
                    out_ref[j, n * W : (n + 1) * W, :] = jnp.where(hit, x[at : at + W].astype(f32), old).astype(bf16)


def attend(asked, asked_there, arrived):
    out = jax.ShapeDtypeStruct((CHIPS, 3 * W, HD), bf16)
    return pl.pallas_call(
        attn_kernel,
        in_specs=[VMEM] * 3,
        out_specs=[VMEM] * 2,
        out_shape=[out] * 2,
        scratch_shapes=[
            pltpu.VMEM((LONG[1], RMAX, KR), f32),
            pltpu.VMEM((RMAX, 256), f32),
            pltpu.VMEM((RMAX, 256), f32),
            pltpu.VMEM((RMAX, HD), f32),
            pltpu.VMEM((6, ROWS, HD), bf16),
            pltpu.SMEM((2, CHIPS), i32),
            pltpu.SMEM((2, CHIPS), i32),
            pltpu.SMEM((2, CHIPS), i32),
            pltpu.SMEM((3,), i32),
        ],
        compiler_params=params(40),
        cost_estimate=pl.CostEstimate(flops=5 * 10**9, bytes_accessed=6 * 2**20, transcendentals=2 * 10**6),
    )(asked, asked_there, arrived)


def combine_kernel(a_ref, b_ref, out_ref):
    R = CHIPS * W

    def read(ref):
        o, t, s = [ref[:, n * W : (n + 1) * W, :].astype(f32).reshape(R, HD) for n in range(3)]
        lse = s[:, 0:1] + s[:, 1:2] + s[:, 2:3]
        drift = s[:, 3:4] + s[:, 4:5] + s[:, 5:6]
        return o, t, lse, drift

    oa, ta, la, da = read(a_ref)
    ob, tb, lb, db = read(b_ref)
    top = jnp.maximum(la, lb)
    wa, wb = jnp.exp2(la - top), jnp.exp2(lb - top)
    inv = 1.0 / (wa + wb)
    wa, wb = wa * inv, wb * inv
    gap = wa * wb * (da - db)
    out_ref[:, 0:W, :] = (wa * oa + wb * ob).astype(bf16).reshape(CHIPS, W, HD)
    out_ref[:, W : 2 * W, :] = (wa * ta + wb * tb + gap * (oa - ob)).astype(bf16).reshape(CHIPS, W, HD)


def combine(a, b):
    return pl.pallas_call(
        combine_kernel,
        in_specs=[VMEM, VMEM],
        out_specs=VMEM,
        out_shape=jax.ShapeDtypeStruct((CHIPS, 2 * W, HD), bf16),
        compiler_params=params(16),
    )(a, b)


CT = 512
STEPS = HALF // CT


def project_kernel(side_ref, x_ref, w_ref, seg_ref, gate_ref, gate_tan_ref, *refs, own):
    if own:
        resid_ref, resid_tan_ref, keep_ref, send_ref, lhs_ref, held_ref, sem = refs
    else:
        keep_ref, send_ref, lhs_ref, held_ref, sem = refs
    start = side_ref[0] * HALF
    copies = []
    for j in range(STEPS):
        cols = pl.ds(pl.multiple_of(start + j * CT, CT), CT)
        copies.append(pltpu.make_async_copy(w_ref.at[:, cols], held_ref.at[j], sem.at[j]))
        copies[j].start()
    for h in range(NH):
        for t in range(PARTS):
            s = worker(h, t)
            lhs_ref[t * W : (t + 1) * W, h * HD : (h + 1) * HD] = x_ref[s, 0:W, :]
            lhs_ref[ROWS + t * W : ROWS + (t + 1) * W, h * HD : (h + 1) * HD] = x_ref[s, W : 2 * W, :]
    one = seg_ref[...] == 1.0
    for j in range(STEPS):
        copies[j].wait()
        out = jnp.dot(lhs_ref[...], held_ref[j], preferred_element_type=f32)
        cols = pl.ds(pl.multiple_of(start + j * CT, CT), CT)
        here = slice(j * CT, (j + 1) * CT)
        gate = jnp.where(one, gate_ref[1:2, cols], gate_ref[0:1, cols])
        gate_tan = jnp.where(one, gate_tan_ref[1:2, cols], gate_tan_ref[0:1, cols])
        a = gate * out[0:ROWS]
        b = gate_tan * out[0:ROWS] + gate * out[ROWS : 2 * ROWS]
        if own:
            a = a + resid_ref[:, here]
            b = b + resid_tan_ref[:, here]
        keep_ref[0, :, here] = a
        keep_ref[1, :, here] = b
        send_ref[0, :, here] = a.astype(bf16)
        send_ref[1, :, here] = b.astype(bf16)


def project(side, x, w, seg, gate, gate_tan, resid):
    own = len(resid) > 0
    return pl.pallas_call(
        lambda *refs: project_kernel(*refs, own=own),
        in_specs=[pl.BlockSpec(memory_space=pltpu.SMEM), VMEM, ANY] + [VMEM] * (3 + len(resid)),
        out_specs=[VMEM] * 2,
        out_shape=[
            jax.ShapeDtypeStruct((2, ROWS, HALF), f32),
            jax.ShapeDtypeStruct((2, ROWS, HALF), bf16),
        ],
        scratch_shapes=[
            pltpu.VMEM((2 * ROWS, NH * HD), bf16),
            pltpu.VMEM((STEPS, NH * HD, CT), bf16),
            pltpu.SemaphoreType.DMA((STEPS,)),
        ],
        compiler_params=params(52),
        cost_estimate=pl.CostEstimate(flops=2 * 2 * ROWS * NH * HD * HALF, bytes_accessed=10 * 2**20, transcendentals=0),
    )(side, x, w, seg, gate, gate_tan, *resid)


def sums(a, b):
    parts = [jnp.sum(x, axis=1, keepdims=True) for x in (a, a * a, b, a * b)]
    lane = lax.broadcasted_iota(i32, (a.shape[0], HD), 1)
    out = jnp.zeros((a.shape[0], HD), f32)
    for i, x in enumerate(parts):
        out = jnp.where(lane == i, x, out)
    return out


def settle_kernel(keep_ref, got_ref, resid_ref, resid_tan_ref, sums_ref):
    a = keep_ref[0] + got_ref[0].astype(f32)
    b = keep_ref[1] + got_ref[1].astype(f32)
    resid_ref[...] = a
    resid_tan_ref[...] = b
    sums_ref[...] = sums(a, b)


FT = 32


def settle(keep, got):
    pair = pl.BlockSpec((2, FT, HALF), lambda j: (0, j, 0))
    half = pl.BlockSpec((FT, HALF), lambda j: (j, 0))
    return pl.pallas_call(
        settle_kernel,
        grid=(ROWS // FT,),
        in_specs=[pair, pair],
        out_specs=[half, half, pl.BlockSpec((FT, HD), lambda j: (j, 0))],
        out_shape=[
            jax.ShapeDtypeStruct((ROWS, HALF), f32),
            jax.ShapeDtypeStruct((ROWS, HALF), f32),
            jax.ShapeDtypeStruct((ROWS, HD), f32),
        ],
        compiler_params=params(24),
    )(keep, got)


def norm_kernel(side_ref, a_ref, b_ref, sums_ref, keep_ref, got_ref, seg_ref, scale_ref, scale_tan_ref, shift_ref, shift_tan_ref, ffn_ref, ffn_tan_ref):
    other = keep_ref[0] + got_ref[0].astype(f32)
    other_tan = keep_ref[1] + got_ref[1].astype(f32)
    total = (sums_ref[...] + sums(other, other_tan)) / D
    mean, mean_tan = total[:, 0:1], total[:, 2:3]
    rstd = lax.rsqrt(total[:, 1:2] - mean * mean + norm_eps)
    cov = total[:, 3:4] - mean * mean_tan
    slope = rstd * rstd * rstd * cov
    one = seg_ref[...] == 1.0
    for side, a, b in ((1 - side_ref[0], other, other_tan), (side_ref[0], a_ref[...], b_ref[...])):
        cols = pl.ds(pl.multiple_of(side * HALF, HALF), HALF)

        def pick(ref):
            return jnp.where(one, ref[1:2, cols], ref[0:1, cols])

        centered = a - mean
        normed = centered * rstd
        normed_tan = (b - mean_tan) * rstd - centered * slope
        scale = 1.0 + pick(scale_ref)
        ffn_ref[:, cols] = (normed * scale + pick(shift_ref)).astype(bf16)
        ffn_tan_ref[:, cols] = (normed_tan * scale + normed * pick(scale_tan_ref) + pick(shift_tan_ref)).astype(bf16)


def norm(side, a, b, moments, keep, got, seg, tables):
    pair = pl.BlockSpec((2, FT, HALF), lambda j: (0, j, 0))
    half = pl.BlockSpec((FT, HALF), lambda j: (j, 0))
    full = pl.BlockSpec((FT, D), lambda j: (j, 0))
    return pl.pallas_call(
        norm_kernel,
        grid=(ROWS // FT,),
        in_specs=[pl.BlockSpec(memory_space=pltpu.SMEM), half, half, pl.BlockSpec((FT, HD), lambda j: (j, 0)), pair, pair, pl.BlockSpec((FT, 1), lambda j: (j, 0))]
        + [pl.BlockSpec((2, D), lambda j: (0, 0))] * 4,
        out_specs=[full, full],
        out_shape=[
            jax.ShapeDtypeStruct((ROWS, D), bf16),
            jax.ShapeDtypeStruct((ROWS, D), bf16),
        ],
        compiler_params=params(24),
    )(side, a, b, moments, keep, got, seg, *tables)


def body(
    queries, keys, values, queries_tan, keys_tan, values_tan, segments, positions, out_weight,
    residual, residual_tan, gate, gate_tan, mod_scale, mod_scale_tan, mod_shift, mod_shift_tan,
):
    frequency = rope_base ** (-jnp.arange(HD // 2, dtype=f32) / (HD // 2))
    angles = positions.astype(f32)[:, None] * jnp.concatenate([frequency, frequency])[None, :]
    sign = jnp.where(jnp.arange(HD) < HD // 2, -1.0, 1.0).astype(f32)
    cosine, sine = jnp.cos(angles), jnp.sin(angles) * sign[None, :]
    clips = segments.astype(f32)
    seg = clips[:, None]
    row = jnp.pad(clips, (HD - ROWS, 0))[None, :]
    swap = [(0, 1), (1, 0)]

    with jax.named_scope("pack"):
        message = pl.pallas_call(
            pack_kernel,
            grid=(NH // SPAN,),
            in_specs=[pl.BlockSpec((ROWS, SPAN * HD), lambda j: (0, j))] * 6
            + [pl.BlockSpec((ROWS, HD), lambda j: (0, 0))] * 2
            + [pl.BlockSpec((ROWS, 1), lambda j: (0, 0)), pl.BlockSpec((1, HD), lambda j: (0, 0))],
            out_specs=pl.BlockSpec((CHIPS // 2, MSG, 256), lambda j: (j, 0, 0)),
            out_shape=jax.ShapeDtypeStruct((CHIPS, MSG, 256), bf16),
            compiler_params=params(),
        )(queries, keys, values, queries_tan, keys_tan, values_tan, cosine, sine, seg, row)
    with jax.named_scope("spread"):
        arrived = lax.all_to_all(message, ("z", "y", "x"), 0, 0, tiled=True)
        asked = lax.slice_in_dim(arrived, 192, MSG, axis=1)
        asked_there = lax.ppermute(asked, "c", swap)

    side = lax.axis_index("head").astype(i32).reshape(1)
    with jax.named_scope("attend"):
        part, there = attend(asked, asked_there, arrived)
        back = lax.ppermute(there, "c", swap)
        answer = combine(part, back)
    with jax.named_scope("collect"):
        attended = lax.all_to_all(answer, ("z", "y", "x"), 0, 0, tiled=True)
    with jax.named_scope("project"):
        keep_other, send_other = project(1 - side, attended, out_weight, seg, gate, gate_tan, ())
        got_mine = lax.ppermute(send_other, "head", swap)
        keep_mine, send_mine = project(side, attended, out_weight, seg, gate, gate_tan, (residual, residual_tan))
        got_other = lax.ppermute(send_mine, "head", swap)
    with jax.named_scope("norm"):
        resid, resid_tan, moments = settle(keep_mine, got_mine)
        tables = (mod_scale, mod_scale_tan, mod_shift, mod_shift_tan)
        ffn, ffn_tan = norm(side, resid, resid_tan, moments, keep_other, got_other, seg, tables)
    return resid, resid_tan, ffn, ffn_tan


def solution(mesh):
    fine = Mesh(mesh.devices.reshape(4, 4, 2, 2, 2), ("z", "y", "x", "c", "head"))
    seq = ("z", "y", "x", "c")
    split = P(seq, "head")
    in_specs = (split,) * 6 + (P(seq), P(seq), P("head", None), split, split) + (P(),) * 6
    out_specs = (split, split, P(seq, None), P(seq, None))
    return jax.shard_map(body, mesh=fine, in_specs=in_specs, out_specs=out_specs, check_vma=False)
```

time: 179 us -> 163 us (0.911)
  local copies, waits for them, and re-layouts: 23 us -> 5.35 us
  waiting for transfers between devices: 45.7 us -> 50.5 us
  starting transfers between devices: 9.84 us -> 6.56 us
    unnamed x48 -> x22, local copies, waits for them, and re-layouts: 22.6 us -> 3.99 us
    ppermute x4 -> x3, waiting for transfers between devices: 20.2 us -> 34 us  [the longest x1 16.3 us: body(): got_mine = lax.ppermute(send_other, 'head', swap)]
    all_to_all x2 -> x1, waiting for transfers between devices: 23.2 us -> 14.3 us  [body(): attended = lax.all_to_all(answer, ('z', 'y', 'x'), 0, 0, tiled=True)]
    all_to_all x2 -> x1, starting transfers between devices: 7.89 us -> 3.89 us  [body(): attended = lax.all_to_all(answer, ('z', 'y', 'x'), 0, 0, tiled=True)]
    pallas_call x9 -> x7, Pallas kernels: 36.1 us -> 35.9 us  [the longest x1 12.8 us: attend(): pl.pallas_call(attn_kernel, in_specs=[VMEM] * 3, out_specs=[VMEM] * 2, ou...]
  transfers between devices with their start and end apart: 7 -> 5, of which waited for: 6 -> 5; matrix products, arithmetic and copies ran while one was open for 0% -> 0% of each run, Pallas kernels for 8% -> 5%
where the time goes in v3:
time: 163 us
  blocking collectives  61.1 us (37%)
  waiting for transfers between devices  50.5 us (31%)
  Pallas kernels  35.9 us (22%)
  starting transfers between devices  6.56 us (4%)
  local copies, waits for them, and re-layouts  5.35 us (3%)
  other arithmetic  2.3 us (1%)
    all_to_all x1, blocking collectives, body(): arrived = lax.all_to_all(message, ('z', 'y', 'x'), 0, 0, tiled=True)  61.1 us
    ppermute x1, waiting for transfers between devices, body(): got_mine = lax.ppermute(send_other, 'head', swap)  16.3 us
    ppermute x1, waiting for transfers between devices, body(): got_other = lax.ppermute(send_mine, 'head', swap)  15.6 us
    all_to_all x1, waiting for transfers between devices, body(): attended = lax.all_to_all(answer, ('z', 'y', 'x'), 0, 0, tiled=True)  14.3 us
    pallas_call x1, Pallas kernels, attend(): pl.pallas_call(attn_kernel, in_specs=[VMEM] * 3, out_specs=[VMEM] * 2, ou...  12.8 us
    pallas_call x2, Pallas kernels, project(): pl.pallas_call(lambda *refs: project_kernel(*refs, own=own), in_specs=[pl...  11.1 us
    pallas_call x1, Pallas kernels, norm(): pl.pallas_call(norm_kernel, grid=(ROWS // FT,), in_specs=[pl.BlockSpec(me...  4.73 us
    unnamed x22, local copies, waits for them, and re-layouts  3.99 us
  transfers between devices with their start and end apart: 5, of which 5 were waited for; matrix products, arithmetic and copies ran while one was open for 0% of the time, Pallas kernels for 5%

profile of v3, /device:TPU:0, one launch (start us, length us, event | category | flops | bytes accessed | tf_op | source)
XLA Modules:
  0.0 162.6 jit_solution(5807403724398910253)
XLA Ops:
  0.6 0.7 convert_element_type.8
  1.3 0.1 compare_select_fusion
  1.4 0.7 fusion.1
  2.0 0.6 pad_bitcast_fusion.row_ref
  2.6 0.7 copy.21.seg_ref.refs_3_
  3.3 0.9 fusion
  4.2 3.5 %pack.1 = bf16[32,240,256]{2,1,0:T(8,128)(2,1)} custom-call(bf16[96,1280]{1,0:T(8,128)(2,1)} %q_ref.1, bf16[96,1280]{1,0:T(8,128)(2,1)} %k_ref.1, bf16[96,1280]{1,0:T(8,128)(2,1)} %v_ref.1, bf16[96,1280]{1,0:T(8,128)(2,1)} %qt_ref.1, bf16[96,1280]{1,0:T(8,128)(2,1)} %kt_ref.1, bf16[96,1280]{1,0:T(8,128)(2,1)} %vt_ref.1, ...), custom_call_target="tpu_custom_call" | custom-call | tf_op jit(solution)/shard_map/pack/pallas_call | solution.py:396
  7.7 61.1 %all_to_all.10.kv_ref = bf16[32,240,256]{2,1,0:T(8,128)(2,1)S(1)} all-to-all(bf16[32,240,256]{2,1,0:T(8,128)(2,1)} %pack.1), channel_id=1, replica_groups=mesh['z'=4,'y'=4,'x'=2,'c'=2,'head'=2] {'z','y','x'}, dimensions={0} | all-to-all | bytes 7864320 | tf_op jit(solution)/shard_map/spread/all_to_all | solution.py:407
  68.8 0.1 slice.4.qa_ref
  68.9 0.0 copy-start.2
  68.9 0.0 copy-start.5
  68.9 0.0 copy-start.6
  68.9 0.1 collective-permute-start
  69.0 2.3 %collective-permute-done.qb_ref = bf16[32,48,256]{2,1,0:T(8,128)(2,1)S(1)} collective-permute-done((bf16[32,48,256]{2,1,0:T(8,128)(2,1)S(1)}, bf16[32,48,256]{2,1,0:T(8,128)(2,1)S(1)}, u32[]{:S(2)}, u32[]{:S(2)}) %collective-permute-start) | collective-permute-done | bytes 786464 | tf_op jit(solution)/shard_map/spread/ppermute | solution.py:409
  71.3 12.8 %attend.2 = (bf16[32,96,128]{2,1,0:T(8,128)(2,1)S(1)}, bf16[32,96,128]{2,1,0:T(8,128)(2,1)S(1)}) custom-call(bf16[32,48,256]{2,1,0:T(8,128)(2,1)S(1)} %slice.4.qa_ref, bf16[32,48,256]{2,1,0:T(8,128)(2,1)S(1)} %collective-permute-done.qb_ref, bf16[32,240,256]{2,1,0:T(8,128)(2,1)S(1)} %all_to_all.10.kv_ref), custom_call_target="tpu_custom_call" | custom-call | flops 5000000000 | bytes 6291456 | tf_op jit(solution)/shard_map/attend/pallas_call | solution.py:194
  84.1 0.4 collective-permute-start.1
  84.5 2.1 %collective-permute-done.1.b_ref = bf16[32,96,128]{2,1,0:T(8,128)(2,1)S(1)} collective-permute-done((bf16[32,96,128]{2,1,0:T(8,128)(2,1)S(1)}, bf16[32,96,128]{2,1,0:T(8,128)(2,1)S(1)}, u32[]{:S(2)}, u32[]{:S(2)}) %collective-permute-start.1) | collective-permute-done | bytes 786464 | tf_op jit(solution)/shard_map/attend/ppermute | solution.py:414
  86.7 1.8 %attend.3 = bf16[32,64,128]{2,1,0:T(8,128)(2,1)} custom-call(bf16[32,96,128]{2,1,0:T(8,128)(2,1)S(1)} %get-tuple-element.15.a_ref, bf16[32,96,128]{2,1,0:T(8,128)(2,1)S(1)} %collective-permute-done.1.b_ref), custom_call_target="tpu_custom_call" | custom-call | tf_op jit(solution)/shard_map/attend/pallas_call | solution.py:236
  88.5 3.9 %all-to-all-start.1 = ((bf16[32,64,128]{2,1,0:T(8,128)(2,1)}), bf16[32,64,128]{2,1,0:T(8,128)(2,1)S(1)}, u32[]{:S(2)}, u32[]{:S(2)}) async-start(bf16[32,64,128]{2,1,0:T(8,128)(2,1)} %attend.3), calls=%async_computation.1 | async-start | bytes 1048576 | tf_op jit(solution)/shard_map/collect/all_to_all | solution.py:417
  92.4 14.3 %all-to-all-done.1.refs_1_ = bf16[32,64,128]{2,1,0:T(8,128)(2,1)S(1)} async-done(((bf16[32,64,128]{2,1,0:T(8,128)(2,1)}), bf16[32,64,128]{2,1,0:T(8,128)(2,1)S(1)}, u32[]{:S(2)}, u32[]{:S(2)}) %all-to-all-start.1) | async-done | bytes 524320 | tf_op jit(solution)/shard_map/collect/all_to_all | solution.py:417
  106.7 0.0 copy-done.2
  106.7 0.0 copy-done.5
  106.7 0.0 copy-done.6
  106.7 4.8 %project.3 = (f32[2,96,2560]{2,1,0:T(8,128)}, bf16[2,96,2560]{2,1,0:T(8,128)(2,1)S(1)}) custom-call(s32[1]{0:T(128)S(6)} %sub.3.refs_0_, bf16[32,64,128]{2,1,0:T(8,128)(2,1)S(1)} %all-to-all-done.1.refs_1_, bf16[1280,5120]{1,0:T(8,128)(2,1)} %refs_2_.3, f32[96,1]{1,0:T(8,128)S(1)} %copy-done.2, f32[2,5120]{1,0:T(2,128)S(1)} %copy-done.5, f32[2,5120]{1,0:T(2,128)S(1)} %copy-done.6), custom_call_target="tpu_custom_call" | custom-call | flops 1258291200 | bytes 10485760 | tf_op jit(solution)/shard_map/project/pallas_call | solution.py:286
  111.6 0.0 copy-start.7
  111.6 0.0 copy-start.8
  111.6 0.0 copy-start.9
  111.6 0.0 copy-start.10
  111.6 0.7 collective-permute-start.2
  112.3 6.3 %project.2 = (f32[2,96,2560]{2,1,0:T(8,128)}, bf16[2,96,2560]{2,1,0:T(8,128)(2,1)S(1)}) custom-call(s32[1]{0:T(128)} %bitcast.refs_0_.side_ref, bf16[32,64,128]{2,1,0:T(8,128)(2,1)S(1)} %all-to-all-done.1.refs_1_, bf16[1280,5120]{1,0:T(8,128)(2,1)} %refs_2_.3, f32[96,1]{1,0:T(8,128)S(1)} %copy-done.2, f32[2,5120]{1,0:T(2,128)S(1)} %copy-done.5, ...), custom_call_target="tpu_custom_call" | custom-call | flops 1258291200 | bytes 10485760 | tf_op jit(solution)/shard_map/project/pallas_call | solution.py:286
  118.6 0.0 copy-start
  118.6 1.5 collective-permute-start.3
  120.1 16.3 %collective-permute-done.2.got_ref = bf16[2,96,2560]{2,1,0:T(8,128)(2,1)S(1)} collective-permute-done((bf16[2,96,2560]{2,1,0:T(8,128)(2,1)S(1)}, bf16[2,96,2560]{2,1,0:T(8,128)(2,1)S(1)}, u32[]{:S(2)}, u32[]{:S(2)}) %collective-permute-start.2) | collective-permute-done | bytes 983072 | tf_op jit(solution)/shard_map/project/ppermute | solution.py:420
  136.4 0.0 copy-start.1
  136.4 1.5 copy-done.1
  137.9 1.9 %norm.2 = (f32[96,2560]{1,0:T(8,128)}, f32[96,2560]{1,0:T(8,128)}, f32[96,128]{1,0:T(8,128)S(1)}) custom-call(f32[2,96,2560]{2,1,0:T(8,128)S(1)} %copy-done.1, bf16[2,96,2560]{2,1,0:T(8,128)(2,1)S(1)} %collective-permute-done.2.got_ref), custom_call_target="tpu_custom_call" | custom-call | tf_op jit(solution)/shard_map/norm/pallas_call | solution.py:327
  139.9 15.6 %collective-permute-done.3.got_ref = bf16[2,96,2560]{2,1,0:T(8,128)(2,1)S(1)} collective-permute-done((bf16[2,96,2560]{2,1,0:T(8,128)(2,1)S(1)}, bf16[2,96,2560]{2,1,0:T(8,128)(2,1)S(1)}, u32[]{:S(2)}, u32[]{:S(2)}) %collective-permute-start.3) | collective-permute-done | bytes 983072 | tf_op jit(solution)/shard_map/project/ppermute | solution.py:422
  155.4 0.0 copy-done.7
  155.4 0.0 copy-done.8
  155.4 0.0 copy-done.9
  155.4 0.0 copy-done.10
  155.4 0.0 copy-done
  155.4 0.0 copy-start.3
  155.5 1.2 copy-done.3
  156.7 0.0 copy-start.4
  156.7 1.2 copy-done.4
  157.9 4.7 %norm.3 = (bf16[96,5120]{1,0:T(8,128)(2,1)}, bf16[96,5120]{1,0:T(8,128)(2,1)}) custom-call(s32[1]{0:T(128)} %bitcast.refs_0_.side_ref, f32[96,2560]{1,0:T(8,128)S(1)} %copy-done.3, f32[96,2560]{1,0:T(8,128)S(1)} %copy-done.4, f32[96,128]{1,0:T(8,128)S(1)} %get-tuple-element.21.sums_ref, f32[2,96,2560]{2,1,0:T(8,128)S(1)} %copy-done, ...), custom_call_target="tpu_custom_call" | custom-call | tf_op jit(solution)/shard_map/norm/pallas_call | solution.py:368
  (1 shorter events, 0.0 us)
Async XLA Ops:
  68.9 37.8 %copy-start.2 = (f32[96,1]{1,0:T(8,128)S(1)}, f32[96,1]{1,0:T(8,128)}, u32[]{:S(2)}) copy-start(f32[96,1]{1,0:T(8,128)} %copy.21.seg_ref.refs_3_) | copy-start | bytes 1156
  68.9 37.8 %copy-start.5 = (f32[2,5120]{1,0:T(2,128)S(1)}, f32[2,5120]{1,0:T(2,128)}, u32[]{:S(2)}) copy-start(f32[2,5120]{1,0:T(2,128)} %refs_4_.3) | copy-start | bytes 122884
  68.9 37.8 %copy-start.6 = (f32[2,5120]{1,0:T(2,128)S(1)}, f32[2,5120]{1,0:T(2,128)}, u32[]{:S(2)}) copy-start(f32[2,5120]{1,0:T(2,128)} %refs_5_.3) | copy-start | bytes 122884
  68.9 2.4 %collective-permute-start = (bf16[32,48,256]{2,1,0:T(8,128)(2,1)S(1)}, bf16[32,48,256]{2,1,0:T(8,128)(2,1)S(1)}, u32[]{:S(2)}, u32[]{:S(2)}) collective-permute-start(bf16[32,48,256]{2,1,0:T(8,128)(2,1)S(1)} %slice.4.qa_ref), channel_id=1, source_target_pairs={{0,2},{2,0},{1,3},{3,1},{4,6},{6,4},{5,7},{7,5},{8,10},{10,8},{9,1... | collective-permute-start | bytes 2359304 | tf_op jit(solution)/shard_map/spread/ppermute | solution.py:409
  84.1 2.5 %collective-permute-start.1 = (bf16[32,96,128]{2,1,0:T(8,128)(2,1)S(1)}, bf16[32,96,128]{2,1,0:T(8,128)(2,1)S(1)}, u32[]{:S(2)}, u32[]{:S(2)}) collective-permute-start(bf16[32,96,128]{2,1,0:T(8,128)(2,1)S(1)} %get-tuple-element.16), channel_id=1, source_target_pairs={{0,2},{2,0},{1,3},{3,1},{4,6},{6,4},{5,7},{7,5},{8,10},{10,8},{9,1... | collective-permute-start | bytes 2359304 | tf_op jit(solution)/shard_map/attend/ppermute | solution.py:414
  88.5 18.2 %all-to-all-start.1 = ((bf16[32,64,128]{2,1,0:T(8,128)(2,1)}), bf16[32,64,128]{2,1,0:T(8,128)(2,1)S(1)}, u32[]{:S(2)}, u32[]{:S(2)}) async-start(bf16[32,64,128]{2,1,0:T(8,128)(2,1)} %attend.3), calls=%async_computation.1 | async-start | bytes 1048576 | tf_op jit(solution)/shard_map/collect/all_to_all | solution.py:417
  111.6 43.9 %copy-start.7 = (f32[2,5120]{1,0:T(2,128)S(1)}, f32[2,5120]{1,0:T(2,128)}, u32[]{:S(2)}) copy-start(f32[2,5120]{1,0:T(2,128)} %scale_ref.1) | copy-start | bytes 122884
  111.6 43.9 %copy-start.8 = (f32[2,5120]{1,0:T(2,128)S(1)}, f32[2,5120]{1,0:T(2,128)}, u32[]{:S(2)}) copy-start(f32[2,5120]{1,0:T(2,128)} %scale_tan_ref.1) | copy-start | bytes 122884
  111.6 43.8 %copy-start.9 = (f32[2,5120]{1,0:T(2,128)S(1)}, f32[2,5120]{1,0:T(2,128)}, u32[]{:S(2)}) copy-start(f32[2,5120]{1,0:T(2,128)} %shift_ref.1) | copy-start | bytes 122884
  111.6 43.8 %copy-start.10 = (f32[2,5120]{1,0:T(2,128)S(1)}, f32[2,5120]{1,0:T(2,128)}, u32[]{:S(2)}) copy-start(f32[2,5120]{1,0:T(2,128)} %shift_tan_ref.1) | copy-start | bytes 122884
  111.6 24.8 %collective-permute-start.2 = (bf16[2,96,2560]{2,1,0:T(8,128)(2,1)S(1)}, bf16[2,96,2560]{2,1,0:T(8,128)(2,1)S(1)}, u32[]{:S(2)}, u32[]{:S(2)}) collective-permute-start(bf16[2,96,2560]{2,1,0:T(8,128)(2,1)S(1)} %get-tuple-element.18), channel_id=1, source_target_pairs={{0,1},{1,0},{2,3},{3,2},{4,5},{5,4},{6,7},{7,6},{8,9},{9,8},{10,11... | collective-permute-start | bytes 2949128 | tf_op jit(solution)/shard_map/project/ppermute | solution.py:420
  118.6 36.8 %copy-start = (f32[2,96,2560]{2,1,0:T(8,128)S(1)}, f32[2,96,2560]{2,1,0:T(8,128)}, u32[]{:S(2)}) copy-start(f32[2,96,2560]{2,1,0:T(8,128)} %get-tuple-element.22.keep_ref) | copy-start | bytes 5898244
  118.6 36.8 %collective-permute-start.3 = (bf16[2,96,2560]{2,1,0:T(8,128)(2,1)S(1)}, bf16[2,96,2560]{2,1,0:T(8,128)(2,1)S(1)}, u32[]{:S(2)}, u32[]{:S(2)}) collective-permute-start(bf16[2,96,2560]{2,1,0:T(8,128)(2,1)S(1)} %get-tuple-element.23), channel_id=1, source_target_pairs={{0,1},{1,0},{2,3},{3,2},{4,5},{5,4},{6,7},{7,6},{8,9},{9,8},{10,11... | collective-permute-start | bytes 2949128 | tf_op jit(solution)/shard_map/project/ppermute | solution.py:422
  136.4 1.5 copy-start.1
  155.4 1.2 copy-start.3
  156.7 1.2 copy-start.4

commit v4 on v3

v4 whole, which is shorter than its diff:
```python
import math

import jax
import jax.numpy as jnp
import numpy as np
from jax import lax
from jax.experimental import pallas as pl
from jax.experimental.pallas import tpu as pltpu
from jax.sharding import Mesh, PartitionSpec as P

D = 5120
HD = 128
NH = 10
ROWS = 96
THIRD = 32
CHIPS = 32
PARTS = 3
SPAN = 5
K, KT, V, VT, QT, Q, TAG, MSG = 0, 96, 192, 288, 384, 416, 448, 464
ASK = QT
HALF = D // 2

W = THIRD
SB = 8
KR = SB * ROWS
LONG, SHORT = (21, 3), (13, 2)
RMAX = LONG[0] * 2 * THIRD

neg_fill = -1e30
norm_eps = 1e-06
rope_base = 10000.0
ln2 = math.log(2.0)
exp_scale = math.log2(math.e) / math.sqrt(HD)

f32 = jnp.float32
bf16 = jnp.bfloat16
i32 = jnp.int32
VMEM = pl.BlockSpec(memory_space=pltpu.VMEM)
ANY = pl.BlockSpec(memory_space=pl.ANY)
NT = (((1,), (1,)), ((), ()))


def worker(h, t):
    return h // SPAN * (CHIPS // 2) + h % SPAN * PARTS + t


def params(mib=56):
    return pltpu.CompilerParams(vmem_limit_bytes=mib * 2**20)


def pack_kernel(q_hbm, k_hbm, v_hbm, qt_hbm, kt_hbm, vt_hbm, freq_ref, pos_ref, seg_ref, out_ref, tag_ref, held_ref, sem_in):
    reads = [pltpu.make_async_copy(x, held_ref.at[i], sem_in.at[i]) for i, x in enumerate((q_hbm, k_hbm, v_hbm, qt_hbm, kt_hbm, vt_hbm))]
    for copy in reads:
        copy.start()
    lane = lax.broadcasted_iota(i32, (ROWS, HD), 1)
    eye = lane == lax.broadcasted_iota(i32, (ROWS, HD), 0)
    pad = jnp.zeros((1, HD - ROWS), f32)
    clip_row = seg_ref[...].astype(f32)

    def column(row):
        return jnp.sum(jnp.where(eye, jnp.concatenate([row, pad], axis=1), 0.0), axis=1, keepdims=True)

    tag = column(clip_row)
    tag_ref[...] = jnp.broadcast_to(tag, (ROWS, HD))
    row = jnp.concatenate([pad, clip_row], axis=1)
    clips = []
    for t in range(PARTS):
        first, last = (tag[t * THIRD + i : t * THIRD + i + 16] for i in (0, 16))
        clips.append(jnp.where(lane[0:16] == 0, first, jnp.where(lane[0:16] == 1, last, row)).astype(bf16))
    angles = column(pos_ref[...].astype(f32)) * freq_ref[...]
    cos = jnp.cos(angles)
    sin = jnp.where(lane < HD // 2, -1.0, 1.0) * jnp.sin(angles)

    def rot(i, cols, factor):
        x = held_ref[i, :, cols].astype(f32)
        y = x * cos + jnp.roll(x, HD // 2, axis=1) * sin
        return (y if factor is None else y * factor).astype(bf16)

    for copy in reads:
        copy.wait()
    writes = []
    for h in range(NH):
        cols = slice(h * HD, (h + 1) * HD)
        q, k = rot(0, cols, exp_scale), rot(1, cols, None)
        qt, kt = rot(3, cols, exp_scale), rot(4, cols, None)
        v, vt = held_ref[2, :, cols], held_ref[5, :, cols]
        for t in range(PARTS):
            s = worker(h, t)
            at = t * THIRD
            out_ref[s, K:KT] = k
            out_ref[s, KT:V] = kt
            out_ref[s, V:VT] = v
            out_ref[s, VT:QT] = vt
            out_ref[s, QT:Q] = qt[at : at + THIRD]
            out_ref[s, Q:TAG] = q[at : at + THIRD]
            out_ref[s, TAG:MSG] = clips[t]
        if h % SPAN == SPAN - 1:
            out_ref[worker(h, 0) + PARTS] = jnp.zeros((MSG, HD), bf16)


def in_hbm(x):
    return pltpu.with_memory_space_constraint(x, pltpu.HBM)


def pack(arrays, freq, positions, segments):
    return pl.pallas_call(
        pack_kernel,
        in_specs=[ANY] * 6 + [VMEM] * 3,
        out_specs=[VMEM, VMEM],
        out_shape=[pltpu.VMEM((CHIPS, MSG, HD), bf16), pltpu.VMEM((ROWS, HD), f32)],
        scratch_shapes=[
            pltpu.VMEM((6, ROWS, NH * HD), bf16),
            pltpu.SemaphoreType.DMA((6,)),
        ],
        compiler_params=params(40),
    )(*[in_hbm(x) for x in (*arrays, freq, positions, segments)])


def bits(tiles):
    rows = jnp.concatenate([t.astype(f32)[0:1, :] for t in tiles], axis=0)
    lane = lax.broadcasted_iota(i32, (CHIPS, HD), 1)
    at = lax.broadcasted_iota(i32, (CHIPS, 1), 0)
    power = jnp.left_shift(jnp.ones((CHIPS, 1), i32), at & 15).astype(f32)
    has0 = 1.0 - jnp.min(jnp.where(lane < 32, 1.0, rows), axis=1, keepdims=True)
    has1 = jnp.max(jnp.where(lane < 32, 0.0, rows), axis=1, keepdims=True)

    def scalar(has):
        low = jnp.sum(jnp.where(at < 16, has * power, 0.0)).astype(i32)
        high = jnp.sum(jnp.where(at < 16, 0.0, has * power)).astype(i32)
        return low | (high << 16)

    return scalar(has0), scalar(has1)


def attn_kernel(qa_ref, qb_ref, kv_ref, oa_ref, ob_ref, s_ref, acc_ref, acct_ref, l_ref, pen_ref, keys_ref, kind_ref, chips_ref, cut_ref):
    own = bits([kv_ref[j, TAG:MSG, :] for j in range(CHIPS)])
    sib = bits([qb_ref[j, TAG - ASK : MSG - ASK, :] for j in range(CHIPS)])
    cut_ref[0] = i32(0)
    cut_ref[1] = i32(0)

    def sort(j, carry):
        cuts, counts = carry[0], list(carry[1:])
        has = [(own[c] >> j) & 1 for c in range(2)]
        both = has[0] & has[1]
        cut_ref[jnp.where(both == 1, jnp.minimum(cuts, 1), 2)] = j
        for c in range(2):
            at = jnp.where(has[c] == 1, counts[c], 31 - (j - counts[c]))
            keys_ref[c, at] = j
            kind_ref[c, at] = jnp.where(both == 1, 2 + 2 * c + jnp.minimum(cuts, 1), 1 - has[c])
            counts[c] = counts[c] + has[c]
            any_has = ((own[c] | sib[c]) >> j) & 1
            n = counts[2 + c]
            chips_ref[c, jnp.where(any_has == 1, n, 31 - (j - n))] = j
            counts[2 + c] = n + any_has
        return (cuts + both, *counts)

    zero = i32(0)
    counted = lax.fori_loop(0, CHIPS, sort, (zero,) * 5)
    long_clip = jnp.where(counted[4] > 16, 1, 0)

    lane = lax.broadcasted_iota(i32, (ROWS, HD), 1)
    eye = lane == lax.broadcasted_iota(i32, (ROWS, HD), 0) + 32
    pen_ref[0] = jnp.zeros((ROWS, HD), bf16)
    pen_ref[1] = jnp.where(lane == 0, neg_fill, 0.0).astype(bf16)
    for p in range(2):
        row = kv_ref[cut_ref[p], TAG:MSG, :].astype(f32)[0:1, :]
        col = jnp.sum(jnp.where(eye, row, 0.0), axis=1, keepdims=True)
        pen_ref[2 + p] = jnp.where(lane == 0, col * neg_fill, 0.0).astype(bf16)
        pen_ref[4 + p] = jnp.where(lane == 0, (1.0 - col) * neg_fill, 0.0).astype(bf16)

    for (chips, blocks), clip in ((LONG, long_clip), (SHORT, 1 - long_clip)):
        R = chips * 2 * THIRD
        listed = [chips_ref[clip, i] for i in range(chips)]
        qt, q = [jnp.concatenate([ref[j, at - ASK : at - ASK + THIRD, :] for j in listed for ref in (qa_ref, qb_ref)], axis=0) for at in (QT, Q)]
        qq = jnp.concatenate([qt, q], axis=1)
        one = jnp.where(lax.broadcasted_iota(i32, (R, HD), 1) == 0, 1.0, 0.0).astype(bf16)
        q = jnp.concatenate([q, one], axis=1)
        m = jnp.full((R, HD), neg_fill, f32)
        for b in range(blocks):
            pairs = [(keys_ref[clip, b * SB + u], kind_ref[clip, b * SB + u]) for u in range(SB)]
            k = jnp.concatenate([jnp.concatenate([kv_ref[j, K:KT, :], pen_ref[n]], axis=1) for j, n in pairs], axis=0)
            s = lax.dot_general(q, k, NT, preferred_element_type=f32)
            s_ref[b, 0:R] = s
            for j in range(KR // HD):
                m = jnp.maximum(m, s[:, j * HD : (j + 1) * HD])
        top = jnp.max(m, axis=1, keepdims=True)
        for b in range(blocks):
            js = [keys_ref[clip, b * SB + u] for u in range(SB)]
            k, kt, v, vt = [jnp.concatenate([kv_ref[j, at : at + ROWS, :] for j in js], axis=0) for at in (K, KT, V, VT)]
            k = jnp.concatenate([k, kt], axis=1)
            v1 = jnp.concatenate([v, jnp.ones((KR, HD), bf16)], axis=1)
            v = jnp.concatenate([v, vt], axis=1)
            st = lax.dot_general(qq, k, NT, preferred_element_type=f32)
            p = jnp.exp2(s_ref[b, 0:R] - top)
            pt = (p * st).astype(bf16)
            l = p[:, 0:HD]
            for j in range(1, KR // HD):
                l = l + p[:, j * HD : (j + 1) * HD]
            acc = jnp.dot(p.astype(bf16), v, preferred_element_type=f32)
            acct = jnp.dot(pt, v1, preferred_element_type=f32)
            if b == 0:
                l_ref[0:R], acc_ref[0:R], acct_ref[0:R] = l, acc, acct
            else:
                l_ref[0:R] += l
                acc_ref[0:R] += acc
                acct_ref[0:R] += acct
        total = jnp.sum(l_ref[0:R], axis=1, keepdims=True)
        inv = 1.0 / total
        inv_tan = inv * ln2
        drift = acct_ref[0:R, 128:256] * inv_tan
        o = acc_ref[0:R, 0:128] * inv
        t = acct_ref[0:R, 0:128] * inv_tan + acc_ref[0:R, 128:256] * inv - drift * o
        lse = jnp.broadcast_to(top + jnp.log2(total), (R, HD))
        where = lax.broadcasted_iota(i32, (R, HD), 1)
        pieces = jnp.zeros((R, HD), f32)
        for first, x in ((0, lse), (3, drift)):
            for i in range(3):
                piece = x.astype(bf16).astype(f32)
                pieces = jnp.where(where == first + i, piece, pieces)
                x = x - piece
        whole = [x.astype(bf16) for x in (o, t, pieces)]
        wanted = clip.astype(f32)
        for i, j in enumerate(listed):
            for core, (q_ref, out_ref) in enumerate(((qa_ref, oa_ref), (qb_ref, ob_ref))):
                at = (2 * i + core) * W
                tags = q_ref[j, TAG - ASK : MSG - ASK, :].astype(f32)
                tag = jnp.concatenate([tags[:, 0:1], tags[:, 1:2]], axis=0)
                hit = jnp.broadcast_to(tag, (W, HD)) == wanted
                for n, x in enumerate(whole):
                    old = out_ref[j, n * W : (n + 1) * W, :].astype(f32)
                    out_ref[j, n * W : (n + 1) * W, :] = jnp.where(hit, x[at : at + W].astype(f32), old).astype(bf16)


def attend(asked, asked_there, arrived):
    out = pltpu.VMEM((CHIPS, 3 * W, HD), bf16)
    return pl.pallas_call(
        attn_kernel,
        in_specs=[VMEM] * 3,
        out_specs=[VMEM] * 2,
        out_shape=[out] * 2,
        scratch_shapes=[
            pltpu.VMEM((LONG[1], RMAX, KR), f32),
            pltpu.VMEM((RMAX, 256), f32),
            pltpu.VMEM((RMAX, 256), f32),
            pltpu.VMEM((RMAX, HD), f32),
            pltpu.VMEM((6, ROWS, HD), bf16),
            pltpu.SMEM((2, CHIPS), i32),
            pltpu.SMEM((2, CHIPS), i32),
            pltpu.SMEM((2, CHIPS), i32),
            pltpu.SMEM((3,), i32),
        ],
        compiler_params=params(40),
        cost_estimate=pl.CostEstimate(flops=9 * 10**9, bytes_accessed=6 * 2**20, transcendentals=4 * 10**6),
    )(*[pltpu.with_memory_space_constraint(x, pltpu.VMEM) for x in (asked, asked_there, arrived)])


def combine_kernel(a_ref, b_ref, out_ref):
    R = CHIPS * W

    def read(ref):
        o, t, s = [ref[:, n * W : (n + 1) * W, :].astype(f32).reshape(R, HD) for n in range(3)]
        lse = s[:, 0:1] + s[:, 1:2] + s[:, 2:3]
        drift = s[:, 3:4] + s[:, 4:5] + s[:, 5:6]
        return o, t, lse, drift

    oa, ta, la, da = read(a_ref)
    ob, tb, lb, db = read(b_ref)
    top = jnp.maximum(la, lb)
    wa, wb = jnp.exp2(la - top), jnp.exp2(lb - top)
    inv = 1.0 / (wa + wb)
    wa, wb = wa * inv, wb * inv
    gap = wa * wb * (da - db)
    out_ref[:, 0:W, :] = (wa * oa + wb * ob).astype(bf16).reshape(CHIPS, W, HD)
    out_ref[:, W : 2 * W, :] = (wa * ta + wb * tb + gap * (oa - ob)).astype(bf16).reshape(CHIPS, W, HD)


def combine(a, b):
    return pl.pallas_call(
        combine_kernel,
        in_specs=[VMEM, VMEM],
        out_specs=VMEM,
        out_shape=pltpu.VMEM((CHIPS, 2 * W, HD), bf16),
        compiler_params=params(16),
    )(a, b)


CT = 512
STEPS = HALF // CT


def project_kernel(side_ref, x_ref, w_hbm, seg_ref, gate_ref, gate_tan_ref, *refs, own):
    if own:
        resid_ref, resid_tan_ref, send_ref, lhs_ref, held_ref, sem = refs
    else:
        send_ref, lhs_ref, held_ref, sem = refs
    start = side_ref[0] * HALF
    reads = []
    for j in range(STEPS):
        cols = pl.ds(pl.multiple_of(start + j * CT, CT), CT)
        reads.append(pltpu.make_async_copy(w_hbm.at[:, cols], held_ref.at[j], sem.at[j]))
        reads[j].start()
    for h in range(NH):
        for t in range(PARTS):
            s = worker(h, t)
            lhs_ref[t * W : (t + 1) * W, h * HD : (h + 1) * HD] = x_ref[s, 0:W, :]
            lhs_ref[ROWS + t * W : ROWS + (t + 1) * W, h * HD : (h + 1) * HD] = x_ref[s, W : 2 * W, :]
    one = seg_ref[:, 0:1] == 1.0
    for j in range(STEPS):
        reads[j].wait()
        out = jnp.dot(lhs_ref[...], held_ref[j], preferred_element_type=f32)
        cols = pl.ds(pl.multiple_of(start + j * CT, CT), CT)
        here = slice(j * CT, (j + 1) * CT)
        gate = jnp.where(one, gate_ref[1:2, cols], gate_ref[0:1, cols])
        gate_tan = jnp.where(one, gate_tan_ref[1:2, cols], gate_tan_ref[0:1, cols])
        a = gate * out[0:ROWS]
        b = gate_tan * out[0:ROWS] + gate * out[ROWS : 2 * ROWS]
        if own:
            a = a + resid_ref[:, here]
            b = b + resid_tan_ref[:, here]
        send_ref[0, :, here] = a.astype(bf16)
        send_ref[1, :, here] = b.astype(bf16)


def project(side, x, w, seg, gate, gate_tan, resid):
    own = len(resid) > 0
    return pl.pallas_call(
        lambda *refs: project_kernel(*refs, own=own),
        in_specs=[pl.BlockSpec(memory_space=pltpu.SMEM), VMEM, ANY] + [VMEM] * (3 + len(resid)),
        out_specs=VMEM,
        out_shape=pltpu.VMEM((2, ROWS, HALF), bf16),
        scratch_shapes=[
            pltpu.VMEM((2 * ROWS, NH * HD), bf16),
            pltpu.VMEM((STEPS, NH * HD, CT), bf16),
            pltpu.SemaphoreType.DMA((STEPS,)),
        ],
        compiler_params=params(48),
        cost_estimate=pl.CostEstimate(flops=2 * 2 * ROWS * NH * HD * HALF, bytes_accessed=10 * 2**20, transcendentals=0),
    )(side, x, in_hbm(w), seg, gate, gate_tan, *resid)


FT = 32


def norm_kernel(
    side_ref, mine_ref, got_mine_ref, other_ref, got_other_ref, seg_ref, scale_ref, scale_tan_ref, shift_ref, shift_tan_ref,
    resid_ref, resid_tan_ref, ffn_ref, ffn_tan_ref,
):
    a = [mine_ref[0].astype(f32) + got_mine_ref[0].astype(f32), other_ref[0].astype(f32) + got_other_ref[0].astype(f32)]
    b = [mine_ref[1].astype(f32) + got_mine_ref[1].astype(f32), other_ref[1].astype(f32) + got_other_ref[1].astype(f32)]
    resid_ref[...] = a[0]
    resid_tan_ref[...] = b[0]

    def average(x, y):
        return jnp.sum(x + y, axis=1, keepdims=True) / D

    mean, mean_tan = average(*a), average(*b)
    rstd = lax.rsqrt(average(a[0] * a[0], a[1] * a[1]) - mean * mean + norm_eps)
    cov = average(a[0] * b[0], a[1] * b[1]) - mean * mean_tan
    slope = rstd * rstd * rstd * cov
    one = seg_ref[:, 0:1] == 1.0
    for i, side in enumerate((side_ref[0], 1 - side_ref[0])):
        cols = pl.ds(pl.multiple_of(side * HALF, HALF), HALF)

        def pick(ref):
            return jnp.where(one, ref[1:2, cols], ref[0:1, cols])

        centered = a[i] - mean
        normed = centered * rstd
        normed_tan = (b[i] - mean_tan) * rstd - centered * slope
        scale = 1.0 + pick(scale_ref)
        ffn_ref[:, cols] = (normed * scale + pick(shift_ref)).astype(bf16)
        ffn_tan_ref[:, cols] = (normed_tan * scale + normed * pick(scale_tan_ref) + pick(shift_tan_ref)).astype(bf16)


def norm(side, mine, got_mine, other, got_other, seg, tables):
    pair = pl.BlockSpec((2, FT, HALF), lambda j: (0, j, 0))
    half = pl.BlockSpec((FT, HALF), lambda j: (j, 0))
    full = pl.BlockSpec((FT, D), lambda j: (j, 0))
    return pl.pallas_call(
        norm_kernel,
        grid=(ROWS // FT,),
        in_specs=[pl.BlockSpec(memory_space=pltpu.SMEM)] + [pair] * 4 + [pl.BlockSpec((FT, HD), lambda j: (j, 0))]
        + [pl.BlockSpec((2, D), lambda j: (0, 0))] * 4,
        out_specs=[half, half, full, full],
        out_shape=[jax.ShapeDtypeStruct((ROWS, HALF), f32)] * 2 + [jax.ShapeDtypeStruct((ROWS, D), bf16)] * 2,
        compiler_params=params(40),
    )(side, mine, got_mine, other, got_other, seg, *tables)


def body(
    queries, keys, values, queries_tan, keys_tan, values_tan, segments, positions, out_weight,
    residual, residual_tan, gate, gate_tan, mod_scale, mod_scale_tan, mod_shift, mod_shift_tan,
):
    frequency = np.float32(rope_base) ** (-np.arange(HD // 2, dtype=np.float32) / np.float32(HD // 2))
    freq = np.concatenate([frequency, frequency])[None, :].astype(np.float32)
    swap = [(0, 1), (1, 0)]

    with jax.named_scope("pack"):
        arrays = (queries, keys, values, queries_tan, keys_tan, values_tan)
        message, seg = pack(arrays, freq, positions[None, :], segments[None, :])
    with jax.named_scope("spread"):
        arrived = lax.all_to_all(message, ("z", "y", "x"), 0, 0, tiled=True)
        asked = lax.slice_in_dim(arrived, ASK, MSG, axis=1)
        asked_there = lax.ppermute(asked, "c", swap)

    side = lax.axis_index("head").astype(i32).reshape(1)
    with jax.named_scope("attend"):
        part, there = attend(asked, asked_there, arrived)
        back = lax.ppermute(there, "c", swap)
        answer = combine(part, back)
    with jax.named_scope("collect"):
        attended = lax.all_to_all(answer, ("z", "y", "x"), 0, 0, tiled=True)
    with jax.named_scope("project"):
        other = project(1 - side, attended, out_weight, seg, gate, gate_tan, ())
        got_mine = lax.ppermute(other, "head", swap)
        mine = project(side, attended, out_weight, seg, gate, gate_tan, (residual, residual_tan))
        got_other = lax.ppermute(mine, "head", swap)
    with jax.named_scope("norm"):
        return tuple(norm(side, mine, got_mine, other, got_other, seg, (mod_scale, mod_scale_tan, mod_shift, mod_shift_tan)))


def solution(mesh):
    fine = Mesh(mesh.devices.reshape(4, 4, 2, 2, 2), ("z", "y", "x", "c", "head"))
    seq = ("z", "y", "x", "c")
    split = P(seq, "head")
    in_specs = (split,) * 6 + (P(seq), P(seq), P("head", None), split, split) + (P(),) * 6
    out_specs = (split, split, P(seq, None), P(seq, None))
    return jax.shard_map(body, mesh=fine, in_specs=in_specs, out_specs=out_specs, check_vma=False)
```

time: 163 us -> 152 us (0.933)
  Pallas kernels: 35.9 us -> 28.6 us
  waiting for transfers between devices: 50.5 us -> 56.7 us
  local copies, waits for them, and re-layouts: 5.35 us -> 0.09 us
  other arithmetic: 2.3 us -> 0 us
    ppermute x2, waiting for transfers between devices: 31.8 us -> 38.1 us  [the longest x1 19.1 us: body(): got_other = lax.ppermute(mine, 'head', swap)]
    pallas_call x2, Pallas kernels: 11.1 us -> 7.04 us  [project(): pl.pallas_call(lambda *refs: project_kernel(*refs, own=own), in_specs=[pl...]
    unnamed x22 -> x16, local copies, waits for them, and re-layouts: 3.99 us -> 0.05 us
    pallas_call x2 -> x1, Pallas kernels: 5.43 us -> 2.9 us  [pack(): pl.pallas_call(pack_kernel, in_specs=[ANY] * 6 + [VMEM] * 3, out_specs=[V...]
  transfers between devices with their start and end apart: 5 -> 5, of which waited for: 5 -> 5; matrix products, arithmetic and copies ran while one was open for 0% -> 0% of each run, Pallas kernels for 5% -> 2%
where the time goes in v4:
time: 152 us
  blocking collectives  59.5 us (39%)
  waiting for transfers between devices  56.7 us (37%)
  Pallas kernels  28.6 us (19%)
  starting transfers between devices  6.55 us (4%)
    all_to_all x1, blocking collectives, body(): arrived = lax.all_to_all(message, ('z', 'y', 'x'), 0, 0, tiled=True)  59.5 us
    ppermute x1, waiting for transfers between devices, body(): got_other = lax.ppermute(mine, 'head', swap)  19.1 us
    ppermute x1, waiting for transfers between devices, body(): got_mine = lax.ppermute(other, 'head', swap)  19.1 us
    all_to_all x1, waiting for transfers between devices, body(): attended = lax.all_to_all(answer, ('z', 'y', 'x'), 0, 0, tiled=True)  14.3 us
    pallas_call x1, Pallas kernels, attend(): pl.pallas_call(attn_kernel, in_specs=[VMEM] * 3, out_specs=[VMEM] * 2, ou...  12.5 us
    pallas_call x2, Pallas kernels, project(): pl.pallas_call(lambda *refs: project_kernel(*refs, own=own), in_specs=[pl...  7.04 us
    pallas_call x1, Pallas kernels, norm(): pl.pallas_call(norm_kernel, grid=(ROWS // FT,), in_specs=[pl.BlockSpec(me...  4.31 us
    all_to_all x1, starting transfers between devices, body(): attended = lax.all_to_all(answer, ('z', 'y', 'x'), 0, 0, tiled=True)  3.89 us
  transfers between devices with their start and end apart: 5, of which 5 were waited for; matrix products, arithmetic and copies ran while one was open for 0% of the time, Pallas kernels for 2%

profile of v4, /device:TPU:0, one launch (start us, length us, event | category | flops | bytes accessed | tf_op | source)
XLA Modules:
  0.0 152.2 jit_solution(8604199977702153749)
XLA Ops:
  0.6 2.9 %pack.1 = (bf16[32,464,128]{2,1,0:T(8,128)(2,1)S(1)}, f32[96,128]{1,0:T(8,128)S(1)}) custom-call(bf16[96,1280]{1,0:T(8,128)(2,1)} %q_hbm.1, bf16[96,1280]{1,0:T(8,128)(2,1)} %k_hbm.1, bf16[96,1280]{1,0:T(8,128)(2,1)} %v_hbm.1, bf16[96,1280]{1,0:T(8,128)(2,1)} %qt_hbm.1, bf16[96,1280]{1,0:T(8,128)(2,1)} %kt_hbm.1, bf16[96,1280]{1,0:T(8,128)(2,1)} %vt_hbm.1, ...), custom_call_target="tpu_custom_call" | custom-call | tf_op jit(solution)/shard_map/pack/pallas_call | solution.py:106
  3.5 59.5 %all_to_all.10.kv_ref = bf16[32,464,128]{2,1,0:T(8,128)(2,1)S(1)} all-to-all(bf16[32,464,128]{2,1,0:T(8,128)(2,1)S(1)} %get-tuple-element.8), channel_id=1, replica_groups=mesh['z'=4,'y'=4,'x'=2,'c'=2,'head'=2] {'z','y','x'}, dimensions={0} | all-to-all | bytes 7602176 | tf_op jit(solution)/shard_map/spread/all_to_all | solution.py:402
  63.1 0.0 copy-start.2
  63.1 0.0 copy-start.3
  63.1 0.1 collective-permute-start
  63.2 2.1 %collective-permute-done.qb_ref = bf16[32,80,128]{2,1,0:T(8,128)(2,1)S(1)} collective-permute-done((bf16[32,80,128]{2,1,0:T(8,128)(2,1)S(1)}, bf16[32,80,128]{2,1,0:T(8,128)(2,1)S(1)}, u32[]{:S(2)}, u32[]{:S(2)}) %collective-permute-start) | collective-permute-done | bytes 655392 | tf_op jit(solution)/shard_map/spread/ppermute | solution.py:404
  65.3 12.5 %attend.2 = (bf16[32,96,128]{2,1,0:T(8,128)(2,1)S(1)}, bf16[32,96,128]{2,1,0:T(8,128)(2,1)S(1)}) custom-call(bf16[32,80,128]{2,1,0:T(8,128)(2,1)S(1)} %slice.4.qa_ref, bf16[32,80,128]{2,1,0:T(8,128)(2,1)S(1)} %collective-permute-done.qb_ref, bf16[32,464,128]{2,1,0:T(8,128)(2,1)S(1)} %all_to_all.10.kv_ref), custom_call_target="tpu_custom_call" | custom-call | flops 8999999488 | bytes 6291456 | tf_op jit(solution)/shard_map/attend/pallas_call | solution.py:236
  77.8 0.0 copy-start
  77.8 0.0 copy-start.1
  77.8 0.4 collective-permute-start.1
  78.2 2.2 %collective-permute-done.1.b_ref = bf16[32,96,128]{2,1,0:T(8,128)(2,1)S(1)} collective-permute-done((bf16[32,96,128]{2,1,0:T(8,128)(2,1)S(1)}, bf16[32,96,128]{2,1,0:T(8,128)(2,1)S(1)}, u32[]{:S(2)}, u32[]{:S(2)}) %collective-permute-start.1) | collective-permute-done | bytes 786464 | tf_op jit(solution)/shard_map/attend/ppermute | solution.py:409
  80.4 1.8 %attend.3 = bf16[32,64,128]{2,1,0:T(8,128)(2,1)} custom-call(bf16[32,96,128]{2,1,0:T(8,128)(2,1)S(1)} %get-tuple-element.9.a_ref, bf16[32,96,128]{2,1,0:T(8,128)(2,1)S(1)} %collective-permute-done.1.b_ref), custom_call_target="tpu_custom_call" | custom-call | tf_op jit(solution)/shard_map/attend/pallas_call | solution.py:278
  82.2 3.9 %all-to-all-start.1 = ((bf16[32,64,128]{2,1,0:T(8,128)(2,1)}), bf16[32,64,128]{2,1,0:T(8,128)(2,1)S(1)}, u32[]{:S(2)}, u32[]{:S(2)}) async-start(bf16[32,64,128]{2,1,0:T(8,128)(2,1)} %attend.3), calls=%async_computation.1 | async-start | bytes 1048576 | tf_op jit(solution)/shard_map/collect/all_to_all | solution.py:412
  86.1 14.3 %all-to-all-done.1.refs_1_ = bf16[32,64,128]{2,1,0:T(8,128)(2,1)S(1)} async-done(((bf16[32,64,128]{2,1,0:T(8,128)(2,1)}), bf16[32,64,128]{2,1,0:T(8,128)(2,1)S(1)}, u32[]{:S(2)}, u32[]{:S(2)}) %all-to-all-start.1) | async-done | bytes 524320 | tf_op jit(solution)/shard_map/collect/all_to_all | solution.py:412
  100.4 0.0 copy-done.2
  100.4 0.0 copy-done.3
  100.4 0.0 copy-done
  100.5 0.0 copy-done.1
  100.5 3.5 %project.2.mine_ref = bf16[2,96,2560]{2,1,0:T(8,128)(2,1)S(1)} custom-call(s32[1]{0:T(128)} %bitcast.refs_0_.side_ref, bf16[32,64,128]{2,1,0:T(8,128)(2,1)S(1)} %all-to-all-done.1.refs_1_, bf16[1280,5120]{1,0:T(8,128)(2,1)} %refs_2_.3, f32[96,128]{1,0:T(8,128)S(1)} %get-tuple-element.11.refs_3_.seg_ref, f32[2,5120]{1,0:T(2,128)S(1)} %copy-done.2, ...), custom_call_target="tpu_custom_call" | custom-call | flops 1258291200 | bytes 10485760 | tf_op jit(solution)/shard_map/project/pallas_call | solution.py:326
  104.0 0.0 copy-start.4
  104.0 0.0 copy-start.5
  104.0 0.0 copy-start.6
  104.0 0.0 copy-start.7
  104.0 0.7 collective-permute-start.3
  104.8 3.5 %project.3.other_ref = bf16[2,96,2560]{2,1,0:T(8,128)(2,1)S(1)} custom-call(s32[1]{0:T(128)S(6)} %sub.3.refs_0_, bf16[32,64,128]{2,1,0:T(8,128)(2,1)S(1)} %all-to-all-done.1.refs_1_, bf16[1280,5120]{1,0:T(8,128)(2,1)} %refs_2_.3, f32[96,128]{1,0:T(8,128)S(1)} %get-tuple-element.11.refs_3_.seg_ref, f32[2,5120]{1,0:T(2,128)S(1)} %copy-done.2, ...), custom_call_target="tpu_custom_call" | custom-call | flops 1258291200 | bytes 10485760 | tf_op jit(solution)/shard_map/project/pallas_call | solution.py:326
  108.3 1.5 collective-permute-start.2
  109.8 19.1 %collective-permute-done.3.got_other_ref = bf16[2,96,2560]{2,1,0:T(8,128)(2,1)S(1)} collective-permute-done((bf16[2,96,2560]{2,1,0:T(8,128)(2,1)S(1)}, bf16[2,96,2560]{2,1,0:T(8,128)(2,1)S(1)}, u32[]{:S(2)}, u32[]{:S(2)}) %collective-permute-start.3) | collective-permute-done | bytes 983072 | tf_op jit(solution)/shard_map/project/ppermute | solution.py:417
  128.8 19.1 %collective-permute-done.2.got_mine_ref = bf16[2,96,2560]{2,1,0:T(8,128)(2,1)S(1)} collective-permute-done((bf16[2,96,2560]{2,1,0:T(8,128)(2,1)S(1)}, bf16[2,96,2560]{2,1,0:T(8,128)(2,1)S(1)}, u32[]{:S(2)}, u32[]{:S(2)}) %collective-permute-start.2) | collective-permute-done | bytes 983072 | tf_op jit(solution)/shard_map/project/ppermute | solution.py:415
  147.9 0.0 copy-done.4
  147.9 0.0 copy-done.5
  147.9 0.0 copy-done.6
  147.9 0.0 copy-done.7
  147.9 4.3 %norm.1 = (f32[96,2560]{1,0:T(8,128)}, f32[96,2560]{1,0:T(8,128)}, bf16[96,5120]{1,0:T(8,128)(2,1)}, bf16[96,5120]{1,0:T(8,128)(2,1)}) custom-call(s32[1]{0:T(128)} %bitcast.refs_0_.side_ref, bf16[2,96,2560]{2,1,0:T(8,128)(2,1)S(1)} %project.2.mine_ref, bf16[2,96,2560]{2,1,0:T(8,128)(2,1)S(1)} %collective-permute-done.2.got_mine_ref, ...), custom_call_target="tpu_custom_call" | custom-call | tf_op jit(solution)/shard_map/norm/pallas_call | solution.py:379
  (1 shorter events, 0.0 us)
Async XLA Ops:
  63.1 37.3 %copy-start.2 = (f32[2,5120]{1,0:T(2,128)S(1)}, f32[2,5120]{1,0:T(2,128)}, u32[]{:S(2)}) copy-start(f32[2,5120]{1,0:T(2,128)} %refs_4_.3) | copy-start | bytes 122884
  63.1 37.3 %copy-start.3 = (f32[2,5120]{1,0:T(2,128)S(1)}, f32[2,5120]{1,0:T(2,128)}, u32[]{:S(2)}) copy-start(f32[2,5120]{1,0:T(2,128)} %refs_5_.3) | copy-start | bytes 122884
  63.1 2.2 %collective-permute-start = (bf16[32,80,128]{2,1,0:T(8,128)(2,1)S(1)}, bf16[32,80,128]{2,1,0:T(8,128)(2,1)S(1)}, u32[]{:S(2)}, u32[]{:S(2)}) collective-permute-start(bf16[32,80,128]{2,1,0:T(8,128)(2,1)S(1)} %slice.4.qa_ref), channel_id=1, source_target_pairs={{0,2},{2,0},{1,3},{3,1},{4,6},{6,4},{5,7},{7,5},{8,10},{10,8},{9,1... | collective-permute-start | bytes 1966088 | tf_op jit(solution)/shard_map/spread/ppermute | solution.py:404
  77.8 22.6 %copy-start = (f32[96,2560]{1,0:T(8,128)S(1)}, f32[96,2560]{1,0:T(8,128)}, u32[]{:S(2)}) copy-start(f32[96,2560]{1,0:T(8,128)} %refs_6_.1) | copy-start | bytes 2949124
  77.8 22.6 %copy-start.1 = (f32[96,2560]{1,0:T(8,128)S(1)}, f32[96,2560]{1,0:T(8,128)}, u32[]{:S(2)}) copy-start(f32[96,2560]{1,0:T(8,128)} %refs_7_.1) | copy-start | bytes 2949124
  77.8 2.5 %collective-permute-start.1 = (bf16[32,96,128]{2,1,0:T(8,128)(2,1)S(1)}, bf16[32,96,128]{2,1,0:T(8,128)(2,1)S(1)}, u32[]{:S(2)}, u32[]{:S(2)}) collective-permute-start(bf16[32,96,128]{2,1,0:T(8,128)(2,1)S(1)} %get-tuple-element.10), channel_id=1, source_target_pairs={{0,2},{2,0},{1,3},{3,1},{4,6},{6,4},{5,7},{7,5},{8,10},{10,8},{9,1... | collective-permute-start | bytes 2359304 | tf_op jit(solution)/shard_map/attend/ppermute | solution.py:409
  82.2 18.2 %all-to-all-start.1 = ((bf16[32,64,128]{2,1,0:T(8,128)(2,1)}), bf16[32,64,128]{2,1,0:T(8,128)(2,1)S(1)}, u32[]{:S(2)}, u32[]{:S(2)}) async-start(bf16[32,64,128]{2,1,0:T(8,128)(2,1)} %attend.3), calls=%async_computation.1 | async-start | bytes 1048576 | tf_op jit(solution)/shard_map/collect/all_to_all | solution.py:412
  104.0 43.9 %copy-start.4 = (f32[2,5120]{1,0:T(2,128)S(1)}, f32[2,5120]{1,0:T(2,128)}, u32[]{:S(2)}) copy-start(f32[2,5120]{1,0:T(2,128)} %scale_ref.1) | copy-start | bytes 122884
  104.0 43.9 %copy-start.5 = (f32[2,5120]{1,0:T(2,128)S(1)}, f32[2,5120]{1,0:T(2,128)}, u32[]{:S(2)}) copy-start(f32[2,5120]{1,0:T(2,128)} %scale_tan_ref.1) | copy-start | bytes 122884
  104.0 43.9 %copy-start.6 = (f32[2,5120]{1,0:T(2,128)S(1)}, f32[2,5120]{1,0:T(2,128)}, u32[]{:S(2)}) copy-start(f32[2,5120]{1,0:T(2,128)} %shift_ref.1) | copy-start | bytes 122884
  104.0 43.9 %copy-start.7 = (f32[2,5120]{1,0:T(2,128)S(1)}, f32[2,5120]{1,0:T(2,128)}, u32[]{:S(2)}) copy-start(f32[2,5120]{1,0:T(2,128)} %shift_tan_ref.1) | copy-start | bytes 122884
  104.0 24.8 %collective-permute-start.3 = (bf16[2,96,2560]{2,1,0:T(8,128)(2,1)S(1)}, bf16[2,96,2560]{2,1,0:T(8,128)(2,1)S(1)}, u32[]{:S(2)}, u32[]{:S(2)}) collective-permute-start(bf16[2,96,2560]{2,1,0:T(8,128)(2,1)S(1)} %project.2.mine_ref), channel_id=1, source_target_pairs={{0,1},{1,0},{2,3},{3,2},{4,5},{5,4},{6,7},{7,6},{8,9},{9,8},{10,11... | collective-permute-start | bytes 2949128 | tf_op jit(solution)/shard_map/project/ppermute | solution.py:417
  108.3 39.6 %collective-permute-start.2 = (bf16[2,96,2560]{2,1,0:T(8,128)(2,1)S(1)}, bf16[2,96,2560]{2,1,0:T(8,128)(2,1)S(1)}, u32[]{:S(2)}, u32[]{:S(2)}) collective-permute-start(bf16[2,96,2560]{2,1,0:T(8,128)(2,1)S(1)} %project.3.other_ref), channel_id=1, source_target_pairs={{0,1},{1,0},{2,3},{3,2},{4,5},{5,4},{6,7},{7,6},{8,9},{9,8},{10,11... | collective-permute-start | bytes 2949128 | tf_op jit(solution)/shard_map/project/ppermute | solution.py:415

commit v5 on v4

--- a/solution.py
+++ b/solution.py
@@ -21,9 +21,8 @@
 HALF = D // 2
 
 W = THIRD
-SB = 8
-KR = SB * ROWS
-LONG, SHORT = (21, 3), (13, 2)
+KR = 768
+LONG, SHORT = (21, (8, 8, 5)), (13, (8, 5))
 RMAX = LONG[0] * 2 * THIRD
 
 neg_fill = -1e30
@@ -48,7 +47,8 @@
     return pltpu.CompilerParams(vmem_limit_bytes=mib * 2**20)
 
 
-def pack_kernel(q_hbm, k_hbm, v_hbm, qt_hbm, kt_hbm, vt_hbm, freq_ref, pos_ref, seg_ref, out_ref, tag_ref, held_ref, sem_in):
+def pack_kernel(side_ref, q_hbm, k_hbm, v_hbm, qt_hbm, kt_hbm, vt_hbm, freq_ref, pos_ref, seg_ref, out_ref, tag_ref, held_ref, sem_in):
+    del side_ref
     reads = [pltpu.make_async_copy(x, held_ref.at[i], sem_in.at[i]) for i, x in enumerate((q_hbm, k_hbm, v_hbm, qt_hbm, kt_hbm, vt_hbm))]
     for copy in reads:
         copy.start()
@@ -102,10 +102,14 @@
     return pltpu.with_memory_space_constraint(x, pltpu.HBM)
 
 
-def pack(arrays, freq, positions, segments):
+def in_vmem(x):
+    return pltpu.with_memory_space_constraint(x, pltpu.VMEM)
+
+
+def pack(side, arrays, freq, positions, segments):
     return pl.pallas_call(
         pack_kernel,
-        in_specs=[ANY] * 6 + [VMEM] * 3,
+        in_specs=[pl.BlockSpec(memory_space=pltpu.SMEM)] + [ANY] * 6 + [VMEM] * 3,
         out_specs=[VMEM, VMEM],
         out_shape=[pltpu.VMEM((CHIPS, MSG, HD), bf16), pltpu.VMEM((ROWS, HD), f32)],
         scratch_shapes=[
@@ -113,7 +117,7 @@
             pltpu.SemaphoreType.DMA((6,)),
         ],
         compiler_params=params(40),
-    )(*[in_hbm(x) for x in (*arrays, freq, positions, segments)])
+    )(side, *[in_hbm(x) for x in (*arrays, freq, positions, segments)])
 
 
 def bits(tiles):
@@ -132,7 +136,18 @@
     return scalar(has0), scalar(has1)
 
 
-def attn_kernel(qa_ref, qb_ref, kv_ref, oa_ref, ob_ref, s_ref, acc_ref, acct_ref, l_ref, pen_ref, keys_ref, kind_ref, chips_ref, cut_ref):
+def attn_kernel(qa_ref, qb_ref, kv_ref, *refs):
+    n = (len(refs) - 12) // 2
+    wanted_later, (oa_ref, ob_ref), fetched = refs[:n], refs[n : n + 2], refs[n + 2 : 2 * n + 2]
+    s_ref, acc_ref, acct_ref, l_ref, pen_ref, keys_ref, kind_ref, chips_ref, cut_ref, sem = refs[2 * n + 2 :]
+    copies = []
+    for src, dst in zip(wanted_later, fetched):
+        cuts = FETCHES if src.shape[0] % (16 * FETCHES) == 0 else 1
+        step = src.shape[0] // cuts
+        for i in range(cuts):
+            rows = slice(i * step, (i + 1) * step)
+            copies.append(pltpu.make_async_copy(src.at[rows], dst.at[rows], sem.at[len(copies)]))
+            copies[-1].start()
     own = bits([kv_ref[j, TAG:MSG, :] for j in range(CHIPS)])
     sib = bits([qb_ref[j, TAG - ASK : MSG - ASK, :] for j in range(CHIPS)])
     cut_ref[0] = i32(0)
@@ -176,25 +191,29 @@
         one = jnp.where(lax.broadcasted_iota(i32, (R, HD), 1) == 0, 1.0, 0.0).astype(bf16)
         q = jnp.concatenate([q, one], axis=1)
         m = jnp.full((R, HD), neg_fill, f32)
-        for b in range(blocks):
-            pairs = [(keys_ref[clip, b * SB + u], kind_ref[clip, b * SB + u]) for u in range(SB)]
-            k = jnp.concatenate([jnp.concatenate([kv_ref[j, K:KT, :], pen_ref[n]], axis=1) for j, n in pairs], axis=0)
-            s = lax.dot_general(q, k, NT, preferred_element_type=f32)
-            s_ref[b, 0:R] = s
-            for j in range(KR // HD):
+        places = [(b, range(sum(blocks[:b]), sum(blocks[: b + 1])), -(-n * ROWS // 256) * 256) for b, n in enumerate(blocks)]
+        for b, span, width in places:
+            gap = width - len(span) * ROWS
+            parts = [jnp.concatenate([kv_ref[keys_ref[clip, i], K:KT, :], pen_ref[kind_ref[clip, i]]], axis=1) for i in span]
+            parts += [jnp.concatenate([jnp.zeros((gap, HD), bf16), pen_ref[1, 0:gap, :]], axis=1)] * (gap > 0)
+            s = lax.dot_general(q, jnp.concatenate(parts, axis=0), NT, preferred_element_type=f32)
+            s_ref[b, 0:R, 0:width] = s
+            for j in range(width // HD):
                 m = jnp.maximum(m, s[:, j * HD : (j + 1) * HD])
         top = jnp.max(m, axis=1, keepdims=True)
-        for b in range(blocks):
-            js = [keys_ref[clip, b * SB + u] for u in range(SB)]
-            k, kt, v, vt = [jnp.concatenate([kv_ref[j, at : at + ROWS, :] for j in js], axis=0) for at in (K, KT, V, VT)]
+        for b, span, width in places:
+            gap = width - len(span) * ROWS
+            fill = [jnp.zeros((gap, HD), bf16)] * (gap > 0)
+            js = [keys_ref[clip, i] for i in span]
+            k, kt, v, vt = [jnp.concatenate([kv_ref[j, at : at + ROWS, :] for j in js] + fill, axis=0) for at in (K, KT, V, VT)]
             k = jnp.concatenate([k, kt], axis=1)
-            v1 = jnp.concatenate([v, jnp.ones((KR, HD), bf16)], axis=1)
+            v1 = jnp.concatenate([v, jnp.ones((width, HD), bf16)], axis=1)
             v = jnp.concatenate([v, vt], axis=1)
             st = lax.dot_general(qq, k, NT, preferred_element_type=f32)
-            p = jnp.exp2(s_ref[b, 0:R] - top)
+            p = jnp.exp2(s_ref[b, 0:R, 0:width] - top)
             pt = (p * st).astype(bf16)
             l = p[:, 0:HD]
-            for j in range(1, KR // HD):
+            for j in range(1, width // HD):
                 l = l + p[:, j * HD : (j + 1) * HD]
             acc = jnp.dot(p.astype(bf16), v, preferred_element_type=f32)
             acct = jnp.dot(pt, v1, preferred_element_type=f32)
@@ -229,17 +248,22 @@
                 for n, x in enumerate(whole):
                     old = out_ref[j, n * W : (n + 1) * W, :].astype(f32)
                     out_ref[j, n * W : (n + 1) * W, :] = jnp.where(hit, x[at : at + W].astype(f32), old).astype(bf16)
-
-
-def attend(asked, asked_there, arrived):
+    for copy in copies:
+        copy.wait()
+
+
+FETCHES = 2
+
+
+def attend(asked, asked_there, arrived, later):
     out = pltpu.VMEM((CHIPS, 3 * W, HD), bf16)
-    return pl.pallas_call(
+    outs = pl.pallas_call(
         attn_kernel,
-        in_specs=[VMEM] * 3,
-        out_specs=[VMEM] * 2,
-        out_shape=[out] * 2,
+        in_specs=[VMEM] * 3 + [ANY] * len(later),
+        out_specs=[VMEM] * (2 + len(later)),
+        out_shape=[out] * 2 + [pltpu.VMEM(x.shape, x.dtype) for x in later],
         scratch_shapes=[
-            pltpu.VMEM((LONG[1], RMAX, KR), f32),
+            pltpu.VMEM((len(LONG[1]), RMAX, KR), f32),
             pltpu.VMEM((RMAX, 256), f32),
             pltpu.VMEM((RMAX, 256), f32),
             pltpu.VMEM((RMAX, HD), f32),
@@ -248,20 +272,26 @@
             pltpu.SMEM((2, CHIPS), i32),
             pltpu.SMEM((2, CHIPS), i32),
             pltpu.SMEM((3,), i32),
+            pltpu.SemaphoreType.DMA((FETCHES * len(later),)),
         ],
-        compiler_params=params(40),
+        compiler_params=params(36),
         cost_estimate=pl.CostEstimate(flops=9 * 10**9, bytes_accessed=6 * 2**20, transcendentals=4 * 10**6),
-    )(*[pltpu.with_memory_space_constraint(x, pltpu.VMEM) for x in (asked, asked_there, arrived)])
+    )(*[in_vmem(x) for x in (asked, asked_there, arrived)], *[in_hbm(x) for x in later])
+    return outs[0], outs[1], outs[2:]
 
 
 def combine_kernel(a_ref, b_ref, out_ref):
     R = CHIPS * W
 
+    row = lax.broadcasted_iota(i32, (HD, 2 * HD), 0)
+    left = lax.broadcasted_iota(i32, (HD, 2 * HD), 1) < HD
+    begin = jnp.where(left, 0, 3)
+    select = jnp.where((row >= begin) & (row < begin + 3), 1.0, 0.0).astype(bf16)
+
     def read(ref):
-        o, t, s = [ref[:, n * W : (n + 1) * W, :].astype(f32).reshape(R, HD) for n in range(3)]
-        lse = s[:, 0:1] + s[:, 1:2] + s[:, 2:3]
-        drift = s[:, 3:4] + s[:, 4:5] + s[:, 5:6]
-        return o, t, lse, drift
+        o, t = [ref[:, n * W : (n + 1) * W, :].astype(f32).reshape(R, HD) for n in range(2)]
+        s = jnp.dot(ref[:, 2 * W : 3 * W, :].reshape(R, HD), select, preferred_element_type=f32)
+        return o, t, s[:, 0:HD], s[:, HD : 2 * HD]
 
     oa, ta, la, da = read(a_ref)
     ob, tb, lb, db = read(b_ref)
@@ -284,21 +314,19 @@
     )(a, b)
 
 
-CT = 512
-STEPS = HALF // CT
-
-
-def project_kernel(side_ref, x_ref, w_hbm, seg_ref, gate_ref, gate_tan_ref, *refs, own):
+CT = 256
+SENDS = 2
+PIECE = HALF // SENDS
+STEPS = PIECE // CT
+
+
+def project_kernel(side_ref, x_ref, w_ref, seg_ref, gate_ref, gate_tan_ref, *refs, own, part):
     if own:
-        resid_ref, resid_tan_ref, send_ref, lhs_ref, held_ref, sem = refs
+        resid_ref, resid_tan_ref, send_ref, lhs_ref = refs
     else:
-        send_ref, lhs_ref, held_ref, sem = refs
-    start = side_ref[0] * HALF
-    reads = []
-    for j in range(STEPS):
-        cols = pl.ds(pl.multiple_of(start + j * CT, CT), CT)
-        reads.append(pltpu.make_async_copy(w_hbm.at[:, cols], held_ref.at[j], sem.at[j]))
-        reads[j].start()
+        send_ref, lhs_ref = refs
+    side = side_ref[0] if own else 1 - side_ref[0]
+    start = side * HALF + part * PIECE
     for h in range(NH):
         for t in range(PARTS):
             s = worker(h, t)
@@ -306,85 +334,92 @@
             lhs_ref[ROWS + t * W : ROWS + (t + 1) * W, h * HD : (h + 1) * HD] = x_ref[s, W : 2 * W, :]
     one = seg_ref[:, 0:1] == 1.0
     for j in range(STEPS):
-        reads[j].wait()
-        out = jnp.dot(lhs_ref[...], held_ref[j], preferred_element_type=f32)
         cols = pl.ds(pl.multiple_of(start + j * CT, CT), CT)
+        out = jnp.dot(lhs_ref[...], w_ref[:, cols], preferred_element_type=f32)
         here = slice(j * CT, (j + 1) * CT)
         gate = jnp.where(one, gate_ref[1:2, cols], gate_ref[0:1, cols])
         gate_tan = jnp.where(one, gate_tan_ref[1:2, cols], gate_tan_ref[0:1, cols])
         a = gate * out[0:ROWS]
         b = gate_tan * out[0:ROWS] + gate * out[ROWS : 2 * ROWS]
         if own:
-            a = a + resid_ref[:, here]
-            b = b + resid_tan_ref[:, here]
+            a = a + resid_ref[:, part * PIECE + j * CT : part * PIECE + (j + 1) * CT]
+            b = b + resid_tan_ref[:, part * PIECE + j * CT : part * PIECE + (j + 1) * CT]
         send_ref[0, :, here] = a.astype(bf16)
         send_ref[1, :, here] = b.astype(bf16)
 
 
-def project(side, x, w, seg, gate, gate_tan, resid):
+def project(side, x, w, seg, gate, gate_tan, resid, part):
     own = len(resid) > 0
     return pl.pallas_call(
-        lambda *refs: project_kernel(*refs, own=own),
-        in_specs=[pl.BlockSpec(memory_space=pltpu.SMEM), VMEM, ANY] + [VMEM] * (3 + len(resid)),
+        lambda *refs: project_kernel(*refs, own=own, part=part),
+        in_specs=[pl.BlockSpec(memory_space=pltpu.SMEM)] + [VMEM] * (5 + len(resid)),
         out_specs=VMEM,
-        out_shape=pltpu.VMEM((2, ROWS, HALF), bf16),
+        out_shape=pltpu.VMEM((2, ROWS, PIECE), bf16),
         scratch_shapes=[
             pltpu.VMEM((2 * ROWS, NH * HD), bf16),
-            pltpu.VMEM((STEPS, NH * HD, CT), bf16),
-            pltpu.SemaphoreType.DMA((STEPS,)),
         ],
-        compiler_params=params(48),
+        compiler_params=params(16),
         cost_estimate=pl.CostEstimate(flops=2 * 2 * ROWS * NH * HD * HALF, bytes_accessed=10 * 2**20, transcendentals=0),
-    )(side, x, in_hbm(w), seg, gate, gate_tan, *resid)
+    )(side, *[in_vmem(x) for x in (x, w, seg, gate, gate_tan, *resid)])
 
 
 FT = 32
 
 
-def norm_kernel(
-    side_ref, mine_ref, got_mine_ref, other_ref, got_other_ref, seg_ref, scale_ref, scale_tan_ref, shift_ref, shift_tan_ref,
-    resid_ref, resid_tan_ref, ffn_ref, ffn_tan_ref,
-):
-    a = [mine_ref[0].astype(f32) + got_mine_ref[0].astype(f32), other_ref[0].astype(f32) + got_other_ref[0].astype(f32)]
-    b = [mine_ref[1].astype(f32) + got_mine_ref[1].astype(f32), other_ref[1].astype(f32) + got_other_ref[1].astype(f32)]
-    resid_ref[...] = a[0]
-    resid_tan_ref[...] = b[0]
-
-    def average(x, y):
-        return jnp.sum(x + y, axis=1, keepdims=True) / D
-
-    mean, mean_tan = average(*a), average(*b)
-    rstd = lax.rsqrt(average(a[0] * a[0], a[1] * a[1]) - mean * mean + norm_eps)
-    cov = average(a[0] * b[0], a[1] * b[1]) - mean * mean_tan
-    slope = rstd * rstd * rstd * cov
-    one = seg_ref[:, 0:1] == 1.0
-    for i, side in enumerate((side_ref[0], 1 - side_ref[0])):
-        cols = pl.ds(pl.multiple_of(side * HALF, HALF), HALF)
-
-        def pick(ref):
-            return jnp.where(one, ref[1:2, cols], ref[0:1, cols])
-
-        centered = a[i] - mean
-        normed = centered * rstd
-        normed_tan = (b[i] - mean_tan) * rstd - centered * slope
-        scale = 1.0 + pick(scale_ref)
-        ffn_ref[:, cols] = (normed * scale + pick(shift_ref)).astype(bf16)
-        ffn_tan_ref[:, cols] = (normed_tan * scale + normed * pick(scale_tan_ref) + pick(shift_tan_ref)).astype(bf16)
+def norm_kernel(side_ref, *refs):
+    rows = [refs[i * SENDS : (i + 1) * SENDS] for i in range(4)]
+    seg_ref, scale_ref, scale_tan_ref, shift_ref, shift_tan_ref = refs[4 * SENDS : 4 * SENDS + 5]
+    outs, held, sem = refs[4 * SENDS + 5 : 4 * SENDS + 9], refs[4 * SENDS + 9 : 4 * SENDS + 13], refs[-1]
+    resid_ref, resid_tan_ref, ffn_ref, ffn_tan_ref = held
+    copies = []
+    for step in range(ROWS // FT):
+        at = slice(step * FT, (step + 1) * FT)
+
+        def whole(kept, got, i):
+            return jnp.concatenate([x[i, at].astype(f32) + y[i, at].astype(f32) for x, y in zip(kept, got)], axis=1)
+
+        a = [whole(rows[0], rows[1], 0), whole(rows[2], rows[3], 0)]
+        b = [whole(rows[0], rows[1], 1), whole(rows[2], rows[3], 1)]
+        resid_ref[at] = a[0]
+        resid_tan_ref[at] = b[0]
+
+        def average(x, y):
+            return jnp.sum(x + y, axis=1, keepdims=True) / D
+
+        mean, mean_tan = average(*a), average(*b)
+        rstd = lax.rsqrt(average(a[0] * a[0], a[1] * a[1]) - mean * mean + norm_eps)
+        cov = average(a[0] * b[0], a[1] * b[1]) - mean * mean_tan
+        slope = rstd * rstd * rstd * cov
+        one = seg_ref[at, 0:1] == 1.0
+        for i, side in enumerate((side_ref[0], 1 - side_ref[0])):
+            cols = pl.ds(pl.multiple_of(side * HALF, HALF), HALF)
+
+            def pick(ref):
+                return jnp.where(one, ref[1:2, cols], ref[0:1, cols])
+
+            centered = a[i] - mean
+            normed = centered * rstd
+            normed_tan = (b[i] - mean_tan) * rstd - centered * slope
+            scale = 1.0 + pick(scale_ref)
+            ffn_ref[at, cols] = (normed * scale + pick(shift_ref)).astype(bf16)
+            ffn_tan_ref[at, cols] = (normed_tan * scale + normed * pick(scale_tan_ref) + pick(shift_tan_ref)).astype(bf16)
+        for i in range(4):
+            copies.append(pltpu.make_async_copy(held[i].at[at], outs[i].at[at], sem.at[step, i]))
+            copies[-1].start()
+    for copy in copies:
+        copy.wait()
 
 
 def norm(side, mine, got_mine, other, got_other, seg, tables):
-    pair = pl.BlockSpec((2, FT, HALF), lambda j: (0, j, 0))
-    half = pl.BlockSpec((FT, HALF), lambda j: (j, 0))
-    full = pl.BlockSpec((FT, D), lambda j: (j, 0))
+    outs = [jax.ShapeDtypeStruct((ROWS, HALF), f32)] * 2 + [jax.ShapeDtypeStruct((ROWS, D), bf16)] * 2
     return pl.pallas_call(
         norm_kernel,
-        grid=(ROWS // FT,),
-        in_specs=[pl.BlockSpec(memory_space=pltpu.SMEM)] + [pair] * 4 + [pl.BlockSpec((FT, HD), lambda j: (j, 0))]
-        + [pl.BlockSpec((2, D), lambda j: (0, 0))] * 4,
-        out_specs=[half, half, full, full],
-        out_shape=[jax.ShapeDtypeStruct((ROWS, HALF), f32)] * 2 + [jax.ShapeDtypeStruct((ROWS, D), bf16)] * 2,
-        compiler_params=params(40),
-    )(side, mine, got_mine, other, got_other, seg, *tables)
+        in_specs=[pl.BlockSpec(memory_space=pltpu.SMEM)] + [VMEM] * (4 * SENDS + 5),
+        out_specs=[ANY] * 4,
+        out_shape=outs,
+        scratch_shapes=[pltpu.VMEM(x.shape, x.dtype) for x in outs] + [pltpu.SemaphoreType.DMA((ROWS // FT, 4))],
+        compiler_params=params(32),
+    )(side, *[in_vmem(x) for x in (*mine, *got_mine, *other, *got_other, seg, *tables)])
 
 
 def body(
@@ -395,28 +430,34 @@
     freq = np.concatenate([frequency, frequency])[None, :].astype(np.float32)
     swap = [(0, 1), (1, 0)]
 
+    side = lax.axis_index("head").astype(i32).reshape(1)
     with jax.named_scope("pack"):
         arrays = (queries, keys, values, queries_tan, keys_tan, values_tan)
-        message, seg = pack(arrays, freq, positions[None, :], segments[None, :])
+        message, seg = pack(side, arrays, freq, positions[None, :], segments[None, :])
     with jax.named_scope("spread"):
         arrived = lax.all_to_all(message, ("z", "y", "x"), 0, 0, tiled=True)
         asked = lax.slice_in_dim(arrived, ASK, MSG, axis=1)
         asked_there = lax.ppermute(asked, "c", swap)
 
-    side = lax.axis_index("head").astype(i32).reshape(1)
     with jax.named_scope("attend"):
-        part, there = attend(asked, asked_there, arrived)
+        later = (out_weight, gate, gate_tan, residual, residual_tan, mod_scale, mod_scale_tan, mod_shift, mod_shift_tan)
+        part, there, later = attend(asked, asked_there, arrived, later)
+        held_weight, held_gate, held_gate_tan, held_resid, held_resid_tan, *tables = later
         back = lax.ppermute(there, "c", swap)
         answer = combine(part, back)
     with jax.named_scope("collect"):
         attended = lax.all_to_all(answer, ("z", "y", "x"), 0, 0, tiled=True)
     with jax.named_scope("project"):
-        other = project(1 - side, attended, out_weight, seg, gate, gate_tan, ())
-        got_mine = lax.ppermute(other, "head", swap)
-        mine = project(side, attended, out_weight, seg, gate, gate_tan, (residual, residual_tan))
-        got_other = lax.ppermute(mine, "head", swap)
+        args = (attended, held_weight, seg, held_gate, held_gate_tan)
+        other, got_mine, mine, got_other = [], [], [], []
+        for part in range(SENDS):
+            other.append(project(side, *args, (), part))
+            got_mine.append(lax.ppermute(other[part], "head", swap))
+        for part in range(SENDS):
+            mine.append(project(side, *args, (held_resid, held_resid_tan), part))
+            got_other.append(lax.ppermute(mine[part], "head", swap))
     with jax.named_scope("norm"):
-        return tuple(norm(side, mine, got_mine, other, got_other, seg, (mod_scale, mod_scale_tan, mod_shift, mod_shift_tan)))
+        return tuple(norm(side, mine, got_mine, other, got_other, seg, tables))
 
 
 def solution(mesh):

time: 152 us -> 146 us (0.961)
  blocking collectives: 59.5 us -> 77 us
  waiting for transfers between devices: 56.7 us -> 40.6 us
  Pallas kernels: 28.6 us -> 22.5 us
  starting transfers between devices: 6.55 us -> 4.67 us
    all_to_all x0 -> x1, blocking collectives: none -> 17.5 us  [body(): attended = lax.all_to_all(answer, ('z', 'y', 'x'), 0, 0, tiled=True)]
    all_to_all x1 -> x0, waiting for transfers between devices: 14.3 us -> none  [body(): attended = lax.all_to_all(answer, ('z', 'y', 'x'), 0, 0, tiled=True)]
    pallas_call x5 -> x7, Pallas kernels: 26.8 us -> 21.9 us  [the longest x1 11.3 us: attend(): pl.pallas_call(attn_kernel, in_specs=[VMEM] * 3 + [ANY] * len(later), out...]
    all_to_all x1 -> x0, starting transfers between devices: 3.89 us -> none  [body(): attended = lax.all_to_all(answer, ('z', 'y', 'x'), 0, 0, tiled=True)]
    ppermute x2 -> x4, starting transfers between devices: 2.18 us -> 4.38 us  [the longest x2 2.2 us: body(): got_other.append(lax.ppermute(mine[part], 'head', swap))]
    ppermute x2 -> x4, waiting for transfers between devices: 38.1 us -> 36.4 us  [the longest x2 18.7 us: body(): got_mine.append(lax.ppermute(other[part], 'head', swap))]
  transfers between devices with their start and end apart: 5 -> 6, of which waited for: 5 -> 6; matrix products, arithmetic and copies ran while one was open for 0% -> 0% of each run, Pallas kernels for 2% -> 2%
where the time goes in v5:
time: 146 us
  blocking collectives  77 us (53%)
  waiting for transfers between devices  40.6 us (28%)
  Pallas kernels  22.5 us (15%)
  starting transfers between devices  4.67 us (3%)
    all_to_all x1, blocking collectives, body(): arrived = lax.all_to_all(message, ('z', 'y', 'x'), 0, 0, tiled=True)  59.5 us
    ppermute x2, waiting for transfers between devices, body(): got_mine.append(lax.ppermute(other[part], 'head', swap))  18.7 us
    ppermute x2, waiting for transfers between devices, body(): got_other.append(lax.ppermute(mine[part], 'head', swap))  17.7 us
    all_to_all x1, blocking collectives, body(): attended = lax.all_to_all(answer, ('z', 'y', 'x'), 0, 0, tiled=True)  17.5 us
    pallas_call x1, Pallas kernels, attend(): pl.pallas_call(attn_kernel, in_specs=[VMEM] * 3 + [ANY] * len(later), out...  11.3 us
    pallas_call x1, Pallas kernels, norm(): pl.pallas_call(norm_kernel, in_specs=[pl.BlockSpec(memory_space=pltpu.SME...  4.07 us
    pallas_call x4, Pallas kernels, project(): pl.pallas_call(lambda *refs: project_kernel(*refs, own=own, part=part), i...  3.6 us
  transfers between devices with their start and end apart: 6, of which 6 were waited for; matrix products, arithmetic and copies ran while one was open for 0% of the time, Pallas kernels for 2%

profile of v5, /device:TPU:0, one launch (start us, length us, event | category | flops | bytes accessed | tf_op | source)
XLA Modules:
  0.0 145.8 jit_solution(18223327900846216961)
XLA Ops:
  0.6 2.9 %pack.1 = (bf16[32,464,128]{2,1,0:T(8,128)(2,1)S(1)}, f32[96,128]{1,0:T(8,128)S(1)}) custom-call(s32[1]{0:T(128)} %bitcast.side_ref.refs_0_, bf16[96,1280]{1,0:T(8,128)(2,1)} %q_hbm.1, bf16[96,1280]{1,0:T(8,128)(2,1)} %k_hbm.1, bf16[96,1280]{1,0:T(8,128)(2,1)} %v_hbm.1, bf16[96,1280]{1,0:T(8,128)(2,1)} %qt_hbm.1, bf16[96,1280]{1,0:T(8,128)(2,1)} %kt_hbm.1, ...), custom_call_target="tpu_custom_call" | custom-call | tf_op jit(solution)/shard_map/pack/pallas_call | solution.py:110
  3.5 59.5 %all_to_all.10.kv_ref = bf16[32,464,128]{2,1,0:T(8,128)(2,1)S(1)} all-to-all(bf16[32,464,128]{2,1,0:T(8,128)(2,1)S(1)} %get-tuple-element.17), channel_id=1, replica_groups=mesh['z'=4,'y'=4,'x'=2,'c'=2,'head'=2] {'z','y','x'}, dimensions={0} | all-to-all | bytes 7602176 | tf_op jit(solution)/shard_map/spread/all_to_all | solution.py:438
  63.1 0.1 collective-permute-start
  63.2 2.1 %collective-permute-done.qb_ref = bf16[32,80,128]{2,1,0:T(8,128)(2,1)S(1)} collective-permute-done((bf16[32,80,128]{2,1,0:T(8,128)(2,1)S(1)}, bf16[32,80,128]{2,1,0:T(8,128)(2,1)S(1)}, u32[]{:S(2)}, u32[]{:S(2)}) %collective-permute-start) | collective-permute-done | bytes 655392 | tf_op jit(solution)/shard_map/spread/ppermute | solution.py:440
  65.3 11.3 %attend.2 = (bf16[32,96,128]{2,1,0:T(8,128)(2,1)S(1)}, bf16[32,96,128]{2,1,0:T(8,128)(2,1)S(1)}, bf16[1280,5120]{1,0:T(8,128)(2,1)S(1)}, f32[2,5120]{1,0:T(2,128...) custom-call(bf16[32,80,128]{2,1,0:T(8,128)(2,1)S(1)} %slice.4.qa_ref, ...), custom_call_target="tpu_custom_call" | custom-call | flops 8999999488 | bytes 6291456 | tf_op jit(solution)/shard_map/attend/pallas_call | solution.py:260
  76.6 0.2 collective-permute-start.1
  76.8 2.2 %collective-permute-done.1.b_ref = bf16[32,96,128]{2,1,0:T(8,128)(2,1)S(1)} collective-permute-done((bf16[32,96,128]{2,1,0:T(8,128)(2,1)S(1)}, bf16[32,96,128]{2,1,0:T(8,128)(2,1)S(1)}, u32[]{:S(2)}, u32[]{:S(2)}) %collective-permute-start.1) | collective-permute-done | bytes 786464 | tf_op jit(solution)/shard_map/attend/ppermute | solution.py:446
  79.0 0.6 attend.3
  79.6 17.5 %all_to_all.11.refs_1_ = bf16[32,64,128]{2,1,0:T(8,128)(2,1)S(1)} all-to-all(bf16[32,64,128]{2,1,0:T(8,128)(2,1)S(1)} %attend.3), channel_id=1, replica_groups=mesh['z'=4,'y'=4,'x'=2,'c'=2,'head'=2] {'z','y','x'}, dimensions={0} | all-to-all | bytes 1048576 | tf_op jit(solution)/shard_map/collect/all_to_all | solution.py:449
  97.1 0.9 project.4.refs_0_
  98.0 0.7 collective-permute-start.4
  98.8 0.9 project.5.refs_1_
  99.7 1.5 %collective-permute-start.5 = (bf16[2,96,1280]{2,1,0:T(8,128)(2,1)S(1)}, bf16[2,96,1280]{2,1,0:T(8,128)(2,1)S(1)}, u32[]{:S(2)}, u32[]{:S(2)}) collective-permute-start(bf16[2,96,1280]{2,1,0:T(8,128)(2,1)S(1)} %project.5.refs_1_), channel_id=1, source_target_pairs={{0,1},{1,0},{2,3},{3,2},{4,5},{5,4},{6,7},{7,6},{8,9},{9,8},{10,11... | collective-permute-start | bytes 1474568 | tf_op jit(solution)/shard_map/project/ppermute | solution.py:458
  101.1 0.9 project.6.refs_4_
  102.0 0.7 collective-permute-start.2
  102.8 0.9 project.7.refs_5_
  103.7 1.5 %collective-permute-start.3 = (bf16[2,96,1280]{2,1,0:T(8,128)(2,1)S(1)}, bf16[2,96,1280]{2,1,0:T(8,128)(2,1)S(1)}, u32[]{:S(2)}, u32[]{:S(2)}) collective-permute-start(bf16[2,96,1280]{2,1,0:T(8,128)(2,1)S(1)} %project.7.refs_5_), channel_id=1, source_target_pairs={{0,1},{1,0},{2,3},{3,2},{4,5},{5,4},{6,7},{7,6},{8,9},{9,8},{10,11... | collective-permute-start | bytes 1474568 | tf_op jit(solution)/shard_map/project/ppermute | solution.py:455
  105.1 7.1 %collective-permute-done.4.refs_6_ = bf16[2,96,1280]{2,1,0:T(8,128)(2,1)S(1)} collective-permute-done((bf16[2,96,1280]{2,1,0:T(8,128)(2,1)S(1)}, bf16[2,96,1280]{2,1,0:T(8,128)(2,1)S(1)}, u32[]{:S(2)}, u32[]{:S(2)}) %collective-permute-start.4) | collective-permute-done | bytes 491552 | tf_op jit(solution)/shard_map/project/ppermute | solution.py:458
  112.3 10.5 %collective-permute-done.5.refs_7_ = bf16[2,96,1280]{2,1,0:T(8,128)(2,1)S(1)} collective-permute-done((bf16[2,96,1280]{2,1,0:T(8,128)(2,1)S(1)}, bf16[2,96,1280]{2,1,0:T(8,128)(2,1)S(1)}, u32[]{:S(2)}, u32[]{:S(2)}) %collective-permute-start.5) | collective-permute-done | bytes 491552 | tf_op jit(solution)/shard_map/project/ppermute | solution.py:458
  122.8 10.5 %collective-permute-done.2.refs_2_ = bf16[2,96,1280]{2,1,0:T(8,128)(2,1)S(1)} collective-permute-done((bf16[2,96,1280]{2,1,0:T(8,128)(2,1)S(1)}, bf16[2,96,1280]{2,1,0:T(8,128)(2,1)S(1)}, u32[]{:S(2)}, u32[]{:S(2)}) %collective-permute-start.2) | collective-permute-done | bytes 491552 | tf_op jit(solution)/shard_map/project/ppermute | solution.py:455
  133.3 8.2 %collective-permute-done.3.refs_3_ = bf16[2,96,1280]{2,1,0:T(8,128)(2,1)S(1)} collective-permute-done((bf16[2,96,1280]{2,1,0:T(8,128)(2,1)S(1)}, bf16[2,96,1280]{2,1,0:T(8,128)(2,1)S(1)}, u32[]{:S(2)}, u32[]{:S(2)}) %collective-permute-start.3) | collective-permute-done | bytes 491552 | tf_op jit(solution)/shard_map/project/ppermute | solution.py:455
  141.5 4.1 %norm.1 = (f32[96,2560]{1,0:T(8,128)}, f32[96,2560]{1,0:T(8,128)}, bf16[96,5120]{1,0:T(8,128)(2,1)}, bf16[96,5120]{1,0:T(8,128)(2,1)}) custom-call(s32[1]{0:T(128)} %bitcast.side_ref.refs_0_, bf16[2,96,1280]{2,1,0:T(8,128)(2,1)S(1)} %project.4.refs_0_, bf16[2,96,1280]{2,1,0:T(8,128)(2,1)S(1)} %project.5.refs_1_, ...), custom_call_target="tpu_custom_call" | custom-call | tf_op jit(solution)/shard_map/norm/pallas_call | solution.py:415
  (1 shorter events, 0.0 us)
Async XLA Ops:
  63.1 2.2 %collective-permute-start = (bf16[32,80,128]{2,1,0:T(8,128)(2,1)S(1)}, bf16[32,80,128]{2,1,0:T(8,128)(2,1)S(1)}, u32[]{:S(2)}, u32[]{:S(2)}) collective-permute-start(bf16[32,80,128]{2,1,0:T(8,128)(2,1)S(1)} %slice.4.qa_ref), channel_id=1, source_target_pairs={{0,2},{2,0},{1,3},{3,1},{4,6},{6,4},{5,7},{7,5},{8,10},{10,8},{9,1... | collective-permute-start | bytes 1966088 | tf_op jit(solution)/shard_map/spread/ppermute | solution.py:440
  76.6 2.4 %collective-permute-start.1 = (bf16[32,96,128]{2,1,0:T(8,128)(2,1)S(1)}, bf16[32,96,128]{2,1,0:T(8,128)(2,1)S(1)}, u32[]{:S(2)}, u32[]{:S(2)}) collective-permute-start(bf16[32,96,128]{2,1,0:T(8,128)(2,1)S(1)} %get-tuple-element.19), channel_id=1, source_target_pairs={{0,2},{2,0},{1,3},{3,1},{4,6},{6,4},{5,7},{7,5},{8,10},{10,8},{9,1... | collective-permute-start | bytes 2359304 | tf_op jit(solution)/shard_map/attend/ppermute | solution.py:446
  98.0 14.2 %collective-permute-start.4 = (bf16[2,96,1280]{2,1,0:T(8,128)(2,1)S(1)}, bf16[2,96,1280]{2,1,0:T(8,128)(2,1)S(1)}, u32[]{:S(2)}, u32[]{:S(2)}) collective-permute-start(bf16[2,96,1280]{2,1,0:T(8,128)(2,1)S(1)} %project.4.refs_0_), channel_id=1, source_target_pairs={{0,1},{1,0},{2,3},{3,2},{4,5},{5,4},{6,7},{7,6},{8,9},{9,8},{10,11... | collective-permute-start | bytes 1474568 | tf_op jit(solution)/shard_map/project/ppermute | solution.py:458
  99.7 23.1 %collective-permute-start.5 = (bf16[2,96,1280]{2,1,0:T(8,128)(2,1)S(1)}, bf16[2,96,1280]{2,1,0:T(8,128)(2,1)S(1)}, u32[]{:S(2)}, u32[]{:S(2)}) collective-permute-start(bf16[2,96,1280]{2,1,0:T(8,128)(2,1)S(1)} %project.5.refs_1_), channel_id=1, source_target_pairs={{0,1},{1,0},{2,3},{3,2},{4,5},{5,4},{6,7},{7,6},{8,9},{9,8},{10,11... | collective-permute-start | bytes 1474568 | tf_op jit(solution)/shard_map/project/ppermute | solution.py:458
  102.0 31.3 %collective-permute-start.2 = (bf16[2,96,1280]{2,1,0:T(8,128)(2,1)S(1)}, bf16[2,96,1280]{2,1,0:T(8,128)(2,1)S(1)}, u32[]{:S(2)}, u32[]{:S(2)}) collective-permute-start(bf16[2,96,1280]{2,1,0:T(8,128)(2,1)S(1)} %project.6.refs_4_), channel_id=1, source_target_pairs={{0,1},{1,0},{2,3},{3,2},{4,5},{5,4},{6,7},{7,6},{8,9},{9,8},{10,11... | collective-permute-start | bytes 1474568 | tf_op jit(solution)/shard_map/project/ppermute | solution.py:455
  103.7 37.9 %collective-permute-start.3 = (bf16[2,96,1280]{2,1,0:T(8,128)(2,1)S(1)}, bf16[2,96,1280]{2,1,0:T(8,128)(2,1)S(1)}, u32[]{:S(2)}, u32[]{:S(2)}) collective-permute-start(bf16[2,96,1280]{2,1,0:T(8,128)(2,1)S(1)} %project.7.refs_5_), channel_id=1, source_target_pairs={{0,1},{1,0},{2,3},{3,2},{4,5},{5,4},{6,7},{7,6},{8,9},{9,8},{10,11... | collective-permute-start | bytes 1474568 | tf_op jit(solution)/shard_map/project/ppermute | solution.py:455

commit v6 on v5

--- a/solution.py
+++ b/solution.py
@@ -17,13 +17,13 @@
 PARTS = 3
 SPAN = 5
 K, KT, V, VT, QT, Q, TAG, MSG = 0, 96, 192, 288, 384, 416, 448, 464
-ASK = QT
 HALF = D // 2
 
 W = THIRD
 KR = 768
 LONG, SHORT = (21, (8, 8, 5)), (13, (8, 5))
-RMAX = LONG[0] * 2 * THIRD
+RLONG, RSHORT = LONG[0] * THIRD, SHORT[0] * THIRD
+RALL = RLONG + RSHORT
 
 neg_fill = -1e30
 norm_eps = 1e-06
@@ -136,26 +136,30 @@
     return scalar(has0), scalar(has1)
 
 
-def attn_kernel(qa_ref, qb_ref, kv_ref, *refs):
-    n = (len(refs) - 12) // 2
-    wanted_later, (oa_ref, ob_ref), fetched = refs[:n], refs[n : n + 2], refs[n + 2 : 2 * n + 2]
-    s_ref, acc_ref, acct_ref, l_ref, pen_ref, keys_ref, kind_ref, chips_ref, cut_ref, sem = refs[2 * n + 2 :]
+def attn_kernel(q_ref, kv_ref, *refs, second):
+    s_ref, pen_ref, keys_ref, kind_ref, chips_ref, cut_ref = refs[-6:]
     copies = []
-    for src, dst in zip(wanted_later, fetched):
-        cuts = FETCHES if src.shape[0] % (16 * FETCHES) == 0 else 1
-        step = src.shape[0] // cuts
-        for i in range(cuts):
-            rows = slice(i * step, (i + 1) * step)
-            copies.append(pltpu.make_async_copy(src.at[rows], dst.at[rows], sem.at[len(copies)]))
-            copies[-1].start()
-    own = bits([kv_ref[j, TAG:MSG, :] for j in range(CHIPS)])
-    sib = bits([qb_ref[j, TAG - ASK : MSG - ASK, :] for j in range(CHIPS)])
+    if second:
+        old_ref, old_stat_ref, out_ref, acc_ref, stat_ref = refs[:-6]
+    else:
+        n = (len(refs) - 9) // 2
+        acc_ref, stat_ref = refs[n : n + 2]
+        sem = refs[-7]
+        for src, dst in zip(refs[:n], refs[n + 2 : 2 * n + 2]):
+            cuts = FETCHES if src.shape[0] % (16 * FETCHES) == 0 else 1
+            step = src.shape[0] // cuts
+            for i in range(cuts):
+                rows = slice(i * step, (i + 1) * step)
+                copies.append(pltpu.make_async_copy(src.at[rows], dst.at[rows], sem.at[len(copies)]))
+                copies[-1].start()
+    asks = bits([q_ref[j, TAG:MSG, :] for j in range(CHIPS)])
+    holds = bits([kv_ref[j, TAG:MSG, :] for j in range(CHIPS)]) if second else asks
     cut_ref[0] = i32(0)
     cut_ref[1] = i32(0)
 
     def sort(j, carry):
         cuts, counts = carry[0], list(carry[1:])
-        has = [(own[c] >> j) & 1 for c in range(2)]
+        has = [(holds[c] >> j) & 1 for c in range(2)]
         both = has[0] & has[1]
         cut_ref[jnp.where(both == 1, jnp.minimum(cuts, 1), 2)] = j
         for c in range(2):
@@ -163,10 +167,10 @@
             keys_ref[c, at] = j
             kind_ref[c, at] = jnp.where(both == 1, 2 + 2 * c + jnp.minimum(cuts, 1), 1 - has[c])
             counts[c] = counts[c] + has[c]
-            any_has = ((own[c] | sib[c]) >> j) & 1
+            ask = (asks[c] >> j) & 1
             n = counts[2 + c]
-            chips_ref[c, jnp.where(any_has == 1, n, 31 - (j - n))] = j
-            counts[2 + c] = n + any_has
+            chips_ref[c, jnp.where(ask == 1, n, 31 - (j - n))] = j
+            counts[2 + c] = n + ask
         return (cuts + both, *counts)
 
     zero = i32(0)
@@ -183,14 +187,15 @@
         pen_ref[2 + p] = jnp.where(lane == 0, col * neg_fill, 0.0).astype(bf16)
         pen_ref[4 + p] = jnp.where(lane == 0, (1.0 - col) * neg_fill, 0.0).astype(bf16)
 
-    for (chips, blocks), clip in ((LONG, long_clip), (SHORT, 1 - long_clip)):
-        R = chips * 2 * THIRD
+    for (chips, blocks), clip, base in ((LONG, long_clip, 0), (SHORT, 1 - long_clip, RLONG)):
+        R = chips * THIRD
+        here = slice(base, base + R)
         listed = [chips_ref[clip, i] for i in range(chips)]
-        qt, q = [jnp.concatenate([ref[j, at - ASK : at - ASK + THIRD, :] for j in listed for ref in (qa_ref, qb_ref)], axis=0) for at in (QT, Q)]
+        qt, q = [jnp.concatenate([q_ref[j, at : at + THIRD, :] for j in listed], axis=0) for at in (QT, Q)]
         qq = jnp.concatenate([qt, q], axis=1)
         one = jnp.where(lax.broadcasted_iota(i32, (R, HD), 1) == 0, 1.0, 0.0).astype(bf16)
         q = jnp.concatenate([q, one], axis=1)
-        m = jnp.full((R, HD), neg_fill, f32)
+        m = old_stat_ref[here, 0:HD] if second else jnp.full((R, HD), neg_fill, f32)
         places = [(b, range(sum(blocks[:b]), sum(blocks[: b + 1])), -(-n * ROWS // 256) * 256) for b, n in enumerate(blocks)]
         for b, span, width in places:
             gap = width - len(span) * ROWS
@@ -201,6 +206,7 @@
             for j in range(width // HD):
                 m = jnp.maximum(m, s[:, j * HD : (j + 1) * HD])
         top = jnp.max(m, axis=1, keepdims=True)
+        m_old = old_stat_ref[here, 0:1] if second else None
         for b, span, width in places:
             gap = width - len(span) * ROWS
             fill = [jnp.zeros((gap, HD), bf16)] * (gap > 0)
@@ -217,37 +223,32 @@
                 l = l + p[:, j * HD : (j + 1) * HD]
             acc = jnp.dot(p.astype(bf16), v, preferred_element_type=f32)
             acct = jnp.dot(pt, v1, preferred_element_type=f32)
-            if b == 0:
-                l_ref[0:R], acc_ref[0:R], acct_ref[0:R] = l, acc, acct
-            else:
-                l_ref[0:R] += l
-                acc_ref[0:R] += acc
-                acct_ref[0:R] += acct
-        total = jnp.sum(l_ref[0:R], axis=1, keepdims=True)
+            if b > 0 or second:
+                fade = jnp.exp2(m_old - top) if b == 0 else None
+                l += stat_ref[here, HD:] if b > 0 else old_stat_ref[here, HD:] * fade
+                acc += acc_ref[here, 0:256] if b > 0 else old_ref[here, 0:256] * fade
+                acct += acc_ref[here, 256:512] if b > 0 else old_ref[here, 256:512] * fade
+            stat_ref[here, HD:] = l
+            acc_ref[here, 0:256] = acc
+            acc_ref[here, 256:512] = acct
+        if not second:
+            stat_ref[here, 0:HD] = jnp.broadcast_to(top, (R, HD))
+            continue
+        total = jnp.sum(stat_ref[here, HD:], axis=1, keepdims=True)
         inv = 1.0 / total
         inv_tan = inv * ln2
-        drift = acct_ref[0:R, 128:256] * inv_tan
-        o = acc_ref[0:R, 0:128] * inv
-        t = acct_ref[0:R, 0:128] * inv_tan + acc_ref[0:R, 128:256] * inv - drift * o
-        lse = jnp.broadcast_to(top + jnp.log2(total), (R, HD))
-        where = lax.broadcasted_iota(i32, (R, HD), 1)
-        pieces = jnp.zeros((R, HD), f32)
-        for first, x in ((0, lse), (3, drift)):
-            for i in range(3):
-                piece = x.astype(bf16).astype(f32)
-                pieces = jnp.where(where == first + i, piece, pieces)
-                x = x - piece
-        whole = [x.astype(bf16) for x in (o, t, pieces)]
+        drift = acc_ref[here, 384:512] * inv_tan
+        o = acc_ref[here, 0:128] * inv
+        t = acc_ref[here, 256:384] * inv_tan + acc_ref[here, 128:256] * inv - drift * o
         wanted = clip.astype(f32)
         for i, j in enumerate(listed):
-            for core, (q_ref, out_ref) in enumerate(((qa_ref, oa_ref), (qb_ref, ob_ref))):
-                at = (2 * i + core) * W
-                tags = q_ref[j, TAG - ASK : MSG - ASK, :].astype(f32)
-                tag = jnp.concatenate([tags[:, 0:1], tags[:, 1:2]], axis=0)
-                hit = jnp.broadcast_to(tag, (W, HD)) == wanted
-                for n, x in enumerate(whole):
-                    old = out_ref[j, n * W : (n + 1) * W, :].astype(f32)
-                    out_ref[j, n * W : (n + 1) * W, :] = jnp.where(hit, x[at : at + W].astype(f32), old).astype(bf16)
+            at = i * W
+            tags = q_ref[j, TAG:MSG, :].astype(f32)
+            tag = jnp.concatenate([tags[:, 0:1], tags[:, 1:2]], axis=0)
+            hit = jnp.broadcast_to(tag, (W, HD)) == wanted
+            for n, x in enumerate((o, t)):
+                old = out_ref[j, n * W : (n + 1) * W, :].astype(f32)
+                out_ref[j, n * W : (n + 1) * W, :] = jnp.where(hit, x[at : at + W], old).astype(bf16)
     for copy in copies:
         copy.wait()
 
@@ -255,63 +256,34 @@
 FETCHES = 2
 
 
-def attend(asked, asked_there, arrived, later):
-    out = pltpu.VMEM((CHIPS, 3 * W, HD), bf16)
+def scratch():
+    lists = [pltpu.SMEM((2, CHIPS), i32)] * 3 + [pltpu.SMEM((3,), i32)]
+    return [pltpu.VMEM((len(LONG[1]), RLONG, KR), f32), pltpu.VMEM((6, ROWS, HD), bf16)] + lists
+
+
+def attend(arrived, later):
     outs = pl.pallas_call(
-        attn_kernel,
-        in_specs=[VMEM] * 3 + [ANY] * len(later),
+        lambda *refs: attn_kernel(*refs, second=False),
+        in_specs=[VMEM] * 2 + [ANY] * len(later),
         out_specs=[VMEM] * (2 + len(later)),
-        out_shape=[out] * 2 + [pltpu.VMEM(x.shape, x.dtype) for x in later],
-        scratch_shapes=[
-            pltpu.VMEM((len(LONG[1]), RMAX, KR), f32),
-            pltpu.VMEM((RMAX, 256), f32),
-            pltpu.VMEM((RMAX, 256), f32),
-            pltpu.VMEM((RMAX, HD), f32),
-            pltpu.VMEM((6, ROWS, HD), bf16),
-            pltpu.SMEM((2, CHIPS), i32),
-            pltpu.SMEM((2, CHIPS), i32),
-            pltpu.SMEM((2, CHIPS), i32),
-            pltpu.SMEM((3,), i32),
-            pltpu.SemaphoreType.DMA((FETCHES * len(later),)),
-        ],
-        compiler_params=params(36),
-        cost_estimate=pl.CostEstimate(flops=9 * 10**9, bytes_accessed=6 * 2**20, transcendentals=4 * 10**6),
-    )(*[in_vmem(x) for x in (asked, asked_there, arrived)], *[in_hbm(x) for x in later])
-    return outs[0], outs[1], outs[2:]
-
-
-def combine_kernel(a_ref, b_ref, out_ref):
-    R = CHIPS * W
-
-    row = lax.broadcasted_iota(i32, (HD, 2 * HD), 0)
-    left = lax.broadcasted_iota(i32, (HD, 2 * HD), 1) < HD
-    begin = jnp.where(left, 0, 3)
-    select = jnp.where((row >= begin) & (row < begin + 3), 1.0, 0.0).astype(bf16)
-
-    def read(ref):
-        o, t = [ref[:, n * W : (n + 1) * W, :].astype(f32).reshape(R, HD) for n in range(2)]
-        s = jnp.dot(ref[:, 2 * W : 3 * W, :].reshape(R, HD), select, preferred_element_type=f32)
-        return o, t, s[:, 0:HD], s[:, HD : 2 * HD]
-
-    oa, ta, la, da = read(a_ref)
-    ob, tb, lb, db = read(b_ref)
-    top = jnp.maximum(la, lb)
-    wa, wb = jnp.exp2(la - top), jnp.exp2(lb - top)
-    inv = 1.0 / (wa + wb)
-    wa, wb = wa * inv, wb * inv
-    gap = wa * wb * (da - db)
-    out_ref[:, 0:W, :] = (wa * oa + wb * ob).astype(bf16).reshape(CHIPS, W, HD)
-    out_ref[:, W : 2 * W, :] = (wa * ta + wb * tb + gap * (oa - ob)).astype(bf16).reshape(CHIPS, W, HD)
-
-
-def combine(a, b):
+        out_shape=[pltpu.VMEM((RALL, 512), f32), pltpu.VMEM((RALL, 2 * HD), f32)] + [pltpu.VMEM(x.shape, x.dtype) for x in later],
+        scratch_shapes=[pltpu.SemaphoreType.DMA((FETCHES * len(later),))] + scratch(),
+        compiler_params=params(28),
+        cost_estimate=pl.CostEstimate(flops=5 * 10**9, bytes_accessed=20 * 2**20, transcendentals=2 * 10**6),
+    )(in_vmem(arrived), in_vmem(arrived), *[in_hbm(x) for x in later])
+    return outs[:2], outs[2:]
+
+
+def attend_more(arrived, swapped, state):
     return pl.pallas_call(
-        combine_kernel,
-        in_specs=[VMEM, VMEM],
+        lambda *refs: attn_kernel(*refs, second=True),
+        in_specs=[VMEM] * 4,
         out_specs=VMEM,
         out_shape=pltpu.VMEM((CHIPS, 2 * W, HD), bf16),
-        compiler_params=params(16),
-    )(a, b)
+        scratch_shapes=[pltpu.VMEM((RALL, 512), f32), pltpu.VMEM((RALL, 2 * HD), f32)] + scratch(),
+        compiler_params=params(28),
+        cost_estimate=pl.CostEstimate(flops=5 * 10**9, bytes_accessed=8 * 2**20, transcendentals=2 * 10**6),
+    )(*[in_vmem(x) for x in (arrived, swapped, *state)])
 
 
 CT = 256
@@ -436,15 +408,12 @@
         message, seg = pack(side, arrays, freq, positions[None, :], segments[None, :])
     with jax.named_scope("spread"):
         arrived = lax.all_to_all(message, ("z", "y", "x"), 0, 0, tiled=True)
-        asked = lax.slice_in_dim(arrived, ASK, MSG, axis=1)
-        asked_there = lax.ppermute(asked, "c", swap)
-
+        swapped = lax.ppermute(arrived, "c", swap)
     with jax.named_scope("attend"):
         later = (out_weight, gate, gate_tan, residual, residual_tan, mod_scale, mod_scale_tan, mod_shift, mod_shift_tan)
-        part, there, later = attend(asked, asked_there, arrived, later)
+        state, later = attend(arrived, later)
         held_weight, held_gate, held_gate_tan, held_resid, held_resid_tan, *tables = later
-        back = lax.ppermute(there, "c", swap)
-        answer = combine(part, back)
+        answer = attend_more(arrived, swapped, state)
     with jax.named_scope("collect"):
         attended = lax.all_to_all(answer, ("z", "y", "x"), 0, 0, tiled=True)
     with jax.named_scope("project"):

time: 146 us -> 143 us (0.979)
  waiting for transfers between devices: 40.6 us -> 37.3 us
    ppermute x2 -> x1, waiting for transfers between devices: 4.24 us -> 0.87 us  [body(): swapped = lax.ppermute(arrived, 'c', swap)]
  transfers between devices with their start and end apart: 6 -> 5, of which waited for: 6 -> 5; matrix products, arithmetic and copies ran while one was open for 0% -> 0% of each run, Pallas kernels for 2% -> 6%
where the time goes in v6:
time: 143 us
  blocking collectives  77.1 us (54%)
  waiting for transfers between devices  37.3 us (26%)
  Pallas kernels  23.1 us (16%)
  starting transfers between devices  4.37 us (3%)
    all_to_all x1, blocking collectives, body(): arrived = lax.all_to_all(message, ('z', 'y', 'x'), 0, 0, tiled=True)  59.5 us
    ppermute x2, waiting for transfers between devices, body(): got_mine.append(lax.ppermute(other[part], 'head', swap))  18.7 us
    ppermute x2, waiting for transfers between devices, body(): got_other.append(lax.ppermute(mine[part], 'head', swap))  17.7 us
    all_to_all x1, blocking collectives, body(): attended = lax.all_to_all(answer, ('z', 'y', 'x'), 0, 0, tiled=True)  17.5 us
    pallas_call x1, Pallas kernels, attend_more(): pl.pallas_call(lambda *refs: attn_kernel(*refs, second=True), in_specs=[V...  6.76 us
    pallas_call x1, Pallas kernels, attend(): pl.pallas_call(lambda *refs: attn_kernel(*refs, second=False), in_specs=[...  5.72 us
    pallas_call x1, Pallas kernels, norm(): pl.pallas_call(norm_kernel, in_specs=[pl.BlockSpec(memory_space=pltpu.SME...  4.07 us
    pallas_call x4, Pallas kernels, project(): pl.pallas_call(lambda *refs: project_kernel(*refs, own=own, part=part), i...  3.62 us
  transfers between devices with their start and end apart: 5, of which 5 were waited for; matrix products, arithmetic and copies ran while one was open for 0% of the time, Pallas kernels for 6%

profile of v6, /device:TPU:0, one launch (start us, length us, event | category | flops | bytes accessed | tf_op | source)
XLA Modules:
  0.0 142.6 jit_solution(2368105109007803588)
XLA Ops:
  0.6 2.9 %pack.1 = (bf16[32,464,128]{2,1,0:T(8,128)(2,1)S(1)}, f32[96,128]{1,0:T(8,128)S(1)}) custom-call(s32[1]{0:T(128)} %bitcast.side_ref.refs_0_, bf16[96,1280]{1,0:T(8,128)(2,1)} %q_hbm.1, bf16[96,1280]{1,0:T(8,128)(2,1)} %k_hbm.1, bf16[96,1280]{1,0:T(8,128)(2,1)} %v_hbm.1, bf16[96,1280]{1,0:T(8,128)(2,1)} %qt_hbm.1, bf16[96,1280]{1,0:T(8,128)(2,1)} %kt_hbm.1, ...), custom_call_target="tpu_custom_call" | custom-call | tf_op jit(solution)/shard_map/pack/pallas_call | solution.py:110
  3.5 59.5 %all_to_all.10.refs_0_.refs_1_ = bf16[32,464,128]{2,1,0:T(8,128)(2,1)S(1)} all-to-all(bf16[32,464,128]{2,1,0:T(8,128)(2,1)S(1)} %get-tuple-element.17), channel_id=1, replica_groups=mesh['z'=4,'y'=4,'x'=2,'c'=2,'head'=2] {'z','y','x'}, dimensions={0} | all-to-all | bytes 7602176 | tf_op jit(solution)/shard_map/spread/all_to_all | solution.py:410
  63.1 0.0 collective-permute-start
  63.1 5.7 %attend.2 = (f32[1088,512]{1,0:T(8,128)S(1)}, f32[1088,256]{1,0:T(8,128)S(1)}, bf16[1280,5120]{1,0:T(8,128)(2,1)S(1)}, f32[2,5120]{1,0:T(2,128)S(1)}, f32[2,5120...) custom-call(bf16[32,464,128]{2,1,0:T(8,128)(2,1)S(1)} %all_to_all.10, ...), custom_call_target="tpu_custom_call" | custom-call | flops 5000000000 | bytes 20971520 | tf_op jit(solution)/shard_map/attend/pallas_call | solution.py:265
  68.8 0.9 collective-permute-done.refs_1_
  69.7 6.8 %attend.3 = bf16[32,64,128]{2,1,0:T(8,128)(2,1)S(1)} custom-call(bf16[32,464,128]{2,1,0:T(8,128)(2,1)S(1)} %all_to_all.10.refs_0_.refs_1_, bf16[32,464,128]{2,1,0:T(8,128)(2,1)S(1)} %collective-permute-done.refs_1_, f32[1088,512]{1,0:T(8,128)S(1)} %get-tuple-element.18.refs_2_, f32[1088,256]{1,0:T(8,128)S(1)} %get-tuple-element.19.refs_3_), custom_call_target="tpu_custom_call" | custom-call | flops 5000000000 | bytes 8388608 | tf_op jit(solution)/shard_map/attend/pallas_call | solution.py:278
  76.4 17.5 %all_to_all.11.refs_1_ = bf16[32,64,128]{2,1,0:T(8,128)(2,1)S(1)} all-to-all(bf16[32,64,128]{2,1,0:T(8,128)(2,1)S(1)} %attend.3), channel_id=1, replica_groups=mesh['z'=4,'y'=4,'x'=2,'c'=2,'head'=2] {'z','y','x'}, dimensions={0} | all-to-all | bytes 1048576 | tf_op jit(solution)/shard_map/collect/all_to_all | solution.py:418
  94.0 0.9 project.4.refs_0_
  94.9 0.7 collective-permute-start.3
  95.6 0.9 project.5.refs_1_
  96.5 1.5 %collective-permute-start.4 = (bf16[2,96,1280]{2,1,0:T(8,128)(2,1)S(1)}, bf16[2,96,1280]{2,1,0:T(8,128)(2,1)S(1)}, u32[]{:S(2)}, u32[]{:S(2)}) collective-permute-start(bf16[2,96,1280]{2,1,0:T(8,128)(2,1)S(1)} %project.5.refs_1_), channel_id=1, source_target_pairs={{0,1},{1,0},{2,3},{3,2},{4,5},{5,4},{6,7},{7,6},{8,9},{9,8},{10,11... | collective-permute-start | bytes 1474568 | tf_op jit(solution)/shard_map/project/ppermute | solution.py:427
  98.0 0.9 project.6.refs_4_
  98.9 0.7 collective-permute-start.1
  99.6 0.9 project.7.refs_5_
  100.5 1.5 %collective-permute-start.2 = (bf16[2,96,1280]{2,1,0:T(8,128)(2,1)S(1)}, bf16[2,96,1280]{2,1,0:T(8,128)(2,1)S(1)}, u32[]{:S(2)}, u32[]{:S(2)}) collective-permute-start(bf16[2,96,1280]{2,1,0:T(8,128)(2,1)S(1)} %project.7.refs_5_), channel_id=1, source_target_pairs={{0,1},{1,0},{2,3},{3,2},{4,5},{5,4},{6,7},{7,6},{8,9},{9,8},{10,11... | collective-permute-start | bytes 1474568 | tf_op jit(solution)/shard_map/project/ppermute | solution.py:424
  102.0 7.1 %collective-permute-done.3.refs_6_ = bf16[2,96,1280]{2,1,0:T(8,128)(2,1)S(1)} collective-permute-done((bf16[2,96,1280]{2,1,0:T(8,128)(2,1)S(1)}, bf16[2,96,1280]{2,1,0:T(8,128)(2,1)S(1)}, u32[]{:S(2)}, u32[]{:S(2)}) %collective-permute-start.3) | collective-permute-done | bytes 491552 | tf_op jit(solution)/shard_map/project/ppermute | solution.py:427
  109.1 10.5 %collective-permute-done.4.refs_7_ = bf16[2,96,1280]{2,1,0:T(8,128)(2,1)S(1)} collective-permute-done((bf16[2,96,1280]{2,1,0:T(8,128)(2,1)S(1)}, bf16[2,96,1280]{2,1,0:T(8,128)(2,1)S(1)}, u32[]{:S(2)}, u32[]{:S(2)}) %collective-permute-start.4) | collective-permute-done | bytes 491552 | tf_op jit(solution)/shard_map/project/ppermute | solution.py:427
  119.7 10.5 %collective-permute-done.1.refs_2_ = bf16[2,96,1280]{2,1,0:T(8,128)(2,1)S(1)} collective-permute-done((bf16[2,96,1280]{2,1,0:T(8,128)(2,1)S(1)}, bf16[2,96,1280]{2,1,0:T(8,128)(2,1)S(1)}, u32[]{:S(2)}, u32[]{:S(2)}) %collective-permute-start.1) | collective-permute-done | bytes 491552 | tf_op jit(solution)/shard_map/project/ppermute | solution.py:424
  130.2 8.2 %collective-permute-done.2.refs_3_ = bf16[2,96,1280]{2,1,0:T(8,128)(2,1)S(1)} collective-permute-done((bf16[2,96,1280]{2,1,0:T(8,128)(2,1)S(1)}, bf16[2,96,1280]{2,1,0:T(8,128)(2,1)S(1)}, u32[]{:S(2)}, u32[]{:S(2)}) %collective-permute-start.2) | collective-permute-done | bytes 491552 | tf_op jit(solution)/shard_map/project/ppermute | solution.py:424
  138.4 4.1 %norm.1 = (f32[96,2560]{1,0:T(8,128)}, f32[96,2560]{1,0:T(8,128)}, bf16[96,5120]{1,0:T(8,128)(2,1)}, bf16[96,5120]{1,0:T(8,128)(2,1)}) custom-call(s32[1]{0:T(128)} %bitcast.side_ref.refs_0_, bf16[2,96,1280]{2,1,0:T(8,128)(2,1)S(1)} %project.4.refs_0_, bf16[2,96,1280]{2,1,0:T(8,128)(2,1)S(1)} %project.5.refs_1_, ...), custom_call_target="tpu_custom_call" | custom-call | tf_op jit(solution)/shard_map/norm/pallas_call | solution.py:387
Async XLA Ops:
  63.1 6.6 %collective-permute-start = (bf16[32,464,128]{2,1,0:T(8,128)(2,1)S(1)}, bf16[32,464,128]{2,1,0:T(8,128)(2,1)S(1)}, u32[]{:S(2)}, u32[]{:S(2)}) collective-permute-start(bf16[32,464,128]{2,1,0:T(8,128)(2,1)S(1)} %all_to_all.10.refs_0_.refs_1_), channel_id=1, source_target_pairs={{0,2},{2,0},{1,3},{3,1},{4,6},{6,4},{5,7},{7,5},{8,10},{10,8},{9,1... | collective-permute-start | bytes 11403272 | tf_op jit(solution)/shard_map/spread/ppermute | solution.py:411
  94.9 14.2 %collective-permute-start.3 = (bf16[2,96,1280]{2,1,0:T(8,128)(2,1)S(1)}, bf16[2,96,1280]{2,1,0:T(8,128)(2,1)S(1)}, u32[]{:S(2)}, u32[]{:S(2)}) collective-permute-start(bf16[2,96,1280]{2,1,0:T(8,128)(2,1)S(1)} %project.4.refs_0_), channel_id=1, source_target_pairs={{0,1},{1,0},{2,3},{3,2},{4,5},{5,4},{6,7},{7,6},{8,9},{9,8},{10,11... | collective-permute-start | bytes 1474568 | tf_op jit(solution)/shard_map/project/ppermute | solution.py:427
  96.5 23.1 %collective-permute-start.4 = (bf16[2,96,1280]{2,1,0:T(8,128)(2,1)S(1)}, bf16[2,96,1280]{2,1,0:T(8,128)(2,1)S(1)}, u32[]{:S(2)}, u32[]{:S(2)}) collective-permute-start(bf16[2,96,1280]{2,1,0:T(8,128)(2,1)S(1)} %project.5.refs_1_), channel_id=1, source_target_pairs={{0,1},{1,0},{2,3},{3,2},{4,5},{5,4},{6,7},{7,6},{8,9},{9,8},{10,11... | collective-permute-start | bytes 1474568 | tf_op jit(solution)/shard_map/project/ppermute | solution.py:427
  98.9 31.3 %collective-permute-start.1 = (bf16[2,96,1280]{2,1,0:T(8,128)(2,1)S(1)}, bf16[2,96,1280]{2,1,0:T(8,128)(2,1)S(1)}, u32[]{:S(2)}, u32[]{:S(2)}) collective-permute-start(bf16[2,96,1280]{2,1,0:T(8,128)(2,1)S(1)} %project.6.refs_4_), channel_id=1, source_target_pairs={{0,1},{1,0},{2,3},{3,2},{4,5},{5,4},{6,7},{7,6},{8,9},{9,8},{10,11... | collective-permute-start | bytes 1474568 | tf_op jit(solution)/shard_map/project/ppermute | solution.py:424
  100.5 37.9 %collective-permute-start.2 = (bf16[2,96,1280]{2,1,0:T(8,128)(2,1)S(1)}, bf16[2,96,1280]{2,1,0:T(8,128)(2,1)S(1)}, u32[]{:S(2)}, u32[]{:S(2)}) collective-permute-start(bf16[2,96,1280]{2,1,0:T(8,128)(2,1)S(1)} %project.7.refs_5_), channel_id=1, source_target_pairs={{0,1},{1,0},{2,3},{3,2},{4,5},{5,4},{6,7},{7,6},{8,9},{9,8},{10,11... | collective-permute-start | bytes 1474568 | tf_op jit(solution)/shard_map/project/ppermute | solution.py:424

commit v7 on v6

--- a/solution.py
+++ b/solution.py
@@ -247,8 +247,9 @@
             tag = jnp.concatenate([tags[:, 0:1], tags[:, 1:2]], axis=0)
             hit = jnp.broadcast_to(tag, (W, HD)) == wanted
             for n, x in enumerate((o, t)):
-                old = out_ref[j, n * W : (n + 1) * W, :].astype(f32)
-                out_ref[j, n * W : (n + 1) * W, :] = jnp.where(hit, x[at : at + W], old).astype(bf16)
+                lanes = slice(n * HD, (n + 1) * HD)
+                old = out_ref[j, :, lanes].astype(f32)
+                out_ref[j, :, lanes] = jnp.where(hit, x[at : at + W], old).astype(bf16)
     for copy in copies:
         copy.wait()
 
@@ -279,7 +280,7 @@
         lambda *refs: attn_kernel(*refs, second=True),
         in_specs=[VMEM] * 4,
         out_specs=VMEM,
-        out_shape=pltpu.VMEM((CHIPS, 2 * W, HD), bf16),
+        out_shape=pltpu.VMEM((CHIPS, W, 2 * HD), bf16),
         scratch_shapes=[pltpu.VMEM((RALL, 512), f32), pltpu.VMEM((RALL, 2 * HD), f32)] + scratch(),
         compiler_params=params(28),
         cost_estimate=pl.CostEstimate(flops=5 * 10**9, bytes_accessed=8 * 2**20, transcendentals=2 * 10**6),
@@ -302,8 +303,8 @@
     for h in range(NH):
         for t in range(PARTS):
             s = worker(h, t)
-            lhs_ref[t * W : (t + 1) * W, h * HD : (h + 1) * HD] = x_ref[s, 0:W, :]
-            lhs_ref[ROWS + t * W : ROWS + (t + 1) * W, h * HD : (h + 1) * HD] = x_ref[s, W : 2 * W, :]
+            lhs_ref[t * W : (t + 1) * W, h * HD : (h + 1) * HD] = x_ref[s, :, 0:HD]
+            lhs_ref[ROWS + t * W : ROWS + (t + 1) * W, h * HD : (h + 1) * HD] = x_ref[s, :, HD : 2 * HD]
     one = seg_ref[:, 0:1] == 1.0
     for j in range(STEPS):
         cols = pl.ds(pl.multiple_of(start + j * CT, CT), CT)
@@ -335,63 +336,91 @@
     )(side, *[in_vmem(x) for x in (x, w, seg, gate, gate_tan, *resid)])
 
 
-FT = 32
-
-
-def norm_kernel(side_ref, *refs):
-    rows = [refs[i * SENDS : (i + 1) * SENDS] for i in range(4)]
-    seg_ref, scale_ref, scale_tan_ref, shift_ref, shift_tan_ref = refs[4 * SENDS : 4 * SENDS + 5]
-    outs, held, sem = refs[4 * SENDS + 5 : 4 * SENDS + 9], refs[4 * SENDS + 9 : 4 * SENDS + 13], refs[-1]
-    resid_ref, resid_tan_ref, ffn_ref, ffn_tan_ref = held
+FT, FN = 16, 16
+
+
+def moments(a, b):
+    lane = lax.broadcasted_iota(i32, (a.shape[0], HD), 1)
+    out = jnp.zeros((a.shape[0], HD), f32)
+    for i, x in enumerate((a, a * a, b, a * b)):
+        out = jnp.where(lane == i, jnp.sum(x, axis=1, keepdims=True), out)
+    return out
+
+
+def settle_kernel(*refs):
+    kept, got, refs = refs[:SENDS], refs[SENDS : 2 * SENDS], refs[2 * SENDS :]
+    seg_ref, tables, (pass_ref, a_ref, b_ref, sums_ref, rows_ref, resid_hbm, resid_tan_hbm, sem) = refs[0], refs[1:5], refs[5:]
+    del pass_ref
     copies = []
     for step in range(ROWS // FT):
         at = slice(step * FT, (step + 1) * FT)
-
-        def whole(kept, got, i):
-            return jnp.concatenate([x[i, at].astype(f32) + y[i, at].astype(f32) for x, y in zip(kept, got)], axis=1)
-
-        a = [whole(rows[0], rows[1], 0), whole(rows[2], rows[3], 0)]
-        b = [whole(rows[0], rows[1], 1), whole(rows[2], rows[3], 1)]
-        resid_ref[at] = a[0]
-        resid_tan_ref[at] = b[0]
-
-        def average(x, y):
-            return jnp.sum(x + y, axis=1, keepdims=True) / D
-
-        mean, mean_tan = average(*a), average(*b)
-        rstd = lax.rsqrt(average(a[0] * a[0], a[1] * a[1]) - mean * mean + norm_eps)
-        cov = average(a[0] * b[0], a[1] * b[1]) - mean * mean_tan
+        a, b = (jnp.concatenate([x[i, at].astype(f32) + y[i, at].astype(f32) for x, y in zip(kept, got)], axis=1) for i in range(2))
+        a_ref[at] = a
+        b_ref[at] = b
+        sums_ref[at] = moments(a, b)
+        for i, (src, dst) in enumerate(((a_ref, resid_hbm), (b_ref, resid_tan_hbm))):
+            copies.append(pltpu.make_async_copy(src.at[at], dst.at[at], sem.at[step, i]))
+            copies[-1].start()
+    one = seg_ref[:, 0:1] == 1.0
+    for i, table in enumerate(tables):
+        row = jnp.where(one, table[1:2, :], table[0:1, :])
+        rows_ref[i] = row + 1.0 if i == 0 else row
+    for copy in copies:
+        copy.wait()
+
+
+def settle(kept, got, seg, tables):
+    half, out = pltpu.VMEM((ROWS, HALF), f32), jax.ShapeDtypeStruct((ROWS, HALF), f32)
+    return pl.pallas_call(
+        settle_kernel,
+        in_specs=[VMEM] * (2 * SENDS + 5),
+        out_specs=[VMEM] * 5 + [ANY] * 2,
+        out_shape=[pltpu.VMEM((2, ROWS, PIECE), bf16), half, half, pltpu.VMEM((ROWS, HD), f32), pltpu.VMEM((4, ROWS, D), f32), out, out],
+        input_output_aliases={SENDS - 1: 0},
+        scratch_shapes=[pltpu.SemaphoreType.DMA((ROWS // FT, 2))],
+        compiler_params=params(16),
+    )(*[in_vmem(x) for x in (*kept, *got, seg, *tables)])
+
+
+def norm_kernel(side_ref, *refs):
+    rows = [refs[i * SENDS : (i + 1) * SENDS] for i in range(2)]
+    a_ref, b_ref, sums_ref, rows_ref = refs[2 * SENDS : 2 * SENDS + 4]
+    outs, held, sem = refs[2 * SENDS + 4 : 2 * SENDS + 6], refs[2 * SENDS + 6 : 2 * SENDS + 8], refs[-1]
+    ffn_ref, ffn_tan_ref = held
+    copies = []
+    for step in range(ROWS // FN):
+        at = slice(step * FN, (step + 1) * FN)
+        a, b = (jnp.concatenate([x[i, at].astype(f32) + y[i, at].astype(f32) for x, y in zip(*rows)], axis=1) for i in range(2))
+        total = (moments(a, b) + sums_ref[at]) / D
+        mean, mean_tan = total[:, 0:1], total[:, 2:3]
+        rstd = lax.rsqrt(total[:, 1:2] - mean * mean + norm_eps)
+        cov = total[:, 3:4] - mean * mean_tan
         slope = rstd * rstd * rstd * cov
-        one = seg_ref[at, 0:1] == 1.0
-        for i, side in enumerate((side_ref[0], 1 - side_ref[0])):
+        for side, x, y in ((1 - side_ref[0], a, b), (side_ref[0], a_ref[at], b_ref[at])):
             cols = pl.ds(pl.multiple_of(side * HALF, HALF), HALF)
-
-            def pick(ref):
-                return jnp.where(one, ref[1:2, cols], ref[0:1, cols])
-
-            centered = a[i] - mean
+            centered = x - mean
             normed = centered * rstd
-            normed_tan = (b[i] - mean_tan) * rstd - centered * slope
-            scale = 1.0 + pick(scale_ref)
-            ffn_ref[at, cols] = (normed * scale + pick(shift_ref)).astype(bf16)
-            ffn_tan_ref[at, cols] = (normed_tan * scale + normed * pick(scale_tan_ref) + pick(shift_tan_ref)).astype(bf16)
-        for i in range(4):
+            normed_tan = (y - mean_tan) * rstd - centered * slope
+            scale, scale_tan, shift, shift_tan = (rows_ref[i, at, cols] for i in range(4))
+            ffn_ref[at, cols] = (normed * scale + shift).astype(bf16)
+            ffn_tan_ref[at, cols] = (normed_tan * scale + normed * scale_tan + shift_tan).astype(bf16)
+        for i in range(2):
             copies.append(pltpu.make_async_copy(held[i].at[at], outs[i].at[at], sem.at[step, i]))
             copies[-1].start()
     for copy in copies:
         copy.wait()
 
 
-def norm(side, mine, got_mine, other, got_other, seg, tables):
-    outs = [jax.ShapeDtypeStruct((ROWS, HALF), f32)] * 2 + [jax.ShapeDtypeStruct((ROWS, D), bf16)] * 2
+def norm(side, other, got_other, settled):
+    outs = [jax.ShapeDtypeStruct((ROWS, D), bf16)] * 2
     return pl.pallas_call(
         norm_kernel,
-        in_specs=[pl.BlockSpec(memory_space=pltpu.SMEM)] + [VMEM] * (4 * SENDS + 5),
-        out_specs=[ANY] * 4,
+        in_specs=[pl.BlockSpec(memory_space=pltpu.SMEM)] + [VMEM] * (2 * SENDS + 4),
+        out_specs=[ANY] * 2,
         out_shape=outs,
-        scratch_shapes=[pltpu.VMEM(x.shape, x.dtype) for x in outs] + [pltpu.SemaphoreType.DMA((ROWS // FT, 4))],
+        scratch_shapes=[pltpu.VMEM(x.shape, x.dtype) for x in outs] + [pltpu.SemaphoreType.DMA((ROWS // FN, 2))],
         compiler_params=params(32),
-    )(side, *[in_vmem(x) for x in (*mine, *got_mine, *other, *got_other, seg, *tables)])
+    )(side, *[in_vmem(x) for x in (*other, *got_other, *settled)])
 
 
 def body(
@@ -418,15 +447,15 @@
         attended = lax.all_to_all(answer, ("z", "y", "x"), 0, 0, tiled=True)
     with jax.named_scope("project"):
         args = (attended, held_weight, seg, held_gate, held_gate_tan)
-        other, got_mine, mine, got_other = [], [], [], []
-        for part in range(SENDS):
-            other.append(project(side, *args, (), part))
-            got_mine.append(lax.ppermute(other[part], "head", swap))
-        for part in range(SENDS):
-            mine.append(project(side, *args, (held_resid, held_resid_tan), part))
-            got_other.append(lax.ppermute(mine[part], "head", swap))
+        other = [project(side, *args, (), part) for part in range(SENDS)]
+        got_mine = [lax.ppermute(x, "head", swap) for x in other]
+        mine = [project(side, *args, (held_resid, held_resid_tan), part) for part in range(SENDS)]
+        got_other = [lax.ppermute(x, "head", swap) for x in mine[:-1]]
+        last, *settled, resid, resid_tan = settle(mine, got_mine, seg, tables)
+        got_other.append(lax.ppermute(last, "head", swap))
     with jax.named_scope("norm"):
-        return tuple(norm(side, mine, got_mine, other, got_other, seg, tables))
+        ffn, ffn_tan = norm(side, other, got_other, settled)
+    return resid, resid_tan, ffn, ffn_tan
 
 
 def solution(mesh):

time: 143 us -> 142 us (level)
    pallas_call x0 -> x1, Pallas kernels: none -> 1.8 us  [settle(): pl.pallas_call(settle_kernel, in_specs=[VMEM] * (2 * SENDS + 5), out_spec...]
  transfers between devices with their start and end apart: 5 -> 5, of which waited for: 5 -> 5; matrix products, arithmetic and copies ran while one was open for 0% -> 0% of each run, Pallas kernels for 6% -> 7%
where the time goes in v7:
time: 142 us; the launch traced here: 141 us
  blocking collectives  77 us (54%)
  waiting for transfers between devices  36.2 us (25%)
  Pallas kernels  23.7 us (17%)
  starting transfers between devices  3.58 us (3%)
    all_to_all x1, blocking collectives, body(): arrived = lax.all_to_all(message, ('z', 'y', 'x'), 0, 0, tiled=True)  59.5 us
    ppermute x2, waiting for transfers between devices, body(): got_mine = [lax.ppermute(x, 'head', swap) for x in other]  19.2 us
    all_to_all x1, blocking collectives, body(): attended = lax.all_to_all(answer, ('z', 'y', 'x'), 0, 0, tiled=True)  17.5 us
    ppermute x1, waiting for transfers between devices, body(): got_other.append(lax.ppermute(last, 'head', swap))  8.18 us
    ppermute x1, waiting for transfers between devices, body(): got_other = [lax.ppermute(x, 'head', swap) for x in mine[:-1]]  8.04 us
    pallas_call x1, Pallas kernels, attend_more(): pl.pallas_call(lambda *refs: attn_kernel(*refs, second=True), in_specs=[V...  6.77 us
    pallas_call x1, Pallas kernels, attend(): pl.pallas_call(lambda *refs: attn_kernel(*refs, second=False), in_specs=[...  5.72 us
    pallas_call x4, Pallas kernels, project(): pl.pallas_call(lambda *refs: project_kernel(*refs, own=own, part=part), i...  3.6 us
  transfers between devices with their start and end apart: 5, of which 5 were waited for; matrix products, arithmetic and copies ran while one was open for 0% of the time, Pallas kernels for 7%

profile of v7, /device:TPU:0, one launch (start us, length us, event | category | flops | bytes accessed | tf_op | source)
XLA Modules:
  0.0 141.4 jit_solution(6851538492441962783)
XLA Ops:
  0.6 2.9 %pack.1 = (bf16[32,464,128]{2,1,0:T(8,128)(2,1)S(1)}, f32[96,128]{1,0:T(8,128)S(1)}) custom-call(s32[1]{0:T(128)} %bitcast.side_ref.refs_0_, bf16[96,1280]{1,0:T(8,128)(2,1)} %q_hbm.1, bf16[96,1280]{1,0:T(8,128)(2,1)} %k_hbm.1, bf16[96,1280]{1,0:T(8,128)(2,1)} %v_hbm.1, bf16[96,1280]{1,0:T(8,128)(2,1)} %qt_hbm.1, bf16[96,1280]{1,0:T(8,128)(2,1)} %kt_hbm.1, ...), custom_call_target="tpu_custom_call" | custom-call | tf_op jit(solution)/shard_map/pack/pallas_call | solution.py:110
  3.5 59.5 %all_to_all.10.refs_0_.refs_1_ = bf16[32,464,128]{2,1,0:T(8,128)(2,1)S(1)} all-to-all(bf16[32,464,128]{2,1,0:T(8,128)(2,1)S(1)} %get-tuple-element.26), channel_id=1, replica_groups=mesh['z'=4,'y'=4,'x'=2,'c'=2,'head'=2] {'z','y','x'}, dimensions={0} | all-to-all | bytes 7602176 | tf_op jit(solution)/shard_map/spread/all_to_all | solution.py:439
  63.1 0.0 collective-permute-start
  63.1 5.7 %attend.2 = (f32[1088,512]{1,0:T(8,128)S(1)}, f32[1088,256]{1,0:T(8,128)S(1)}, bf16[1280,5120]{1,0:T(8,128)(2,1)S(1)}, f32[2,5120]{1,0:T(2,128)S(1)}, f32[2,5120...) custom-call(bf16[32,464,128]{2,1,0:T(8,128)(2,1)S(1)} %all_to_all.10, ...), custom_call_target="tpu_custom_call" | custom-call | flops 5000000000 | bytes 20971520 | tf_op jit(solution)/shard_map/attend/pallas_call | solution.py:266
  68.8 0.9 collective-permute-done.refs_1_
  69.7 6.8 %attend.3 = bf16[32,32,256]{2,1,0:T(8,128)(2,1)S(1)} custom-call(bf16[32,464,128]{2,1,0:T(8,128)(2,1)S(1)} %all_to_all.10.refs_0_.refs_1_, bf16[32,464,128]{2,1,0:T(8,128)(2,1)S(1)} %collective-permute-done.refs_1_, f32[1088,512]{1,0:T(8,128)S(1)} %get-tuple-element.27.refs_2_, f32[1088,256]{1,0:T(8,128)S(1)} %get-tuple-element.28.refs_3_), custom_call_target="tpu_custom_call" | custom-call | flops 5000000000 | bytes 8388608 | tf_op jit(solution)/shard_map/attend/pallas_call | solution.py:279
  76.4 17.5 %all_to_all.11.refs_1_ = bf16[32,32,256]{2,1,0:T(8,128)(2,1)S(1)} all-to-all(bf16[32,32,256]{2,1,0:T(8,128)(2,1)S(1)} %attend.3), channel_id=1, replica_groups=mesh['z'=4,'y'=4,'x'=2,'c'=2,'head'=2] {'z','y','x'}, dimensions={0} | all-to-all | bytes 1048576 | tf_op jit(solution)/shard_map/collect/all_to_all | solution.py:447
  94.0 0.9 project.7.refs_0_
  94.9 0.7 collective-permute-start.1
  95.6 0.9 project.8.refs_1_
  96.5 1.5 %collective-permute-start.2 = (bf16[2,96,1280]{2,1,0:T(8,128)(2,1)S(1)}, bf16[2,96,1280]{2,1,0:T(8,128)(2,1)S(1)}, u32[]{:S(2)}, u32[]{:S(2)}) collective-permute-start(bf16[2,96,1280]{2,1,0:T(8,128)(2,1)S(1)} %project.8.refs_1_), channel_id=1, source_target_pairs={{0,1},{1,0},{2,3},{3,2},{4,5},{5,4},{6,7},{7,6},{8,9},{9,8},{10,11... | collective-permute-start | bytes 1474568 | tf_op jit(solution)/shard_map/project/ppermute | solution.py:451
  98.0 0.9 project.5.refs_0_
  98.9 0.7 collective-permute-start.3
  99.6 0.9 project.6.refs_1_
  100.5 8.6 %collective-permute-done.1.refs_2_ = bf16[2,96,1280]{2,1,0:T(8,128)(2,1)S(1)} collective-permute-done((bf16[2,96,1280]{2,1,0:T(8,128)(2,1)S(1)}, bf16[2,96,1280]{2,1,0:T(8,128)(2,1)S(1)}, u32[]{:S(2)}, u32[]{:S(2)}) %collective-permute-start.1) | collective-permute-done | bytes 491552 | tf_op jit(solution)/shard_map/project/ppermute | solution.py:451
  109.1 10.5 %collective-permute-done.2.refs_3_ = bf16[2,96,1280]{2,1,0:T(8,128)(2,1)S(1)} collective-permute-done((bf16[2,96,1280]{2,1,0:T(8,128)(2,1)S(1)}, bf16[2,96,1280]{2,1,0:T(8,128)(2,1)S(1)}, u32[]{:S(2)}, u32[]{:S(2)}) %collective-permute-start.2) | collective-permute-done | bytes 491552 | tf_op jit(solution)/shard_map/project/ppermute | solution.py:451
  119.7 1.8 %project.9 = (bf16[2,96,1280]{2,1,0:T(8,128)(2,1)S(1)}, f32[96,2560]{1,0:T(8,128)S(1)}, f32[96,2560]{1,0:T(8,128)S(1)}, f32[96,128]{1,0:T(8,128)S(1)}, f32[4,96,...) custom-call(bf16[2,96,1280]{2,1,0:T(8,128)(2,1)S(1)} %project.5.refs_0_, ...), custom_call_target="tpu_custom_call", output_to_operand_aliasing={{0}: (1, {})} | custom-call | tf_op jit(solution)/shard_map/project/pallas_call | solution.py:374
  121.5 0.7 collective-permute-start.4
  122.2 8.0 %collective-permute-done.3.refs_2_ = bf16[2,96,1280]{2,1,0:T(8,128)(2,1)S(1)} collective-permute-done((bf16[2,96,1280]{2,1,0:T(8,128)(2,1)S(1)}, bf16[2,96,1280]{2,1,0:T(8,128)(2,1)S(1)}, u32[]{:S(2)}, u32[]{:S(2)}) %collective-permute-start.3) | collective-permute-done | bytes 491552 | tf_op jit(solution)/shard_map/project/ppermute | solution.py:453
  130.2 8.2 %collective-permute-done.4.refs_3_ = bf16[2,96,1280]{2,1,0:T(8,128)(2,1)S(1)} collective-permute-done((bf16[2,96,1280]{2,1,0:T(8,128)(2,1)S(1)}, bf16[2,96,1280]{2,1,0:T(8,128)(2,1)S(1)}, u32[]{:S(2)}, u32[]{:S(2)}) %collective-permute-start.4) | collective-permute-done | bytes 491552 | tf_op jit(solution)/shard_map/project/ppermute | solution.py:455
  138.4 2.9 %norm.1 = (bf16[96,5120]{1,0:T(8,128)(2,1)}, bf16[96,5120]{1,0:T(8,128)(2,1)}) custom-call(s32[1]{0:T(128)} %bitcast.side_ref.refs_0_, bf16[2,96,1280]{2,1,0:T(8,128)(2,1)S(1)} %project.7.refs_0_, bf16[2,96,1280]{2,1,0:T(8,128)(2,1)S(1)} %project.8.refs_1_, bf16[2,96,1280]{2,1,0:T(8,128)(2,1)S(1)} %collective-permute-done.3.refs_2_, ...), custom_call_target="tpu_custom_call" | custom-call | tf_op jit(solution)/shard_map/norm/pallas_call | solution.py:416
Async XLA Ops:
  63.1 6.6 %collective-permute-start = (bf16[32,464,128]{2,1,0:T(8,128)(2,1)S(1)}, bf16[32,464,128]{2,1,0:T(8,128)(2,1)S(1)}, u32[]{:S(2)}, u32[]{:S(2)}) collective-permute-start(bf16[32,464,128]{2,1,0:T(8,128)(2,1)S(1)} %all_to_all.10.refs_0_.refs_1_), channel_id=1, source_target_pairs={{0,2},{2,0},{1,3},{3,1},{4,6},{6,4},{5,7},{7,5},{8,10},{10,8},{9,1... | collective-permute-start | bytes 11403272 | tf_op jit(solution)/shard_map/spread/ppermute | solution.py:440
  94.9 14.2 %collective-permute-start.1 = (bf16[2,96,1280]{2,1,0:T(8,128)(2,1)S(1)}, bf16[2,96,1280]{2,1,0:T(8,128)(2,1)S(1)}, u32[]{:S(2)}, u32[]{:S(2)}) collective-permute-start(bf16[2,96,1280]{2,1,0:T(8,128)(2,1)S(1)} %project.7.refs_0_), channel_id=1, source_target_pairs={{0,1},{1,0},{2,3},{3,2},{4,5},{5,4},{6,7},{7,6},{8,9},{9,8},{10,11... | collective-permute-start | bytes 1474568 | tf_op jit(solution)/shard_map/project/ppermute | solution.py:451
  96.5 23.2 %collective-permute-start.2 = (bf16[2,96,1280]{2,1,0:T(8,128)(2,1)S(1)}, bf16[2,96,1280]{2,1,0:T(8,128)(2,1)S(1)}, u32[]{:S(2)}, u32[]{:S(2)}) collective-permute-start(bf16[2,96,1280]{2,1,0:T(8,128)(2,1)S(1)} %project.8.refs_1_), channel_id=1, source_target_pairs={{0,1},{1,0},{2,3},{3,2},{4,5},{5,4},{6,7},{7,6},{8,9},{9,8},{10,11... | collective-permute-start | bytes 1474568 | tf_op jit(solution)/shard_map/project/ppermute | solution.py:451
  98.9 31.3 %collective-permute-start.3 = (bf16[2,96,1280]{2,1,0:T(8,128)(2,1)S(1)}, bf16[2,96,1280]{2,1,0:T(8,128)(2,1)S(1)}, u32[]{:S(2)}, u32[]{:S(2)}) collective-permute-start(bf16[2,96,1280]{2,1,0:T(8,128)(2,1)S(1)} %project.5.refs_0_), channel_id=1, source_target_pairs={{0,1},{1,0},{2,3},{3,2},{4,5},{5,4},{6,7},{7,6},{8,9},{9,8},{10,11... | collective-permute-start | bytes 1474568 | tf_op jit(solution)/shard_map/project/ppermute | solution.py:453
  121.5 16.9 %collective-permute-start.4 = (bf16[2,96,1280]{2,1,0:T(8,128)(2,1)S(1)}, bf16[2,96,1280]{2,1,0:T(8,128)(2,1)S(1)}, u32[]{:S(2)}, u32[]{:S(2)}) collective-permute-start(bf16[2,96,1280]{2,1,0:T(8,128)(2,1)S(1)} %get-tuple-element.41), channel_id=1, source_target_pairs={{0,1},{1,0},{2,3},{3,2},{4,5},{5,4},{6,7},{7,6},{8,9},{9,8},{10,11... | collective-permute-start | bytes 1474568 | tf_op jit(solution)/shard_map/project/ppermute | solution.py:455

commit v8 on v7

--- a/solution.py
+++ b/solution.py
@@ -137,14 +137,14 @@
 
 
 def attn_kernel(q_ref, kv_ref, *refs, second):
-    s_ref, pen_ref, keys_ref, kind_ref, chips_ref, cut_ref = refs[-6:]
+    long_ref, short_ref, pen_ref, keys_ref, kind_ref, chips_ref, cut_ref = refs[-7:]
     copies = []
     if second:
-        old_ref, old_stat_ref, out_ref, acc_ref, stat_ref = refs[:-6]
+        old_ref, old_stat_ref, out_ref, acc_ref, stat_ref = refs[:-7]
     else:
-        n = (len(refs) - 9) // 2
+        n = (len(refs) - 10) // 2
         acc_ref, stat_ref = refs[n : n + 2]
-        sem = refs[-7]
+        sem = refs[-8]
         for src, dst in zip(refs[:n], refs[n + 2 : 2 * n + 2]):
             cuts = FETCHES if src.shape[0] % (16 * FETCHES) == 0 else 1
             step = src.shape[0] // cuts
@@ -187,7 +187,8 @@
         pen_ref[2 + p] = jnp.where(lane == 0, col * neg_fill, 0.0).astype(bf16)
         pen_ref[4 + p] = jnp.where(lane == 0, (1.0 - col) * neg_fill, 0.0).astype(bf16)
 
-    for (chips, blocks), clip, base in ((LONG, long_clip, 0), (SHORT, 1 - long_clip, RLONG)):
+    held = []
+    for (chips, blocks), clip, base, s_ref in ((LONG, long_clip, 0, long_ref), (SHORT, 1 - long_clip, RLONG, short_ref)):
         R = chips * THIRD
         here = slice(base, base + R)
         listed = [chips_ref[clip, i] for i in range(chips)]
@@ -207,6 +208,8 @@
                 m = jnp.maximum(m, s[:, j * HD : (j + 1) * HD])
         top = jnp.max(m, axis=1, keepdims=True)
         m_old = old_stat_ref[here, 0:1] if second else None
+        held.append((clip, here, s_ref, listed, qq, places, top, m_old, R))
+    for clip, here, s_ref, listed, qq, places, top, m_old, R in held:
         for b, span, width in places:
             gap = width - len(span) * ROWS
             fill = [jnp.zeros((gap, HD), bf16)] * (gap > 0)
@@ -259,7 +262,8 @@
 
 def scratch():
     lists = [pltpu.SMEM((2, CHIPS), i32)] * 3 + [pltpu.SMEM((3,), i32)]
-    return [pltpu.VMEM((len(LONG[1]), RLONG, KR), f32), pltpu.VMEM((6, ROWS, HD), bf16)] + lists
+    scores = [pltpu.VMEM((len(LONG[1]), RLONG, KR), f32), pltpu.VMEM((len(SHORT[1]), RSHORT, KR), f32)]
+    return scores + [pltpu.VMEM((6, ROWS, HD), bf16)] + lists
 
 
 def attend(arrived, later):
@@ -287,8 +291,8 @@
     )(*[in_vmem(x) for x in (arrived, swapped, *state)])
 
 
-CT = 256
-SENDS = 2
+CT = 512
+SENDS = 5
 PIECE = HALF // SENDS
 STEPS = PIECE // CT
 
@@ -436,7 +440,7 @@
         arrays = (queries, keys, values, queries_tan, keys_tan, values_tan)
         message, seg = pack(side, arrays, freq, positions[None, :], segments[None, :])
     with jax.named_scope("spread"):
-        arrived = lax.all_to_all(message, ("z", "y", "x"), 0, 0, tiled=True)
+        arrived = lax.all_to_all(message, ("x", "z", "y"), 0, 0, tiled=True)
         swapped = lax.ppermute(arrived, "c", swap)
     with jax.named_scope("attend"):
         later = (out_weight, gate, gate_tan, residual, residual_tan, mod_scale, mod_scale_tan, mod_shift, mod_shift_tan)
@@ -444,7 +448,7 @@
         held_weight, held_gate, held_gate_tan, held_resid, held_resid_tan, *tables = later
         answer = attend_more(arrived, swapped, state)
     with jax.named_scope("collect"):
-        attended = lax.all_to_all(answer, ("z", "y", "x"), 0, 0, tiled=True)
+        attended = lax.all_to_all(answer, ("x", "z", "y"), 0, 0, tiled=True)
     with jax.named_scope("project"):
         args = (attended, held_weight, seg, held_gate, held_gate_tan)
         other = [project(side, *args, (), part) for part in range(SENDS)]

time: 142 us -> 139 us (0.979)
  waiting for transfers between devices: 36.2 us -> 28.7 us
  starting transfers between devices: 3.58 us -> 8.93 us
    ppermute x2 -> x5, waiting for transfers between devices: 19.2 us -> 12.2 us  [body(): got_mine = [lax.ppermute(x, 'head', swap) for x in other]]
    ppermute x1, waiting for transfers between devices: 8.18 us -> 2.11 us  [body(): got_other.append(lax.ppermute(last, 'head', swap))]
    ppermute x1 -> x4, waiting for transfers between devices: 8.04 us -> 13.7 us  [body(): got_other = [lax.ppermute(x, 'head', swap) for x in mine[:-1]]]
    ppermute x2 -> x5, starting transfers between devices: 2.18 us -> 4.99 us  [body(): got_mine = [lax.ppermute(x, 'head', swap) for x in other]]
    ppermute x1 -> x4, starting transfers between devices: 0.72 us -> 3.29 us  [body(): got_other = [lax.ppermute(x, 'head', swap) for x in mine[:-1]]]
    pallas_call x4 -> x10, Pallas kernels: 3.6 us -> 4.73 us  [project(): pl.pallas_call(lambda *refs: project_kernel(*refs, own=own, part=part), i...]
  transfers between devices with their start and end apart: 5 -> 11, of which waited for: 5 -> 10; matrix products, arithmetic and copies ran while one was open for 0% -> 0% of each run, Pallas kernels for 7% -> 9%
where the time goes in v8:
time: 139 us
  blocking collectives  76 us (55%)
  waiting for transfers between devices  28.7 us (21%)
  Pallas kernels  24.5 us (18%)
  starting transfers between devices  8.93 us (6%)
    all_to_all x1, blocking collectives, body(): arrived = lax.all_to_all(message, ('x', 'z', 'y'), 0, 0, tiled=True)  58.8 us
    all_to_all x1, blocking collectives, body(): attended = lax.all_to_all(answer, ('x', 'z', 'y'), 0, 0, tiled=True)  17.2 us
    ppermute x4, waiting for transfers between devices, body(): got_other = [lax.ppermute(x, 'head', swap) for x in mine[:-1]]  13.7 us
    ppermute x5, waiting for transfers between devices, body(): got_mine = [lax.ppermute(x, 'head', swap) for x in other]  12.2 us
    pallas_call x1, Pallas kernels, attend_more(): pl.pallas_call(lambda *refs: attn_kernel(*refs, second=True), in_specs=[V...  6.33 us
    pallas_call x1, Pallas kernels, attend(): pl.pallas_call(lambda *refs: attn_kernel(*refs, second=False), in_specs=[...  5.85 us
    ppermute x5, starting transfers between devices, body(): got_mine = [lax.ppermute(x, 'head', swap) for x in other]  4.99 us
    pallas_call x10, Pallas kernels, project(): pl.pallas_call(lambda *refs: project_kernel(*refs, own=own, part=part), i...  4.73 us
  transfers between devices with their start and end apart: 11, of which 10 were waited for; matrix products, arithmetic and copies ran while one was open for 0% of the time, Pallas kernels for 9%

profile of v8, /device:TPU:0, one launch (start us, length us, event | category | flops | bytes accessed | tf_op | source)
XLA Modules:
  0.0 139.0 jit_solution(7603789652797288341)
XLA Ops:
  0.6 2.9 %pack.1 = (bf16[32,464,128]{2,1,0:T(8,128)(2,1)S(1)}, f32[96,128]{1,0:T(8,128)S(1)}) custom-call(s32[1]{0:T(128)} %bitcast.side_ref.refs_0_, bf16[96,1280]{1,0:T(8,128)(2,1)} %q_hbm.1, bf16[96,1280]{1,0:T(8,128)(2,1)} %k_hbm.1, bf16[96,1280]{1,0:T(8,128)(2,1)} %v_hbm.1, bf16[96,1280]{1,0:T(8,128)(2,1)} %qt_hbm.1, bf16[96,1280]{1,0:T(8,128)(2,1)} %kt_hbm.1, ...), custom_call_target="tpu_custom_call" | custom-call | tf_op jit(solution)/shard_map/pack/pallas_call | solution.py:110
  3.5 58.8 %all_to_all.10.refs_0_.refs_1_ = bf16[32,464,128]{2,1,0:T(8,128)(2,1)S(1)} all-to-all(bf16[32,464,128]{2,1,0:T(8,128)(2,1)S(1)} %get-tuple-element.26), channel_id=1, replica_groups=mesh['z'=4,'y'=4,'x'=2,'c'=2,'head'=2] {'x','z','y'}, dimensions={0} | all-to-all | bytes 7602176 | tf_op jit(solution)/shard_map/spread/all_to_all | solution.py:443
  62.3 0.0 collective-permute-start
  62.3 5.9 %attend.2 = (f32[1088,512]{1,0:T(8,128)S(1)}, f32[1088,256]{1,0:T(8,128)S(1)}, bf16[1280,5120]{1,0:T(8,128)(2,1)S(1)}, f32[2,5120]{1,0:T(2,128)S(1)}, f32[2,5120...) custom-call(bf16[32,464,128]{2,1,0:T(8,128)(2,1)S(1)} %all_to_all.10, ...), custom_call_target="tpu_custom_call" | custom-call | flops 5000000000 | bytes 20971520 | tf_op jit(solution)/shard_map/attend/pallas_call | solution.py:270
  68.2 0.7 collective-permute-done.refs_1_
  68.9 6.3 %attend.3 = bf16[32,32,256]{2,1,0:T(8,128)(2,1)S(1)} custom-call(bf16[32,464,128]{2,1,0:T(8,128)(2,1)S(1)} %all_to_all.10.refs_0_.refs_1_, bf16[32,464,128]{2,1,0:T(8,128)(2,1)S(1)} %collective-permute-done.refs_1_, f32[1088,512]{1,0:T(8,128)S(1)} %get-tuple-element.27.refs_2_, f32[1088,256]{1,0:T(8,128)S(1)} %get-tuple-element.28.refs_3_), custom_call_target="tpu_custom_call" | custom-call | flops 5000000000 | bytes 8388608 | tf_op jit(solution)/shard_map/attend/pallas_call | solution.py:283
  75.3 17.2 %all_to_all.11.refs_1_ = bf16[32,32,256]{2,1,0:T(8,128)(2,1)S(1)} all-to-all(bf16[32,32,256]{2,1,0:T(8,128)(2,1)S(1)} %attend.3), channel_id=1, replica_groups=mesh['z'=4,'y'=4,'x'=2,'c'=2,'head'=2] {'x','z','y'}, dimensions={0} | all-to-all | bytes 1048576 | tf_op jit(solution)/shard_map/collect/all_to_all | solution.py:451
  92.5 0.5 project.16.refs_0_
  92.9 0.6 collective-permute-start.1
  93.6 0.5 project.17.refs_1_
  94.0 1.6 %collective-permute-start.2 = (bf16[2,96,512]{2,1,0:T(8,128)(2,1)S(1)}, bf16[2,96,512]{2,1,0:T(8,128)(2,1)S(1)}, u32[]{:S(2)}, u32[]{:S(2)}) collective-permute-start(bf16[2,96,512]{2,1,0:T(8,128)(2,1)S(1)} %project.17.refs_1_), channel_id=1, source_target_pairs={{0,1},{1,0},{2,3},{3,2},{4,5},{5,4},{6,7},{7,6},{8,9},{9,8},{10,11... | collective-permute-start | bytes 589832 | tf_op jit(solution)/shard_map/project/ppermute | solution.py:455
  95.6 0.5 project.18.refs_2_
  96.1 0.6 collective-permute-start.3
  96.7 0.5 project.19.refs_3_
  97.2 1.6 %collective-permute-start.4 = (bf16[2,96,512]{2,1,0:T(8,128)(2,1)S(1)}, bf16[2,96,512]{2,1,0:T(8,128)(2,1)S(1)}, u32[]{:S(2)}, u32[]{:S(2)}) collective-permute-start(bf16[2,96,512]{2,1,0:T(8,128)(2,1)S(1)} %project.19.refs_3_), channel_id=1, source_target_pairs={{0,1},{1,0},{2,3},{3,2},{4,5},{5,4},{6,7},{7,6},{8,9},{9,8},{10,11... | collective-permute-start | bytes 589832 | tf_op jit(solution)/shard_map/project/ppermute | solution.py:455
  98.8 0.5 project.20.refs_4_
  99.2 0.6 collective-permute-start.5
  99.8 0.5 project.14.refs_3_
  100.3 0.5 project.13.refs_2_
  100.8 0.5 project.12.refs_1_
  101.3 0.5 project.11.refs_0_
  101.8 0.5 project.15.refs_4_
  102.2 0.0 collective-permute-done.1.refs_5_
  102.3 1.6 %collective-permute-start.6 = (bf16[2,96,512]{2,1,0:T(8,128)(2,1)S(1)}, bf16[2,96,512]{2,1,0:T(8,128)(2,1)S(1)}, u32[]{:S(2)}, u32[]{:S(2)}) collective-permute-start(bf16[2,96,512]{2,1,0:T(8,128)(2,1)S(1)} %project.11.refs_0_), channel_id=1, source_target_pairs={{0,1},{1,0},{2,3},{3,2},{4,5},{5,4},{6,7},{7,6},{8,9},{9,8},{10,11... | collective-permute-start | bytes 589832 | tf_op jit(solution)/shard_map/project/ppermute | solution.py:457
  103.9 1.2 collective-permute-done.2.refs_6_
  105.1 0.6 collective-permute-start.7
  105.6 3.6 %collective-permute-done.3.refs_7_ = bf16[2,96,512]{2,1,0:T(8,128)(2,1)S(1)} collective-permute-done((bf16[2,96,512]{2,1,0:T(8,128)(2,1)S(1)}, bf16[2,96,512]{2,1,0:T(8,128)(2,1)S(1)}, u32[]{:S(2)}, u32[]{:S(2)}) %collective-permute-start.3) | collective-permute-done | bytes 196640 | tf_op jit(solution)/shard_map/project/ppermute | solution.py:455
  109.3 0.6 collective-permute-start.8
  109.8 3.6 %collective-permute-done.4.refs_8_ = bf16[2,96,512]{2,1,0:T(8,128)(2,1)S(1)} collective-permute-done((bf16[2,96,512]{2,1,0:T(8,128)(2,1)S(1)}, bf16[2,96,512]{2,1,0:T(8,128)(2,1)S(1)}, u32[]{:S(2)}, u32[]{:S(2)}) %collective-permute-start.4) | collective-permute-done | bytes 196640 | tf_op jit(solution)/shard_map/project/ppermute | solution.py:455
  113.5 0.6 collective-permute-start.9
  114.1 3.6 %collective-permute-done.5.refs_9_ = bf16[2,96,512]{2,1,0:T(8,128)(2,1)S(1)} collective-permute-done((bf16[2,96,512]{2,1,0:T(8,128)(2,1)S(1)}, bf16[2,96,512]{2,1,0:T(8,128)(2,1)S(1)}, u32[]{:S(2)}, u32[]{:S(2)}) %collective-permute-start.5) | collective-permute-done | bytes 196640 | tf_op jit(solution)/shard_map/project/ppermute | solution.py:455
  117.7 1.8 %project.21 = (bf16[2,96,512]{2,1,0:T(8,128)(2,1)S(1)}, f32[96,2560]{1,0:T(8,128)S(1)}, f32[96,2560]{1,0:T(8,128)S(1)}, f32[96,128]{1,0:T(8,128)S(1)}, f32[4,96,...) custom-call(bf16[2,96,512]{2,1,0:T(8,128)(2,1)S(1)} %project.11.refs_0_, ...), custom_call_target="tpu_custom_call", output_to_operand_aliasing={{0}: (4, {})} | custom-call | tf_op jit(solution)/shard_map/project/pallas_call | solution.py:378
  119.5 0.6 collective-permute-start.10
  120.2 1.8 %collective-permute-done.6.refs_5_ = bf16[2,96,512]{2,1,0:T(8,128)(2,1)S(1)} collective-permute-done((bf16[2,96,512]{2,1,0:T(8,128)(2,1)S(1)}, bf16[2,96,512]{2,1,0:T(8,128)(2,1)S(1)}, u32[]{:S(2)}, u32[]{:S(2)}) %collective-permute-start.6) | collective-permute-done | bytes 196640 | tf_op jit(solution)/shard_map/project/ppermute | solution.py:457
  121.9 4.2 %collective-permute-done.7.refs_6_ = bf16[2,96,512]{2,1,0:T(8,128)(2,1)S(1)} collective-permute-done((bf16[2,96,512]{2,1,0:T(8,128)(2,1)S(1)}, bf16[2,96,512]{2,1,0:T(8,128)(2,1)S(1)}, u32[]{:S(2)}, u32[]{:S(2)}) %collective-permute-start.7) | collective-permute-done | bytes 196640 | tf_op jit(solution)/shard_map/project/ppermute | solution.py:457
  126.1 4.2 %collective-permute-done.8.refs_7_ = bf16[2,96,512]{2,1,0:T(8,128)(2,1)S(1)} collective-permute-done((bf16[2,96,512]{2,1,0:T(8,128)(2,1)S(1)}, bf16[2,96,512]{2,1,0:T(8,128)(2,1)S(1)}, u32[]{:S(2)}, u32[]{:S(2)}) %collective-permute-start.8) | collective-permute-done | bytes 196640 | tf_op jit(solution)/shard_map/project/ppermute | solution.py:457
  130.3 3.5 %collective-permute-done.9.refs_8_ = bf16[2,96,512]{2,1,0:T(8,128)(2,1)S(1)} collective-permute-done((bf16[2,96,512]{2,1,0:T(8,128)(2,1)S(1)}, bf16[2,96,512]{2,1,0:T(8,128)(2,1)S(1)}, u32[]{:S(2)}, u32[]{:S(2)}) %collective-permute-start.9) | collective-permute-done | bytes 196640 | tf_op jit(solution)/shard_map/project/ppermute | solution.py:457
  133.9 2.1 %collective-permute-done.10.refs_9_ = bf16[2,96,512]{2,1,0:T(8,128)(2,1)S(1)} collective-permute-done((bf16[2,96,512]{2,1,0:T(8,128)(2,1)S(1)}, bf16[2,96,512]{2,1,0:T(8,128)(2,1)S(1)}, u32[]{:S(2)}, u32[]{:S(2)}) %collective-permute-start.10) | collective-permute-done | bytes 196640 | tf_op jit(solution)/shard_map/project/ppermute | solution.py:459
  136.0 2.9 %norm.1 = (bf16[96,5120]{1,0:T(8,128)(2,1)}, bf16[96,5120]{1,0:T(8,128)(2,1)}) custom-call(s32[1]{0:T(128)} %bitcast.side_ref.refs_0_, bf16[2,96,512]{2,1,0:T(8,128)(2,1)S(1)} %project.16.refs_0_, bf16[2,96,512]{2,1,0:T(8,128)(2,1)S(1)} %project.17.refs_1_, bf16[2,96,512]{2,1,0:T(8,128)(2,1)S(1)} %project.18.refs_2_, ...), custom_call_target="tpu_custom_call" | custom-call | tf_op jit(solution)/shard_map/norm/pallas_call | solution.py:420
Async XLA Ops:
  62.3 6.6 %collective-permute-start = (bf16[32,464,128]{2,1,0:T(8,128)(2,1)S(1)}, bf16[32,464,128]{2,1,0:T(8,128)(2,1)S(1)}, u32[]{:S(2)}, u32[]{:S(2)}) collective-permute-start(bf16[32,464,128]{2,1,0:T(8,128)(2,1)S(1)} %all_to_all.10.refs_0_.refs_1_), channel_id=1, source_target_pairs={{0,2},{2,0},{1,3},{3,1},{4,6},{6,4},{5,7},{7,5},{8,10},{10,8},{9,1... | collective-permute-start | bytes 11403272 | tf_op jit(solution)/shard_map/spread/ppermute | solution.py:444
  92.9 9.3 %collective-permute-start.1 = (bf16[2,96,512]{2,1,0:T(8,128)(2,1)S(1)}, bf16[2,96,512]{2,1,0:T(8,128)(2,1)S(1)}, u32[]{:S(2)}, u32[]{:S(2)}) collective-permute-start(bf16[2,96,512]{2,1,0:T(8,128)(2,1)S(1)} %project.16.refs_0_), channel_id=1, source_target_pairs={{0,1},{1,0},{2,3},{3,2},{4,5},{5,4},{6,7},{7,6},{8,9},{9,8},{10,11... | collective-permute-start | bytes 589832 | tf_op jit(solution)/shard_map/project/ppermute | solution.py:455
  94.0 11.0 %collective-permute-start.2 = (bf16[2,96,512]{2,1,0:T(8,128)(2,1)S(1)}, bf16[2,96,512]{2,1,0:T(8,128)(2,1)S(1)}, u32[]{:S(2)}, u32[]{:S(2)}) collective-permute-start(bf16[2,96,512]{2,1,0:T(8,128)(2,1)S(1)} %project.17.refs_1_), channel_id=1, source_target_pairs={{0,1},{1,0},{2,3},{3,2},{4,5},{5,4},{6,7},{7,6},{8,9},{9,8},{10,11... | collective-permute-start | bytes 589832 | tf_op jit(solution)/shard_map/project/ppermute | solution.py:455
  96.1 13.2 %collective-permute-start.3 = (bf16[2,96,512]{2,1,0:T(8,128)(2,1)S(1)}, bf16[2,96,512]{2,1,0:T(8,128)(2,1)S(1)}, u32[]{:S(2)}, u32[]{:S(2)}) collective-permute-start(bf16[2,96,512]{2,1,0:T(8,128)(2,1)S(1)} %project.18.refs_2_), channel_id=1, source_target_pairs={{0,1},{1,0},{2,3},{3,2},{4,5},{5,4},{6,7},{7,6},{8,9},{9,8},{10,11... | collective-permute-start | bytes 589832 | tf_op jit(solution)/shard_map/project/ppermute | solution.py:455
  97.2 16.3 %collective-permute-start.4 = (bf16[2,96,512]{2,1,0:T(8,128)(2,1)S(1)}, bf16[2,96,512]{2,1,0:T(8,128)(2,1)S(1)}, u32[]{:S(2)}, u32[]{:S(2)}) collective-permute-start(bf16[2,96,512]{2,1,0:T(8,128)(2,1)S(1)} %project.19.refs_3_), channel_id=1, source_target_pairs={{0,1},{1,0},{2,3},{3,2},{4,5},{5,4},{6,7},{7,6},{8,9},{9,8},{10,11... | collective-permute-start | bytes 589832 | tf_op jit(solution)/shard_map/project/ppermute | solution.py:455
  99.2 18.5 %collective-permute-start.5 = (bf16[2,96,512]{2,1,0:T(8,128)(2,1)S(1)}, bf16[2,96,512]{2,1,0:T(8,128)(2,1)S(1)}, u32[]{:S(2)}, u32[]{:S(2)}) collective-permute-start(bf16[2,96,512]{2,1,0:T(8,128)(2,1)S(1)} %project.20.refs_4_), channel_id=1, source_target_pairs={{0,1},{1,0},{2,3},{3,2},{4,5},{5,4},{6,7},{7,6},{8,9},{9,8},{10,11... | collective-permute-start | bytes 589832 | tf_op jit(solution)/shard_map/project/ppermute | solution.py:455
  102.3 19.7 %collective-permute-start.6 = (bf16[2,96,512]{2,1,0:T(8,128)(2,1)S(1)}, bf16[2,96,512]{2,1,0:T(8,128)(2,1)S(1)}, u32[]{:S(2)}, u32[]{:S(2)}) collective-permute-start(bf16[2,96,512]{2,1,0:T(8,128)(2,1)S(1)} %project.11.refs_0_), channel_id=1, source_target_pairs={{0,1},{1,0},{2,3},{3,2},{4,5},{5,4},{6,7},{7,6},{8,9},{9,8},{10,11... | collective-permute-start | bytes 589832 | tf_op jit(solution)/shard_map/project/ppermute | solution.py:457
  105.1 21.1 %collective-permute-start.7 = (bf16[2,96,512]{2,1,0:T(8,128)(2,1)S(1)}, bf16[2,96,512]{2,1,0:T(8,128)(2,1)S(1)}, u32[]{:S(2)}, u32[]{:S(2)}) collective-permute-start(bf16[2,96,512]{2,1,0:T(8,128)(2,1)S(1)} %project.12.refs_1_), channel_id=1, source_target_pairs={{0,1},{1,0},{2,3},{3,2},{4,5},{5,4},{6,7},{7,6},{8,9},{9,8},{10,11... | collective-permute-start | bytes 589832 | tf_op jit(solution)/shard_map/project/ppermute | solution.py:457
  109.3 21.1 %collective-permute-start.8 = (bf16[2,96,512]{2,1,0:T(8,128)(2,1)S(1)}, bf16[2,96,512]{2,1,0:T(8,128)(2,1)S(1)}, u32[]{:S(2)}, u32[]{:S(2)}) collective-permute-start(bf16[2,96,512]{2,1,0:T(8,128)(2,1)S(1)} %project.13.refs_2_), channel_id=1, source_target_pairs={{0,1},{1,0},{2,3},{3,2},{4,5},{5,4},{6,7},{7,6},{8,9},{9,8},{10,11... | collective-permute-start | bytes 589832 | tf_op jit(solution)/shard_map/project/ppermute | solution.py:457
  113.5 20.4 %collective-permute-start.9 = (bf16[2,96,512]{2,1,0:T(8,128)(2,1)S(1)}, bf16[2,96,512]{2,1,0:T(8,128)(2,1)S(1)}, u32[]{:S(2)}, u32[]{:S(2)}) collective-permute-start(bf16[2,96,512]{2,1,0:T(8,128)(2,1)S(1)} %project.14.refs_3_), channel_id=1, source_target_pairs={{0,1},{1,0},{2,3},{3,2},{4,5},{5,4},{6,7},{7,6},{8,9},{9,8},{10,11... | collective-permute-start | bytes 589832 | tf_op jit(solution)/shard_map/project/ppermute | solution.py:457
  119.5 16.5 %collective-permute-start.10 = (bf16[2,96,512]{2,1,0:T(8,128)(2,1)S(1)}, bf16[2,96,512]{2,1,0:T(8,128)(2,1)S(1)}, u32[]{:S(2)}, u32[]{:S(2)}) collective-permute-start(bf16[2,96,512]{2,1,0:T(8,128)(2,1)S(1)} %get-tuple-element.41), channel_id=1, source_target_pairs={{0,1},{1,0},{2,3},{3,2},{4,5},{5,4},{6,7},{7,6},{8,9},{9,8},{10,11... | collective-permute-start | bytes 589832 | tf_op jit(solution)/shard_map/project/ppermute | solution.py:459

commit v9 on v8

--- a/solution.py
+++ b/solution.py
@@ -49,9 +49,12 @@
 
 def pack_kernel(side_ref, q_hbm, k_hbm, v_hbm, qt_hbm, kt_hbm, vt_hbm, freq_ref, pos_ref, seg_ref, out_ref, tag_ref, held_ref, sem_in):
     del side_ref
-    reads = [pltpu.make_async_copy(x, held_ref.at[i], sem_in.at[i]) for i, x in enumerate((q_hbm, k_hbm, v_hbm, qt_hbm, kt_hbm, vt_hbm))]
-    for copy in reads:
-        copy.start()
+    reads = []
+    for part in range(NH // SPAN):
+        cols = slice(part * SPAN * HD, (part + 1) * SPAN * HD)
+        for i, x in enumerate((q_hbm, k_hbm, v_hbm, qt_hbm, kt_hbm, vt_hbm)):
+            reads.append(pltpu.make_async_copy(x.at[:, cols], held_ref.at[i, :, cols], sem_in.at[part, i]))
+            reads[-1].start()
     lane = lax.broadcasted_iota(i32, (ROWS, HD), 1)
     eye = lane == lax.broadcasted_iota(i32, (ROWS, HD), 0)
     pad = jnp.zeros((1, HD - ROWS), f32)
@@ -76,10 +79,11 @@
         y = x * cos + jnp.roll(x, HD // 2, axis=1) * sin
         return (y if factor is None else y * factor).astype(bf16)
 
-    for copy in reads:
-        copy.wait()
     writes = []
     for h in range(NH):
+        if h % SPAN == 0:
+            for copy in reads[h // SPAN * 6 : h // SPAN * 6 + 6]:
+                copy.wait()
         cols = slice(h * HD, (h + 1) * HD)
         q, k = rot(0, cols, exp_scale), rot(1, cols, None)
         qt, kt = rot(3, cols, exp_scale), rot(4, cols, None)
@@ -114,7 +118,7 @@
         out_shape=[pltpu.VMEM((CHIPS, MSG, HD), bf16), pltpu.VMEM((ROWS, HD), f32)],
         scratch_shapes=[
             pltpu.VMEM((6, ROWS, NH * HD), bf16),
-            pltpu.SemaphoreType.DMA((6,)),
+            pltpu.SemaphoreType.DMA((NH // SPAN, 6)),
         ],
         compiler_params=params(40),
     )(side, *[in_hbm(x) for x in (*arrays, freq, positions, segments)])
@@ -440,7 +444,7 @@
         arrays = (queries, keys, values, queries_tan, keys_tan, values_tan)
         message, seg = pack(side, arrays, freq, positions[None, :], segments[None, :])
     with jax.named_scope("spread"):
-        arrived = lax.all_to_all(message, ("x", "z", "y"), 0, 0, tiled=True)
+        arrived = lax.all_to_all(message, ("x", "y", "z"), 0, 0, tiled=True)
         swapped = lax.ppermute(arrived, "c", swap)
     with jax.named_scope("attend"):
         later = (out_weight, gate, gate_tan, residual, residual_tan, mod_scale, mod_scale_tan, mod_shift, mod_shift_tan)
@@ -448,7 +452,7 @@
         held_weight, held_gate, held_gate_tan, held_resid, held_resid_tan, *tables = later
         answer = attend_more(arrived, swapped, state)
     with jax.named_scope("collect"):
-        attended = lax.all_to_all(answer, ("x", "z", "y"), 0, 0, tiled=True)
+        attended = lax.all_to_all(answer, ("x", "y", "z"), 0, 0, tiled=True)
     with jax.named_scope("project"):
         args = (attended, held_weight, seg, held_gate, held_gate_tan)
         other = [project(side, *args, (), part) for part in range(SENDS)]

time: 139 us -> 139 us (level)
  no operation moved by 1% of the time
where the time goes in v9:
time: 139 us
  blocking collectives  76.1 us (55%)
  waiting for transfers between devices  28.1 us (20%)
  Pallas kernels  24.3 us (17%)
  starting transfers between devices  9.33 us (7%)
    all_to_all x1, blocking collectives, body(): arrived = lax.all_to_all(message, ('x', 'y', 'z'), 0, 0, tiled=True)  58.6 us
    all_to_all x1, blocking collectives, body(): attended = lax.all_to_all(answer, ('x', 'y', 'z'), 0, 0, tiled=True)  17.5 us
    ppermute x4, waiting for transfers between devices, body(): got_other = [lax.ppermute(x, 'head', swap) for x in mine[:-1]]  13.4 us
    ppermute x5, waiting for transfers between devices, body(): got_mine = [lax.ppermute(x, 'head', swap) for x in other]  11.9 us
    pallas_call x1, Pallas kernels, attend_more(): pl.pallas_call(lambda *refs: attn_kernel(*refs, second=True), in_specs=[V...  6.33 us
    pallas_call x1, Pallas kernels, attend(): pl.pallas_call(lambda *refs: attn_kernel(*refs, second=False), in_specs=[...  5.83 us
    ppermute x5, starting transfers between devices, body(): got_mine = [lax.ppermute(x, 'head', swap) for x in other]  5.09 us
    pallas_call x10, Pallas kernels, project(): pl.pallas_call(lambda *refs: project_kernel(*refs, own=own, part=part), i...  4.73 us
  transfers between devices with their start and end apart: 11, of which 10 were waited for; matrix products, arithmetic and copies ran while one was open for 0% of the time, Pallas kernels for 9%

profile of v9, /device:TPU:0, one launch (start us, length us, event | category | flops | bytes accessed | tf_op | source)
XLA Modules:
  0.0 138.7 jit_solution(14576821367126180097)
XLA Ops:
  0.6 2.7 %pack.1 = (bf16[32,464,128]{2,1,0:T(8,128)(2,1)S(1)}, f32[96,128]{1,0:T(8,128)S(1)}) custom-call(s32[1]{0:T(128)} %bitcast.side_ref.refs_0_, bf16[96,1280]{1,0:T(8,128)(2,1)} %q_hbm.1, bf16[96,1280]{1,0:T(8,128)(2,1)} %k_hbm.1, bf16[96,1280]{1,0:T(8,128)(2,1)} %v_hbm.1, bf16[96,1280]{1,0:T(8,128)(2,1)} %qt_hbm.1, bf16[96,1280]{1,0:T(8,128)(2,1)} %kt_hbm.1, ...), custom_call_target="tpu_custom_call" | custom-call | tf_op jit(solution)/shard_map/pack/pallas_call | solution.py:114
  3.4 58.6 %all_to_all.10.refs_0_.refs_1_ = bf16[32,464,128]{2,1,0:T(8,128)(2,1)S(1)} all-to-all(bf16[32,464,128]{2,1,0:T(8,128)(2,1)S(1)} %get-tuple-element.26), channel_id=1, replica_groups=mesh['z'=4,'y'=4,'x'=2,'c'=2,'head'=2] {'x','y','z'}, dimensions={0} | all-to-all | bytes 7602176 | tf_op jit(solution)/shard_map/spread/all_to_all | solution.py:447
  62.0 0.0 collective-permute-start
  62.0 5.8 %attend.2 = (f32[1088,512]{1,0:T(8,128)S(1)}, f32[1088,256]{1,0:T(8,128)S(1)}, bf16[1280,5120]{1,0:T(8,128)(2,1)S(1)}, f32[2,5120]{1,0:T(2,128)S(1)}, f32[2,5120...) custom-call(bf16[32,464,128]{2,1,0:T(8,128)(2,1)S(1)} %all_to_all.10, ...), custom_call_target="tpu_custom_call" | custom-call | flops 5000000000 | bytes 20971520 | tf_op jit(solution)/shard_map/attend/pallas_call | solution.py:274
  67.8 0.8 collective-permute-done.refs_1_
  68.6 6.3 %attend.3 = bf16[32,32,256]{2,1,0:T(8,128)(2,1)S(1)} custom-call(bf16[32,464,128]{2,1,0:T(8,128)(2,1)S(1)} %all_to_all.10.refs_0_.refs_1_, bf16[32,464,128]{2,1,0:T(8,128)(2,1)S(1)} %collective-permute-done.refs_1_, f32[1088,512]{1,0:T(8,128)S(1)} %get-tuple-element.27.refs_2_, f32[1088,256]{1,0:T(8,128)S(1)} %get-tuple-element.28.refs_3_), custom_call_target="tpu_custom_call" | custom-call | flops 5000000000 | bytes 8388608 | tf_op jit(solution)/shard_map/attend/pallas_call | solution.py:287
  74.9 17.5 %all_to_all.11.refs_1_ = bf16[32,32,256]{2,1,0:T(8,128)(2,1)S(1)} all-to-all(bf16[32,32,256]{2,1,0:T(8,128)(2,1)S(1)} %attend.3), channel_id=1, replica_groups=mesh['z'=4,'y'=4,'x'=2,'c'=2,'head'=2] {'x','y','z'}, dimensions={0} | all-to-all | bytes 1048576 | tf_op jit(solution)/shard_map/collect/all_to_all | solution.py:455
  92.4 0.5 project.16.refs_0_
  92.9 0.7 collective-permute-start.1
  93.6 0.5 project.17.refs_1_
  94.1 1.5 %collective-permute-start.2 = (bf16[2,96,512]{2,1,0:T(8,128)(2,1)S(1)}, bf16[2,96,512]{2,1,0:T(8,128)(2,1)S(1)}, u32[]{:S(2)}, u32[]{:S(2)}) collective-permute-start(bf16[2,96,512]{2,1,0:T(8,128)(2,1)S(1)} %project.17.refs_1_), channel_id=1, source_target_pairs={{0,1},{1,0},{2,3},{3,2},{4,5},{5,4},{6,7},{7,6},{8,9},{9,8},{10,11... | collective-permute-start | bytes 589832 | tf_op jit(solution)/shard_map/project/ppermute | solution.py:459
  95.6 0.5 project.18.refs_2_
  96.0 0.7 collective-permute-start.3
  96.8 0.5 project.19.refs_3_
  97.2 1.5 %collective-permute-start.4 = (bf16[2,96,512]{2,1,0:T(8,128)(2,1)S(1)}, bf16[2,96,512]{2,1,0:T(8,128)(2,1)S(1)}, u32[]{:S(2)}, u32[]{:S(2)}) collective-permute-start(bf16[2,96,512]{2,1,0:T(8,128)(2,1)S(1)} %project.19.refs_3_), channel_id=1, source_target_pairs={{0,1},{1,0},{2,3},{3,2},{4,5},{5,4},{6,7},{7,6},{8,9},{9,8},{10,11... | collective-permute-start | bytes 589832 | tf_op jit(solution)/shard_map/project/ppermute | solution.py:459
  98.7 0.5 project.20.refs_4_
  99.2 0.7 collective-permute-start.5
  99.9 0.5 project.14.refs_3_
  100.4 0.5 project.13.refs_2_
  100.8 0.5 project.12.refs_1_
  101.3 0.5 project.11.refs_0_
  101.8 0.5 project.15.refs_4_
  102.3 0.0 collective-permute-done.1.refs_5_
  102.3 1.5 %collective-permute-start.6 = (bf16[2,96,512]{2,1,0:T(8,128)(2,1)S(1)}, bf16[2,96,512]{2,1,0:T(8,128)(2,1)S(1)}, u32[]{:S(2)}, u32[]{:S(2)}) collective-permute-start(bf16[2,96,512]{2,1,0:T(8,128)(2,1)S(1)} %project.11.refs_0_), channel_id=1, source_target_pairs={{0,1},{1,0},{2,3},{3,2},{4,5},{5,4},{6,7},{7,6},{8,9},{9,8},{10,11... | collective-permute-start | bytes 589832 | tf_op jit(solution)/shard_map/project/ppermute | solution.py:461
  103.8 1.2 collective-permute-done.2.refs_6_
  105.0 0.7 collective-permute-start.7
  105.7 3.5 %collective-permute-done.3.refs_7_ = bf16[2,96,512]{2,1,0:T(8,128)(2,1)S(1)} collective-permute-done((bf16[2,96,512]{2,1,0:T(8,128)(2,1)S(1)}, bf16[2,96,512]{2,1,0:T(8,128)(2,1)S(1)}, u32[]{:S(2)}, u32[]{:S(2)}) %collective-permute-start.3) | collective-permute-done | bytes 196640 | tf_op jit(solution)/shard_map/project/ppermute | solution.py:459
  109.2 0.7 collective-permute-start.8
  109.9 3.5 %collective-permute-done.4.refs_8_ = bf16[2,96,512]{2,1,0:T(8,128)(2,1)S(1)} collective-permute-done((bf16[2,96,512]{2,1,0:T(8,128)(2,1)S(1)}, bf16[2,96,512]{2,1,0:T(8,128)(2,1)S(1)}, u32[]{:S(2)}, u32[]{:S(2)}) %collective-permute-start.4) | collective-permute-done | bytes 196640 | tf_op jit(solution)/shard_map/project/ppermute | solution.py:459
  113.4 0.7 collective-permute-start.9
  114.1 3.5 %collective-permute-done.5.refs_9_ = bf16[2,96,512]{2,1,0:T(8,128)(2,1)S(1)} collective-permute-done((bf16[2,96,512]{2,1,0:T(8,128)(2,1)S(1)}, bf16[2,96,512]{2,1,0:T(8,128)(2,1)S(1)}, u32[]{:S(2)}, u32[]{:S(2)}) %collective-permute-start.5) | collective-permute-done | bytes 196640 | tf_op jit(solution)/shard_map/project/ppermute | solution.py:459
  117.7 1.8 %project.21 = (bf16[2,96,512]{2,1,0:T(8,128)(2,1)S(1)}, f32[96,2560]{1,0:T(8,128)S(1)}, f32[96,2560]{1,0:T(8,128)S(1)}, f32[96,128]{1,0:T(8,128)S(1)}, f32[4,96,...) custom-call(bf16[2,96,512]{2,1,0:T(8,128)(2,1)S(1)} %project.11.refs_0_, ...), custom_call_target="tpu_custom_call", output_to_operand_aliasing={{0}: (4, {})} | custom-call | tf_op jit(solution)/shard_map/project/pallas_call | solution.py:382
  119.5 0.7 collective-permute-start.10
  120.2 1.7 %collective-permute-done.6.refs_5_ = bf16[2,96,512]{2,1,0:T(8,128)(2,1)S(1)} collective-permute-done((bf16[2,96,512]{2,1,0:T(8,128)(2,1)S(1)}, bf16[2,96,512]{2,1,0:T(8,128)(2,1)S(1)}, u32[]{:S(2)}, u32[]{:S(2)}) %collective-permute-start.6) | collective-permute-done | bytes 196640 | tf_op jit(solution)/shard_map/project/ppermute | solution.py:461
  121.9 4.2 %collective-permute-done.7.refs_6_ = bf16[2,96,512]{2,1,0:T(8,128)(2,1)S(1)} collective-permute-done((bf16[2,96,512]{2,1,0:T(8,128)(2,1)S(1)}, bf16[2,96,512]{2,1,0:T(8,128)(2,1)S(1)}, u32[]{:S(2)}, u32[]{:S(2)}) %collective-permute-start.7) | collective-permute-done | bytes 196640 | tf_op jit(solution)/shard_map/project/ppermute | solution.py:461
  126.1 4.2 %collective-permute-done.8.refs_7_ = bf16[2,96,512]{2,1,0:T(8,128)(2,1)S(1)} collective-permute-done((bf16[2,96,512]{2,1,0:T(8,128)(2,1)S(1)}, bf16[2,96,512]{2,1,0:T(8,128)(2,1)S(1)}, u32[]{:S(2)}, u32[]{:S(2)}) %collective-permute-start.8) | collective-permute-done | bytes 196640 | tf_op jit(solution)/shard_map/project/ppermute | solution.py:461
  130.3 3.3 %collective-permute-done.9.refs_8_ = bf16[2,96,512]{2,1,0:T(8,128)(2,1)S(1)} collective-permute-done((bf16[2,96,512]{2,1,0:T(8,128)(2,1)S(1)}, bf16[2,96,512]{2,1,0:T(8,128)(2,1)S(1)}, u32[]{:S(2)}, u32[]{:S(2)}) %collective-permute-start.9) | collective-permute-done | bytes 196640 | tf_op jit(solution)/shard_map/project/ppermute | solution.py:461
  133.6 2.1 %collective-permute-done.10.refs_9_ = bf16[2,96,512]{2,1,0:T(8,128)(2,1)S(1)} collective-permute-done((bf16[2,96,512]{2,1,0:T(8,128)(2,1)S(1)}, bf16[2,96,512]{2,1,0:T(8,128)(2,1)S(1)}, u32[]{:S(2)}, u32[]{:S(2)}) %collective-permute-start.10) | collective-permute-done | bytes 196640 | tf_op jit(solution)/shard_map/project/ppermute | solution.py:463
  135.7 2.9 %norm.1 = (bf16[96,5120]{1,0:T(8,128)(2,1)}, bf16[96,5120]{1,0:T(8,128)(2,1)}) custom-call(s32[1]{0:T(128)} %bitcast.side_ref.refs_0_, bf16[2,96,512]{2,1,0:T(8,128)(2,1)S(1)} %project.16.refs_0_, bf16[2,96,512]{2,1,0:T(8,128)(2,1)S(1)} %project.17.refs_1_, bf16[2,96,512]{2,1,0:T(8,128)(2,1)S(1)} %project.18.refs_2_, ...), custom_call_target="tpu_custom_call" | custom-call | tf_op jit(solution)/shard_map/norm/pallas_call | solution.py:424
Async XLA Ops:
  62.0 6.6 %collective-permute-start = (bf16[32,464,128]{2,1,0:T(8,128)(2,1)S(1)}, bf16[32,464,128]{2,1,0:T(8,128)(2,1)S(1)}, u32[]{:S(2)}, u32[]{:S(2)}) collective-permute-start(bf16[32,464,128]{2,1,0:T(8,128)(2,1)S(1)} %all_to_all.10.refs_0_.refs_1_), channel_id=1, source_target_pairs={{0,2},{2,0},{1,3},{3,1},{4,6},{6,4},{5,7},{7,5},{8,10},{10,8},{9,1... | collective-permute-start | bytes 11403272 | tf_op jit(solution)/shard_map/spread/ppermute | solution.py:448
  92.9 9.4 %collective-permute-start.1 = (bf16[2,96,512]{2,1,0:T(8,128)(2,1)S(1)}, bf16[2,96,512]{2,1,0:T(8,128)(2,1)S(1)}, u32[]{:S(2)}, u32[]{:S(2)}) collective-permute-start(bf16[2,96,512]{2,1,0:T(8,128)(2,1)S(1)} %project.16.refs_0_), channel_id=1, source_target_pairs={{0,1},{1,0},{2,3},{3,2},{4,5},{5,4},{6,7},{7,6},{8,9},{9,8},{10,11... | collective-permute-start | bytes 589832 | tf_op jit(solution)/shard_map/project/ppermute | solution.py:459
  94.1 10.9 %collective-permute-start.2 = (bf16[2,96,512]{2,1,0:T(8,128)(2,1)S(1)}, bf16[2,96,512]{2,1,0:T(8,128)(2,1)S(1)}, u32[]{:S(2)}, u32[]{:S(2)}) collective-permute-start(bf16[2,96,512]{2,1,0:T(8,128)(2,1)S(1)} %project.17.refs_1_), channel_id=1, source_target_pairs={{0,1},{1,0},{2,3},{3,2},{4,5},{5,4},{6,7},{7,6},{8,9},{9,8},{10,11... | collective-permute-start | bytes 589832 | tf_op jit(solution)/shard_map/project/ppermute | solution.py:459
  96.0 13.2 %collective-permute-start.3 = (bf16[2,96,512]{2,1,0:T(8,128)(2,1)S(1)}, bf16[2,96,512]{2,1,0:T(8,128)(2,1)S(1)}, u32[]{:S(2)}, u32[]{:S(2)}) collective-permute-start(bf16[2,96,512]{2,1,0:T(8,128)(2,1)S(1)} %project.18.refs_2_), channel_id=1, source_target_pairs={{0,1},{1,0},{2,3},{3,2},{4,5},{5,4},{6,7},{7,6},{8,9},{9,8},{10,11... | collective-permute-start | bytes 589832 | tf_op jit(solution)/shard_map/project/ppermute | solution.py:459
  97.2 16.2 %collective-permute-start.4 = (bf16[2,96,512]{2,1,0:T(8,128)(2,1)S(1)}, bf16[2,96,512]{2,1,0:T(8,128)(2,1)S(1)}, u32[]{:S(2)}, u32[]{:S(2)}) collective-permute-start(bf16[2,96,512]{2,1,0:T(8,128)(2,1)S(1)} %project.19.refs_3_), channel_id=1, source_target_pairs={{0,1},{1,0},{2,3},{3,2},{4,5},{5,4},{6,7},{7,6},{8,9},{9,8},{10,11... | collective-permute-start | bytes 589832 | tf_op jit(solution)/shard_map/project/ppermute | solution.py:459
  99.2 18.5 %collective-permute-start.5 = (bf16[2,96,512]{2,1,0:T(8,128)(2,1)S(1)}, bf16[2,96,512]{2,1,0:T(8,128)(2,1)S(1)}, u32[]{:S(2)}, u32[]{:S(2)}) collective-permute-start(bf16[2,96,512]{2,1,0:T(8,128)(2,1)S(1)} %project.20.refs_4_), channel_id=1, source_target_pairs={{0,1},{1,0},{2,3},{3,2},{4,5},{5,4},{6,7},{7,6},{8,9},{9,8},{10,11... | collective-permute-start | bytes 589832 | tf_op jit(solution)/shard_map/project/ppermute | solution.py:459
  102.3 19.6 %collective-permute-start.6 = (bf16[2,96,512]{2,1,0:T(8,128)(2,1)S(1)}, bf16[2,96,512]{2,1,0:T(8,128)(2,1)S(1)}, u32[]{:S(2)}, u32[]{:S(2)}) collective-permute-start(bf16[2,96,512]{2,1,0:T(8,128)(2,1)S(1)} %project.11.refs_0_), channel_id=1, source_target_pairs={{0,1},{1,0},{2,3},{3,2},{4,5},{5,4},{6,7},{7,6},{8,9},{9,8},{10,11... | collective-permute-start | bytes 589832 | tf_op jit(solution)/shard_map/project/ppermute | solution.py:461
  105.0 21.1 %collective-permute-start.7 = (bf16[2,96,512]{2,1,0:T(8,128)(2,1)S(1)}, bf16[2,96,512]{2,1,0:T(8,128)(2,1)S(1)}, u32[]{:S(2)}, u32[]{:S(2)}) collective-permute-start(bf16[2,96,512]{2,1,0:T(8,128)(2,1)S(1)} %project.12.refs_1_), channel_id=1, source_target_pairs={{0,1},{1,0},{2,3},{3,2},{4,5},{5,4},{6,7},{7,6},{8,9},{9,8},{10,11... | collective-permute-start | bytes 589832 | tf_op jit(solution)/shard_map/project/ppermute | solution.py:461
  109.2 21.1 %collective-permute-start.8 = (bf16[2,96,512]{2,1,0:T(8,128)(2,1)S(1)}, bf16[2,96,512]{2,1,0:T(8,128)(2,1)S(1)}, u32[]{:S(2)}, u32[]{:S(2)}) collective-permute-start(bf16[2,96,512]{2,1,0:T(8,128)(2,1)S(1)} %project.13.refs_2_), channel_id=1, source_target_pairs={{0,1},{1,0},{2,3},{3,2},{4,5},{5,4},{6,7},{7,6},{8,9},{9,8},{10,11... | collective-permute-start | bytes 589832 | tf_op jit(solution)/shard_map/project/ppermute | solution.py:461
  113.4 20.1 %collective-permute-start.9 = (bf16[2,96,512]{2,1,0:T(8,128)(2,1)S(1)}, bf16[2,96,512]{2,1,0:T(8,128)(2,1)S(1)}, u32[]{:S(2)}, u32[]{:S(2)}) collective-permute-start(bf16[2,96,512]{2,1,0:T(8,128)(2,1)S(1)} %project.14.refs_3_), channel_id=1, source_target_pairs={{0,1},{1,0},{2,3},{3,2},{4,5},{5,4},{6,7},{7,6},{8,9},{9,8},{10,11... | collective-permute-start | bytes 589832 | tf_op jit(solution)/shard_map/project/ppermute | solution.py:461
  119.5 16.2 %collective-permute-start.10 = (bf16[2,96,512]{2,1,0:T(8,128)(2,1)S(1)}, bf16[2,96,512]{2,1,0:T(8,128)(2,1)S(1)}, u32[]{:S(2)}, u32[]{:S(2)}) collective-permute-start(bf16[2,96,512]{2,1,0:T(8,128)(2,1)S(1)} %get-tuple-element.41), channel_id=1, source_target_pairs={{0,1},{1,0},{2,3},{3,2},{4,5},{5,4},{6,7},{7,6},{8,9},{9,8},{10,11... | collective-permute-start | bytes 589832 | tf_op jit(solution)/shard_map/project/ppermute | solution.py:463

commit v10 on v9

--- a/solution.py
+++ b/solution.py
@@ -295,8 +295,8 @@
     )(*[in_vmem(x) for x in (arrived, swapped, *state)])
 
 
-CT = 512
-SENDS = 5
+CT = 256
+SENDS = 10
 PIECE = HALF // SENDS
 STEPS = PIECE // CT
 

time: 139 us -> 139 us (level)
  waiting for transfers between devices: 28.1 us -> 11.6 us
  starting transfers between devices: 9.33 us -> 23.5 us
  Pallas kernels: 24.3 us -> 26.5 us
    ppermute x5 -> x10, waiting for transfers between devices: 11.9 us -> 2.99 us  [body(): got_mine = [lax.ppermute(x, 'head', swap) for x in other]]
    ppermute x4 -> x9, starting transfers between devices: 3.5 us -> 11.6 us  [body(): got_other = [lax.ppermute(x, 'head', swap) for x in mine[:-1]]]
    ppermute x4 -> x9, waiting for transfers between devices: 13.4 us -> 6.83 us  [body(): got_other = [lax.ppermute(x, 'head', swap) for x in mine[:-1]]]
    ppermute x5 -> x10, starting transfers between devices: 5.09 us -> 10.6 us  [body(): got_mine = [lax.ppermute(x, 'head', swap) for x in other]]
    pallas_call x10 -> x20, Pallas kernels: 4.73 us -> 6.97 us  [project(): pl.pallas_call(lambda *refs: project_kernel(*refs, own=own, part=part), i...]
  transfers between devices with their start and end apart: 11 -> 21, of which waited for: 10 -> 13; matrix products, arithmetic and copies ran while one was open for 0% -> 0% of each run, Pallas kernels for 9% -> 10%
where the time goes in v10:
time: 139 us
  blocking collectives  76.1 us (55%)
  Pallas kernels  26.5 us (19%)
  starting transfers between devices  23.5 us (17%)
  waiting for transfers between devices  11.6 us (8%)
    all_to_all x1, blocking collectives, body(): arrived = lax.all_to_all(message, ('x', 'y', 'z'), 0, 0, tiled=True)  58.6 us
    all_to_all x1, blocking collectives, body(): attended = lax.all_to_all(answer, ('x', 'y', 'z'), 0, 0, tiled=True)  17.4 us
    ppermute x9, starting transfers between devices, body(): got_other = [lax.ppermute(x, 'head', swap) for x in mine[:-1]]  11.6 us
    ppermute x10, starting transfers between devices, body(): got_mine = [lax.ppermute(x, 'head', swap) for x in other]  10.6 us
    pallas_call x20, Pallas kernels, project(): pl.pallas_call(lambda *refs: project_kernel(*refs, own=own, part=part), i...  6.97 us
    ppermute x9, waiting for transfers between devices, body(): got_other = [lax.ppermute(x, 'head', swap) for x in mine[:-1]]  6.83 us
    pallas_call x1, Pallas kernels, attend_more(): pl.pallas_call(lambda *refs: attn_kernel(*refs, second=True), in_specs=[V...  6.3 us
    pallas_call x1, Pallas kernels, attend(): pl.pallas_call(lambda *refs: attn_kernel(*refs, second=False), in_specs=[...  5.84 us
  transfers between devices with their start and end apart: 21, of which 13 were waited for; matrix products, arithmetic and copies ran while one was open for 0% of the time, Pallas kernels for 10%

profile of v10, /device:TPU:0, one launch (start us, length us, event | category | flops | bytes accessed | tf_op | source)
XLA Modules:
  0.0 138.7 jit_solution(6312525425418356553)
XLA Ops:
  0.6 2.7 %pack.1 = (bf16[32,464,128]{2,1,0:T(8,128)(2,1)S(1)}, f32[96,128]{1,0:T(8,128)S(1)}) custom-call(s32[1]{0:T(128)} %bitcast.side_ref.refs_0_, bf16[96,1280]{1,0:T(8,128)(2,1)} %q_hbm.1, bf16[96,1280]{1,0:T(8,128)(2,1)} %k_hbm.1, bf16[96,1280]{1,0:T(8,128)(2,1)} %v_hbm.1, bf16[96,1280]{1,0:T(8,128)(2,1)} %qt_hbm.1, bf16[96,1280]{1,0:T(8,128)(2,1)} %kt_hbm.1, ...), custom_call_target="tpu_custom_call" | custom-call | tf_op jit(solution)/shard_map/pack/pallas_call | solution.py:114
  3.4 58.6 %all_to_all.10.refs_0_.refs_1_ = bf16[32,464,128]{2,1,0:T(8,128)(2,1)S(1)} all-to-all(bf16[32,464,128]{2,1,0:T(8,128)(2,1)S(1)} %get-tuple-element.26), channel_id=1, replica_groups=mesh['z'=4,'y'=4,'x'=2,'c'=2,'head'=2] {'x','y','z'}, dimensions={0} | all-to-all | bytes 7602176 | tf_op jit(solution)/shard_map/spread/all_to_all | solution.py:447
  62.0 5.8 %attend.2 = (f32[1088,512]{1,0:T(8,128)S(1)}, f32[1088,256]{1,0:T(8,128)S(1)}, bf16[1280,5120]{1,0:T(8,128)(2,1)S(1)}, f32[2,5120]{1,0:T(2,128)S(1)}, f32[2,5120...) custom-call(bf16[32,464,128]{2,1,0:T(8,128)(2,1)S(1)} %all_to_all.10, ...), custom_call_target="tpu_custom_call" | custom-call | flops 5000000000 | bytes 20971520 | tf_op jit(solution)/shard_map/attend/pallas_call | solution.py:274
  67.9 0.7 collective-permute-done.refs_1_
  68.6 6.3 %attend.3 = bf16[32,32,256]{2,1,0:T(8,128)(2,1)S(1)} custom-call(bf16[32,464,128]{2,1,0:T(8,128)(2,1)S(1)} %all_to_all.10.refs_0_.refs_1_, bf16[32,464,128]{2,1,0:T(8,128)(2,1)S(1)} %collective-permute-done.refs_1_, f32[1088,512]{1,0:T(8,128)S(1)} %get-tuple-element.27.refs_2_, f32[1088,256]{1,0:T(8,128)S(1)} %get-tuple-element.28.refs_3_), custom_call_target="tpu_custom_call" | custom-call | flops 5000000000 | bytes 8388608 | tf_op jit(solution)/shard_map/attend/pallas_call | solution.py:287
  74.9 17.4 %all_to_all.11.refs_1_ = bf16[32,32,256]{2,1,0:T(8,128)(2,1)S(1)} all-to-all(bf16[32,32,256]{2,1,0:T(8,128)(2,1)S(1)} %attend.3), channel_id=1, replica_groups=mesh['z'=4,'y'=4,'x'=2,'c'=2,'head'=2] {'x','y','z'}, dimensions={0} | all-to-all | bytes 1048576 | tf_op jit(solution)/shard_map/collect/all_to_all | solution.py:455
  92.7 0.7 collective-permute-start.1
  93.8 1.4 %collective-permute-start.2 = (bf16[2,96,256]{2,1,0:T(8,128)(2,1)S(1)}, bf16[2,96,256]{2,1,0:T(8,128)(2,1)S(1)}, u32[]{:S(2)}, u32[]{:S(2)}) collective-permute-start(bf16[2,96,256]{2,1,0:T(8,128)(2,1)S(1)} %project.32.refs_1_), channel_id=1, source_target_pairs={{0,1},{1,0},{2,3},{3,2},{4,5},{5,4},{6,7},{7,6},{8,9},{9,8},{10,11... | collective-permute-start | bytes 294920 | tf_op jit(solution)/shard_map/project/ppermute | solution.py:459
  95.6 0.8 collective-permute-start.3
  96.7 1.4 %collective-permute-start.4 = (bf16[2,96,256]{2,1,0:T(8,128)(2,1)S(1)}, bf16[2,96,256]{2,1,0:T(8,128)(2,1)S(1)}, u32[]{:S(2)}, u32[]{:S(2)}) collective-permute-start(bf16[2,96,256]{2,1,0:T(8,128)(2,1)S(1)} %project.34.refs_3_), channel_id=1, source_target_pairs={{0,1},{1,0},{2,3},{3,2},{4,5},{5,4},{6,7},{7,6},{8,9},{9,8},{10,11... | collective-permute-start | bytes 294920 | tf_op jit(solution)/shard_map/project/ppermute | solution.py:459
  98.1 0.4 project.35.refs_4_
  98.5 0.7 collective-permute-start.5
  99.6 0.4 project.39.refs_8_
  100.7 0.4 project.36.refs_5_
  101.4 0.4 project.28.refs_7_
  101.7 0.4 project.27.refs_6_
  102.8 0.4 project.24.refs_3_
  103.2 0.4 project.23.refs_2_
  103.9 1.4 %collective-permute-start.6 = (bf16[2,96,256]{2,1,0:T(8,128)(2,1)S(1)}, bf16[2,96,256]{2,1,0:T(8,128)(2,1)S(1)}, u32[]{:S(2)}, u32[]{:S(2)}) collective-permute-start(bf16[2,96,256]{2,1,0:T(8,128)(2,1)S(1)} %project.36.refs_5_), channel_id=1, source_target_pairs={{0,1},{1,0},{2,3},{3,2},{4,5},{5,4},{6,7},{7,6},{8,9},{9,8},{10,11... | collective-permute-start | bytes 294920 | tf_op jit(solution)/shard_map/project/ppermute | solution.py:459
  105.3 0.7 collective-permute-start.7
  106.0 1.4 collective-permute-start.8
  107.4 0.7 collective-permute-start.9
  108.0 1.4 collective-permute-start.10
  109.4 0.4 project.21.refs_0_
  109.8 1.3 collective-permute-start.11
  111.0 0.7 collective-permute-done.7.refs_16_
  111.8 1.4 collective-permute-start.12
  113.2 0.7 collective-permute-done.8.refs_17_
  113.9 1.4 collective-permute-start.13
  115.3 0.7 collective-permute-done.9.refs_18_
  116.0 1.4 collective-permute-start.14
  117.4 0.7 collective-permute-done.10.refs_19_
  118.1 1.4 collective-permute-start.15
  119.8 1.8 %project.41 = (bf16[2,96,256]{2,1,0:T(8,128)(2,1)S(1)}, f32[96,2560]{1,0:T(8,128)S(1)}, f32[96,2560]{1,0:T(8,128)S(1)}, f32[96,128]{1,0:T(8,128)S(1)}, f32[4,96,...) custom-call(bf16[2,96,256]{2,1,0:T(8,128)(2,1)S(1)} %project.21.refs_0_, ...), custom_call_target="tpu_custom_call", output_to_operand_aliasing={{0}: (9, {})} | custom-call | tf_op jit(solution)/shard_map/project/pallas_call | solution.py:382
  121.6 0.8 collective-permute-start.16
  122.4 1.3 collective-permute-start.17
  123.8 0.7 collective-permute-done.13.refs_12_
  124.4 1.4 collective-permute-start.18
  125.8 0.7 collective-permute-done.14.refs_13_
  126.5 1.4 collective-permute-start.19
  127.9 0.7 collective-permute-done.15.refs_14_
  128.6 1.4 collective-permute-start.20
  130.0 0.7 collective-permute-done.16.refs_15_
  130.8 1.8 %collective-permute-done.17.refs_16_ = bf16[2,96,256]{2,1,0:T(8,128)(2,1)S(1)} collective-permute-done((bf16[2,96,256]{2,1,0:T(8,128)(2,1)S(1)}, bf16[2,96,256]{2,1,0:T(8,128)(2,1)S(1)}, u32[]{:S(2)}, u32[]{:S(2)}) %collective-permute-start.17) | collective-permute-done | bytes 98336 | tf_op jit(solution)/shard_map/project/ppermute | solution.py:461
  132.6 1.1 collective-permute-done.18.refs_17_
  133.6 1.1 collective-permute-done.19.refs_18_
  134.7 1.1 collective-permute-done.20.refs_19_
  135.7 2.9 %norm.1 = (bf16[96,5120]{1,0:T(8,128)(2,1)}, bf16[96,5120]{1,0:T(8,128)(2,1)}) custom-call(s32[1]{0:T(128)} %bitcast.side_ref.refs_0_, bf16[2,96,256]{2,1,0:T(8,128)(2,1)S(1)} %project.31.refs_0_, bf16[2,96,256]{2,1,0:T(8,128)(2,1)S(1)} %project.32.refs_1_, bf16[2,96,256]{2,1,0:T(8,128)(2,1)S(1)} %project.33.refs_2_, ...), custom_call_target="tpu_custom_call" | custom-call | tf_op jit(solution)/shard_map/norm/pallas_call | solution.py:424
  (21 shorter events, 4.1 us)
Async XLA Ops:
  62.0 6.6 %collective-permute-start = (bf16[32,464,128]{2,1,0:T(8,128)(2,1)S(1)}, bf16[32,464,128]{2,1,0:T(8,128)(2,1)S(1)}, u32[]{:S(2)}, u32[]{:S(2)}) collective-permute-start(bf16[32,464,128]{2,1,0:T(8,128)(2,1)S(1)} %all_to_all.10.refs_0_.refs_1_), channel_id=1, source_target_pairs={{0,2},{2,0},{1,3},{3,1},{4,6},{6,4},{5,7},{7,5},{8,10},{10,8},{9,1... | collective-permute-start | bytes 11403272 | tf_op jit(solution)/shard_map/spread/ppermute | solution.py:448
  92.7 11.2 %collective-permute-start.1 = (bf16[2,96,256]{2,1,0:T(8,128)(2,1)S(1)}, bf16[2,96,256]{2,1,0:T(8,128)(2,1)S(1)}, u32[]{:S(2)}, u32[]{:S(2)}) collective-permute-start(bf16[2,96,256]{2,1,0:T(8,128)(2,1)S(1)} %project.31.refs_0_), channel_id=1, source_target_pairs={{0,1},{1,0},{2,3},{3,2},{4,5},{5,4},{6,7},{7,6},{8,9},{9,8},{10,11... | collective-permute-start | bytes 294920 | tf_op jit(solution)/shard_map/project/ppermute | solution.py:459
  93.8 11.5 %collective-permute-start.2 = (bf16[2,96,256]{2,1,0:T(8,128)(2,1)S(1)}, bf16[2,96,256]{2,1,0:T(8,128)(2,1)S(1)}, u32[]{:S(2)}, u32[]{:S(2)}) collective-permute-start(bf16[2,96,256]{2,1,0:T(8,128)(2,1)S(1)} %project.32.refs_1_), channel_id=1, source_target_pairs={{0,1},{1,0},{2,3},{3,2},{4,5},{5,4},{6,7},{7,6},{8,9},{9,8},{10,11... | collective-permute-start | bytes 294920 | tf_op jit(solution)/shard_map/project/ppermute | solution.py:459
  95.6 10.4 %collective-permute-start.3 = (bf16[2,96,256]{2,1,0:T(8,128)(2,1)S(1)}, bf16[2,96,256]{2,1,0:T(8,128)(2,1)S(1)}, u32[]{:S(2)}, u32[]{:S(2)}) collective-permute-start(bf16[2,96,256]{2,1,0:T(8,128)(2,1)S(1)} %project.33.refs_2_), channel_id=1, source_target_pairs={{0,1},{1,0},{2,3},{3,2},{4,5},{5,4},{6,7},{7,6},{8,9},{9,8},{10,11... | collective-permute-start | bytes 294920 | tf_op jit(solution)/shard_map/project/ppermute | solution.py:459
  96.7 10.7 %collective-permute-start.4 = (bf16[2,96,256]{2,1,0:T(8,128)(2,1)S(1)}, bf16[2,96,256]{2,1,0:T(8,128)(2,1)S(1)}, u32[]{:S(2)}, u32[]{:S(2)}) collective-permute-start(bf16[2,96,256]{2,1,0:T(8,128)(2,1)S(1)} %project.34.refs_3_), channel_id=1, source_target_pairs={{0,1},{1,0},{2,3},{3,2},{4,5},{5,4},{6,7},{7,6},{8,9},{9,8},{10,11... | collective-permute-start | bytes 294920 | tf_op jit(solution)/shard_map/project/ppermute | solution.py:459
  98.5 9.5 %collective-permute-start.5 = (bf16[2,96,256]{2,1,0:T(8,128)(2,1)S(1)}, bf16[2,96,256]{2,1,0:T(8,128)(2,1)S(1)}, u32[]{:S(2)}, u32[]{:S(2)}) collective-permute-start(bf16[2,96,256]{2,1,0:T(8,128)(2,1)S(1)} %project.35.refs_4_), channel_id=1, source_target_pairs={{0,1},{1,0},{2,3},{3,2},{4,5},{5,4},{6,7},{7,6},{8,9},{9,8},{10,11... | collective-permute-start | bytes 294920 | tf_op jit(solution)/shard_map/project/ppermute | solution.py:459
  103.9 5.9 %collective-permute-start.6 = (bf16[2,96,256]{2,1,0:T(8,128)(2,1)S(1)}, bf16[2,96,256]{2,1,0:T(8,128)(2,1)S(1)}, u32[]{:S(2)}, u32[]{:S(2)}) collective-permute-start(bf16[2,96,256]{2,1,0:T(8,128)(2,1)S(1)} %project.36.refs_5_), channel_id=1, source_target_pairs={{0,1},{1,0},{2,3},{3,2},{4,5},{5,4},{6,7},{7,6},{8,9},{9,8},{10,11... | collective-permute-start | bytes 294920 | tf_op jit(solution)/shard_map/project/ppermute | solution.py:459
  105.3 6.5 %collective-permute-start.7 = (bf16[2,96,256]{2,1,0:T(8,128)(2,1)S(1)}, bf16[2,96,256]{2,1,0:T(8,128)(2,1)S(1)}, u32[]{:S(2)}, u32[]{:S(2)}) collective-permute-start(bf16[2,96,256]{2,1,0:T(8,128)(2,1)S(1)} %project.37.refs_6_), channel_id=1, source_target_pairs={{0,1},{1,0},{2,3},{3,2},{4,5},{5,4},{6,7},{7,6},{8,9},{9,8},{10,11... | collective-permute-start | bytes 294920 | tf_op jit(solution)/shard_map/project/ppermute | solution.py:459
  106.0 7.9 %collective-permute-start.8 = (bf16[2,96,256]{2,1,0:T(8,128)(2,1)S(1)}, bf16[2,96,256]{2,1,0:T(8,128)(2,1)S(1)}, u32[]{:S(2)}, u32[]{:S(2)}) collective-permute-start(bf16[2,96,256]{2,1,0:T(8,128)(2,1)S(1)} %project.38.refs_7_), channel_id=1, source_target_pairs={{0,1},{1,0},{2,3},{3,2},{4,5},{5,4},{6,7},{7,6},{8,9},{9,8},{10,11... | collective-permute-start | bytes 294920 | tf_op jit(solution)/shard_map/project/ppermute | solution.py:459
  107.4 8.7 %collective-permute-start.9 = (bf16[2,96,256]{2,1,0:T(8,128)(2,1)S(1)}, bf16[2,96,256]{2,1,0:T(8,128)(2,1)S(1)}, u32[]{:S(2)}, u32[]{:S(2)}) collective-permute-start(bf16[2,96,256]{2,1,0:T(8,128)(2,1)S(1)} %project.39.refs_8_), channel_id=1, source_target_pairs={{0,1},{1,0},{2,3},{3,2},{4,5},{5,4},{6,7},{7,6},{8,9},{9,8},{10,11... | collective-permute-start | bytes 294920 | tf_op jit(solution)/shard_map/project/ppermute | solution.py:459
  108.0 10.1 %collective-permute-start.10 = (bf16[2,96,256]{2,1,0:T(8,128)(2,1)S(1)}, bf16[2,96,256]{2,1,0:T(8,128)(2,1)S(1)}, u32[]{:S(2)}, u32[]{:S(2)}) collective-permute-start(bf16[2,96,256]{2,1,0:T(8,128)(2,1)S(1)} %project.40.refs_9_), channel_id=1, source_target_pairs={{0,1},{1,0},{2,3},{3,2},{4,5},{5,4},{6,7},{7,6},{8,9},{9,8},{10,11... | collective-permute-start | bytes 294920 | tf_op jit(solution)/shard_map/project/ppermute | solution.py:459
  109.8 11.9 %collective-permute-start.11 = (bf16[2,96,256]{2,1,0:T(8,128)(2,1)S(1)}, bf16[2,96,256]{2,1,0:T(8,128)(2,1)S(1)}, u32[]{:S(2)}, u32[]{:S(2)}) collective-permute-start(bf16[2,96,256]{2,1,0:T(8,128)(2,1)S(1)} %project.21.refs_0_), channel_id=1, source_target_pairs={{0,1},{1,0},{2,3},{3,2},{4,5},{5,4},{6,7},{7,6},{8,9},{9,8},{10,11... | collective-permute-start | bytes 294920 | tf_op jit(solution)/shard_map/project/ppermute | solution.py:461
  111.8 10.6 %collective-permute-start.12 = (bf16[2,96,256]{2,1,0:T(8,128)(2,1)S(1)}, bf16[2,96,256]{2,1,0:T(8,128)(2,1)S(1)}, u32[]{:S(2)}, u32[]{:S(2)}) collective-permute-start(bf16[2,96,256]{2,1,0:T(8,128)(2,1)S(1)} %project.22.refs_1_), channel_id=1, source_target_pairs={{0,1},{1,0},{2,3},{3,2},{4,5},{5,4},{6,7},{7,6},{8,9},{9,8},{10,11... | collective-permute-start | bytes 294920 | tf_op jit(solution)/shard_map/project/ppermute | solution.py:461
  113.9 10.5 %collective-permute-start.13 = (bf16[2,96,256]{2,1,0:T(8,128)(2,1)S(1)}, bf16[2,96,256]{2,1,0:T(8,128)(2,1)S(1)}, u32[]{:S(2)}, u32[]{:S(2)}) collective-permute-start(bf16[2,96,256]{2,1,0:T(8,128)(2,1)S(1)} %project.23.refs_2_), channel_id=1, source_target_pairs={{0,1},{1,0},{2,3},{3,2},{4,5},{5,4},{6,7},{7,6},{8,9},{9,8},{10,11... | collective-permute-start | bytes 294920 | tf_op jit(solution)/shard_map/project/ppermute | solution.py:461
  116.0 10.5 %collective-permute-start.14 = (bf16[2,96,256]{2,1,0:T(8,128)(2,1)S(1)}, bf16[2,96,256]{2,1,0:T(8,128)(2,1)S(1)}, u32[]{:S(2)}, u32[]{:S(2)}) collective-permute-start(bf16[2,96,256]{2,1,0:T(8,128)(2,1)S(1)} %project.24.refs_3_), channel_id=1, source_target_pairs={{0,1},{1,0},{2,3},{3,2},{4,5},{5,4},{6,7},{7,6},{8,9},{9,8},{10,11... | collective-permute-start | bytes 294920 | tf_op jit(solution)/shard_map/project/ppermute | solution.py:461
  118.1 10.5 %collective-permute-start.15 = (bf16[2,96,256]{2,1,0:T(8,128)(2,1)S(1)}, bf16[2,96,256]{2,1,0:T(8,128)(2,1)S(1)}, u32[]{:S(2)}, u32[]{:S(2)}) collective-permute-start(bf16[2,96,256]{2,1,0:T(8,128)(2,1)S(1)} %project.25.refs_4_), channel_id=1, source_target_pairs={{0,1},{1,0},{2,3},{3,2},{4,5},{5,4},{6,7},{7,6},{8,9},{9,8},{10,11... | collective-permute-start | bytes 294920 | tf_op jit(solution)/shard_map/project/ppermute | solution.py:461
  121.6 9.1 %collective-permute-start.16 = (bf16[2,96,256]{2,1,0:T(8,128)(2,1)S(1)}, bf16[2,96,256]{2,1,0:T(8,128)(2,1)S(1)}, u32[]{:S(2)}, u32[]{:S(2)}) collective-permute-start(bf16[2,96,256]{2,1,0:T(8,128)(2,1)S(1)} %project.26.refs_5_), channel_id=1, source_target_pairs={{0,1},{1,0},{2,3},{3,2},{4,5},{5,4},{6,7},{7,6},{8,9},{9,8},{10,11... | collective-permute-start | bytes 294920 | tf_op jit(solution)/shard_map/project/ppermute | solution.py:461
  122.4 10.2 %collective-permute-start.17 = (bf16[2,96,256]{2,1,0:T(8,128)(2,1)S(1)}, bf16[2,96,256]{2,1,0:T(8,128)(2,1)S(1)}, u32[]{:S(2)}, u32[]{:S(2)}) collective-permute-start(bf16[2,96,256]{2,1,0:T(8,128)(2,1)S(1)} %project.27.refs_6_), channel_id=1, source_target_pairs={{0,1},{1,0},{2,3},{3,2},{4,5},{5,4},{6,7},{7,6},{8,9},{9,8},{10,11... | collective-permute-start | bytes 294920 | tf_op jit(solution)/shard_map/project/ppermute | solution.py:461
  124.4 9.2 %collective-permute-start.18 = (bf16[2,96,256]{2,1,0:T(8,128)(2,1)S(1)}, bf16[2,96,256]{2,1,0:T(8,128)(2,1)S(1)}, u32[]{:S(2)}, u32[]{:S(2)}) collective-permute-start(bf16[2,96,256]{2,1,0:T(8,128)(2,1)S(1)} %project.28.refs_7_), channel_id=1, source_target_pairs={{0,1},{1,0},{2,3},{3,2},{4,5},{5,4},{6,7},{7,6},{8,9},{9,8},{10,11... | collective-permute-start | bytes 294920 | tf_op jit(solution)/shard_map/project/ppermute | solution.py:461
  126.5 8.1 %collective-permute-start.19 = (bf16[2,96,256]{2,1,0:T(8,128)(2,1)S(1)}, bf16[2,96,256]{2,1,0:T(8,128)(2,1)S(1)}, u32[]{:S(2)}, u32[]{:S(2)}) collective-permute-start(bf16[2,96,256]{2,1,0:T(8,128)(2,1)S(1)} %project.29.refs_8_), channel_id=1, source_target_pairs={{0,1},{1,0},{2,3},{3,2},{4,5},{5,4},{6,7},{7,6},{8,9},{9,8},{10,11... | collective-permute-start | bytes 294920 | tf_op jit(solution)/shard_map/project/ppermute | solution.py:461
  128.6 7.1 %collective-permute-start.20 = (bf16[2,96,256]{2,1,0:T(8,128)(2,1)S(1)}, bf16[2,96,256]{2,1,0:T(8,128)(2,1)S(1)}, u32[]{:S(2)}, u32[]{:S(2)}) collective-permute-start(bf16[2,96,256]{2,1,0:T(8,128)(2,1)S(1)} %get-tuple-element.41), channel_id=1, source_target_pairs={{0,1},{1,0},{2,3},{3,2},{4,5},{5,4},{6,7},{7,6},{8,9},{9,8},{10,11... | collective-permute-start | bytes 294920 | tf_op jit(solution)/shard_map/project/ppermute | solution.py:463
